TPU v7x, 32 devices: a whole 2x2x4 slice. The times are simulated.
32 devices in a mesh: outer: 8 (over y, x, core), node: 4 (over z).
Axes of the slice: x: 2, y: 2, z: 4, core: 2. Of those that a mesh axis runs over, the one named last changes fastest.
Arguments:
- context: bfloat16 [2048, 4096], P('outer', 'node'), may hold values from -6 to 6
- grad_out: bfloat16 [2048, 4096], P('outer', 'node'), may hold values from -6 to 6
- out_weight: bfloat16 [4096, 4096], P('node', 'outer'), may hold values from -0.09375 to 0.09375
Outputs:
- context_grad: bfloat16 [2048, 4096], P('outer', 'node')
- weight_grad: float32 [4096, 4096], P('node', 'outer')
All inputs are finite; a program needn't handle non-finite values.
Results may differ from a plain program's by a relative error of at most 0.001.
Values may be sent and summed in bfloat16 or wider, within the bound.
No kernel may reach another device: no remote copies, remote signals or barrier semaphores. Data moves between devices by JAX's collectives and lax.ppermute only.
A program may use at most 64 MiB of HBM per device.

v0:
```python
import math

import jax
import jax.numpy as jnp
from jax import lax
from jax.sharding import PartitionSpec as P


def body(context, grad_out, out_weight):
    grad_full = lax.all_gather(grad_out, "node", axis=1, tiled=True)
    context_grad = lax.dot_general(
        grad_full,
        lax.all_gather(out_weight, "outer", axis=1, tiled=True),
        (((1,), (1,)), ((), ())),
        preferred_element_type=jnp.float32,
    ).astype(jnp.bfloat16)
    norm_scale = 1.0 / math.sqrt(grad_full.shape[0] * lax.axis_size("outer"))
    owner_cols = lax.all_to_all(grad_full, "outer", split_axis=1, concat_axis=0, tiled=True)
    weight_grad = (
        lax.dot_general(
            lax.all_gather(context, "outer", axis=0, tiled=True),
            owner_cols,
            (((0,), (0,)), ((), ())),
            preferred_element_type=jnp.float32,
        )
        * norm_scale
    )
    return (context_grad, weight_grad)


def solution(mesh):
    in_specs = (P("outer", "node"), P("outer", "node"), P("node", "outer"))
    out_specs = (P("outer", "node"), P("node", "outer"))
    return jax.shard_map(body, mesh=mesh, in_specs=in_specs, out_specs=out_specs, check_vma=False)
```

profile of v0, /device:TPU:0, one launch (start us, length us, event | category | flops | bytes accessed | tf_op | source)
XLA Modules:
  0.0 178.9 jit_solution(4898946849767928203)
XLA Ops:
  7.2 0.0 all-gather.4.cloned.1.call-start
  7.2 2.0 %copy.5 = bf16[256,1024]{0,1:T(8,128)(2,1)} copy(bf16[256,1024]{1,0:T(8,128)(2,1)} %param.4) | data formatting | bytes 1048576 | tf_op args[1]
  9.3 0.0 all-gather.4.cloned.1.call-update
  9.3 0.0 all-gather.8.cloned.1.call-start
  9.3 0.7 all-gather.8.cloned.1.call-update
  10.0 0.0 all-gather.6.cloned.1.call-start
  10.1 0.7 all-gather.6.cloned.1.call-update
  10.8 48.0 %all-gather.4.cloned.1.call-done = bf16[256,4096]{0,1:T(8,128)(2,1)} async-done(((bf16[256,1024]{0,1:T(8,128)(2,1)}), bf16[256,4096]{0,1:T(8,128)(2,1)}) %all-gather.4.cloned.1.call-update) | async-done | bytes 2097168 | tf_op jit(solution)/shard_map/all_gather | solution.py:10
  58.8 35.8 %all_to_all.19 = bf16[256,8,512]{0,2,1:T(8,128)(2,1)S(1)} all-to-all(bf16[256,8,512]{0,2,1:T(8,128)(2,1)} %bitcast.9), channel_id=1, replica_groups=mesh['outer'=8,'node'=4] {'outer'}, dimensions={1} | all-to-all | bytes 4194304 | tf_op jit(solution)/shard_map/all_to_all | solution.py:18
  94.7 2.4 %copy.6 = bf16[8,256,512]{2,1,0:T(8,128)(2,1)} copy(bf16[8,256,512]{1,2,0:T(8,128)(2,1)S(1)} %bitcast.7) | data formatting | bytes 4194304 | tf_op jit(solution)/shard_map/all_to_all | solution.py:18
  97.0 10.9 %all-gather.8.cloned.1.call-done = bf16[2048,1024]{1,0:T(8,128)(2,1)} async-done(((bf16[256,1024]{1,0:T(8,128)(2,1)}), bf16[2048,1024]{1,0:T(8,128)(2,1)}) %all-gather.8.cloned.1.call-update) | async-done | bytes 4194320 | tf_op jit(solution)/shard_map/all_gather | solution.py:21
  107.9 0.0 copy-start
  107.9 6.7 %convolution_multiply_fusion = f32[1024,512]{1,0:T(8,128)} fusion(bf16[2048,1024]{1,0:T(8,128)(2,1)} %all-gather.8.cloned.1.call-done, bf16[2048,512]{1,0:T(8,128)(2,1)} %bitcast.8), kind=kOutput, calls=%fused_computation | convolution fusion | flops 2148007936 | bytes 8388608 | tf_op jit(solution)/shard_map/dot_general | solution.py:20
  114.6 51.2 %all-gather.6.cloned.1.call-done = bf16[1024,4096]{1,0:T(8,128)(2,1)} async-done(((bf16[1024,512]{1,0:T(8,128)(2,1)}), bf16[1024,4096]{1,0:T(8,128)(2,1)}) %all-gather.6.cloned.1.call-update) | async-done | bytes 8388624 | tf_op jit(solution)/shard_map/all_gather | solution.py:13
  165.8 0.0 copy-done
  165.8 6.6 %convolution_convert_fusion = bf16[256,1024]{1,0:T(8,128)(2,1)} fusion(bf16[256,4096]{0,1:T(8,128)(2,1)S(1)} %copy-done, bf16[1024,4096]{1,0:T(8,128)(2,1)} %all-gather.6.cloned.1.call-done), kind=kOutput, calls=%fused_computation.1 | convolution fusion | flops 2147745792 | bytes 11010048 | tf_op jit(solution)/shard_map/dot_general | solution.py:11
Async XLA Ops:
  7.2 51.6 %all-gather.4.cloned.1.call-start = ((), (), s32[]{:S(2)}) async-start(), calls=%async_computation.1 | async-start | bytes 2621440 | tf_op jit(solution)/shard_map/all_gather | solution.py:10
  9.3 98.7 %all-gather.8.cloned.1.call-start = ((), (), s32[]{:S(2)}) async-start(), calls=%async_computation.3 | async-start | bytes 4718592 | tf_op jit(solution)/shard_map/all_gather | solution.py:21
  10.0 155.8 %all-gather.6.cloned.1.call-start = ((), (), s32[]{:S(2)}) async-start(), calls=%async_computation.2 | async-start | bytes 9437184 | tf_op jit(solution)/shard_map/all_gather | solution.py:13
  107.9 57.9 %copy-start = (bf16[256,4096]{0,1:T(8,128)(2,1)S(1)}, bf16[256,4096]{0,1:T(8,128)(2,1)}, u32[]{:S(2)}) copy-start(bf16[256,4096]{0,1:T(8,128)(2,1)} %all-gather.4.cloned.1.call-done) | copy-start | bytes 6291460
Sparse Core Ops, SparseCore 0:
  10.1 48.6 all-gather.3
  60.7 47.1 all-gather.7
  109.8 55.9 all-gather.5
where the time goes:
time: 179 us
  waiting for transfers between devices  112 us (63%)
  blocking collectives  35.8 us (20%)
  between operations  13.7 us (8%)
  matrix products  13.2 us (7%)
  local copies, waits for them, and re-layouts  4.43 us (2%)
    all_gather x1, waiting for transfers between devices, body(): lax.all_gather(out_weight, 'outer', axis=1, tiled=True)  51.2 us
    all_gather x1, waiting for transfers between devices, body(): grad_full = lax.all_gather(grad_out, 'node', axis=1, tiled=True)  48 us
    all_to_all x1, blocking collectives, body(): lax.all_to_all(grad_full, 'outer', split_axis=1, concat_axis=0, tiled=True)  35.8 us
    all_gather x1, waiting for transfers between devices, body(): lax.all_gather(context, 'outer', axis=0, tiled=True)  10.9 us
    dot_general x1, matrix products, body(): lax.dot_general(lax.all_gather(context, 'outer', axis=0, tiled=True), own...  6.68 us
    dot_general x1, matrix products, body(): lax.dot_general(grad_full, lax.all_gather(out_weight, 'outer', axis=1, ti...  6.56 us
  transfers between devices with their start and end apart: 3, of which 3 were waited for; matrix products, arithmetic and copies ran while one was open for 5% of the time, Pallas kernels for 0%

commit v1 on v0

v1 whole, which is shorter than its diff:
```python
import math

import jax
import jax.numpy as jnp
from jax import lax
from jax.sharding import PartitionSpec as P


def plane_of(outer):
    cores = 2 if outer % 2 == 0 else 1
    chips = outer // cores
    cols = max(d for d in range(1, math.isqrt(chips) + 1) if chips % d == 0)
    return chips // cols, cols, cores


def shift(array, db, da, dc):
    outer = lax.axis_size("outer")
    rows, cols, cores = plane_of(outer)

    def source(o):
        b, a, c = o // (cols * cores), o // cores % cols, o % cores
        return ((b + db) % rows * cols + (a + da) % cols) * cores + (c + dc) % cores

    return lax.ppermute(array, "outer", [(source(o), o) for o in range(outer)])


def halves(array, axis):
    half = array.shape[axis] // 2
    return [lax.slice_in_dim(array, 0, half, axis=axis), lax.slice_in_dim(array, half, 2 * half, axis=axis)]


def gather(array, axis):
    rows, cols, cores = plane_of(lax.axis_size("outer"))
    first, second = halves(array, axis)
    got = {(0, 0): [first, second]}
    for da in range(1, cols):
        got[0, da] = [shift(first, 0, da, 0), shift(second, 0, da, 0)]
    for db in range(1, rows):
        got[db, 0] = [shift(first, db, 0, 0), shift(second, db, 0, 0)]
    for db in range(1, rows):
        for da in range(1, cols):
            got[db, da] = [shift(got[0, da][0], db, 0, 0), shift(got[db, 0][1], 0, da, 0)]
    out = {}
    for (db, da), pair in got.items():
        out[db, da, 0] = pair
        for dc in range(1, cores):
            out[db, da, dc] = [shift(piece, 0, 0, dc) for piece in pair]
    return out


def position(db, da, dc):
    rows, cols, cores = plane_of(lax.axis_size("outer"))
    o = lax.axis_index("outer")
    b, a, c = o // (cols * cores), o // cores % cols, o % cores
    return ((b + db) % rows * cols + (a + da) % cols) * cores + (c + dc) % cores


def ring(array):
    node = lax.axis_size("node")
    me = lax.axis_index("node")
    blocks = {0: array}
    up, down = array, array
    for step in range(1, node // 2 + 1):
        up = lax.ppermute(up, "node", [(i, (i + 1) % node) for i in range(node)])
        blocks[node - step] = up
        if 2 * step < node:
            down = lax.ppermute(down, "node", [((i + 1) % node, i) for i in range(node)])
            blocks[step] = down
    whole = jnp.zeros((node,) + array.shape, array.dtype)
    for d, block in blocks.items():
        whole = lax.dynamic_update_index_in_dim(whole, block, (me + d) % node, 0)
    return whole


def body(context, grad_out, out_weight):
    outer = lax.axis_size("outer")
    rows, cols, cores = plane_of(outer)
    tokens = grad_out.shape[0]
    width = out_weight.shape[1]
    norm_scale = 1.0 / math.sqrt(tokens * outer)

    grad = ring(grad_out)
    per = grad_out.shape[1] // width

    def columns(first, count):
        if per:
            block = lax.dynamic_slice(grad, (first // (per * width), 0, first % (per * width)), (1, tokens, count))
            return block.reshape(tokens, count)
        wide = grad.transpose(1, 0, 2).reshape(tokens, -1)
        return lax.dynamic_slice_in_dim(wide, first, count, axis=1)

    weights = gather(out_weight, 1)
    contexts = gather(context, 0)

    context_grad = 0.0
    weight_grad = 0.0
    for at, pair in weights.items():
        half = width // 2
        for h, piece in enumerate(pair):
            context_grad += lax.dot_general(
                columns(position(*at) * width + h * half, half),
                piece,
                (((1,), (1,)), ((), ())),
                preferred_element_type=jnp.float32,
            )
    for at, pair in contexts.items():
        back = (-at[0] % rows, -at[1] % cols, -at[2] % cores)
        mine = columns(position(*back) * width, width)
        theirs = mine if at == (0, 0, 0) else shift(mine, *at)
        half = tokens // 2
        for h, piece in enumerate(pair):
            weight_grad += lax.dot_general(
                piece,
                theirs[h * half : (h + 1) * half],
                (((0,), (0,)), ((), ())),
                preferred_element_type=jnp.float32,
            )
    return (context_grad.astype(jnp.bfloat16), weight_grad * norm_scale)


def solution(mesh):
    in_specs = (P("outer", "node"), P("outer", "node"), P("node", "outer"))
    out_specs = (P("outer", "node"), P("node", "outer"))
    return jax.shard_map(body, mesh=mesh, in_specs=in_specs, out_specs=out_specs, check_vma=False)
```

time: 179 us -> 192 us (1.073)
  blocking collectives: 35.8 us -> 0 us
  starting transfers between devices: 0.12 us -> 30.3 us
  matrix products: 13.2 us -> 35.5 us
  between operations: 13.7 us -> 0.99 us
  local copies, waits for them, and re-layouts: 4.43 us -> 12.1 us
    ppermute x0 -> x38, waiting for transfers between devices: none -> 112 us  [the longest x35 89 us: shift(): return lax.ppermute(array, 'outer', [(source(o), o) for o in range(outer)])]
    all_gather x3 -> x0, waiting for transfers between devices: 110 us -> none  [the longest x1 51.2 us: body(): lax.all_gather(out_weight, 'outer', axis=1, tiled=True)]
    all_to_all x1 -> x0, blocking collectives: 35.8 us -> none  [body(): lax.all_to_all(grad_full, 'outer', split_axis=1, concat_axis=0, tiled=True)]
    ppermute x0 -> x38, starting transfers between devices: none -> 30.3 us  [the longest x35 25.2 us: shift(): return lax.ppermute(array, 'outer', [(source(o), o) for o in range(outer)])]
    dot_general x2 -> x32, matrix products: 13.2 us -> 35.5 us  [the longest x16 24.1 us: body(): lax.dot_general(piece, theirs[h * half:(h + 1) * half], (((0,), (0,)), ((...]
    slice x0 -> x2, local copies, waits for them, and re-layouts: none -> 4.14 us  [the longest x1 2.23 us: halves(): lax.slice_in_dim(array, 0, half, axis=axis)]
    dynamic_update_slice x0 -> x4, local copies, waits for them, and re-layouts: none -> 3.34 us  [ring(): whole = lax.dynamic_update_index_in_dim(whole, block, (me + d) % node, 0)]
    all_to_all x1 -> x0, local copies, waits for them, and re-layouts: 2.39 us -> none  [body(): lax.all_to_all(grad_full, 'outer', split_axis=1, concat_axis=0, tiled=True)]
  transfers between devices with their start and end apart: 3 -> 38, of which waited for: 3 -> 15; matrix products, arithmetic and copies ran while one was open for 5% -> 23% of each run, Pallas kernels for 0% -> 0%
where the time goes in v1:
time: 192 us; the launch traced here: 191 us
  waiting for transfers between devices  112 us (58%)
  matrix products  35.5 us (18%)
  starting transfers between devices  30.3 us (16%)
  local copies, waits for them, and re-layouts  12.1 us (6%)
    ppermute x35, waiting for transfers between devices, shift(): return lax.ppermute(array, 'outer', [(source(o), o) for o in range(outer)])  89 us
    ppermute x35, starting transfers between devices, shift(): return lax.ppermute(array, 'outer', [(source(o), o) for o in range(outer)])  25.2 us
    dot_general x16, matrix products, body(): lax.dot_general(piece, theirs[h * half:(h + 1) * half], (((0,), (0,)), ((...  24.1 us
    ppermute x2, waiting for transfers between devices, ring(): up = lax.ppermute(up, 'node', [(i, (i + 1) % node) for i in range(node)])  14.2 us
    dot_general x16, matrix products, body(): lax.dot_general(columns(position(*at) * width + h * half, half), piece, (...  11.5 us
    ppermute x1, waiting for transfers between devices, ring(): lax.ppermute(down, 'node', [((i + 1) % node, i) for i in range(node)])  8.85 us
    unnamed x13, local copies, waits for them, and re-layouts  4.16 us
  transfers between devices with their start and end apart: 38, of which 15 were waited for; matrix products, arithmetic and copies ran while one was open for 23% of the time, Pallas kernels for 0%

profile of v1, /device:TPU:0, one launch (start us, length us, event | category | flops | bytes accessed | tf_op | source)
XLA Modules:
  0.0 191.1 jit_solution(7146745435015262385)
XLA Ops:
  0.6 3.1 %collective-permute-start = (bf16[256,1024]{1,0:T(8,128)(2,1)}, bf16[256,1024]{1,0:T(8,128)(2,1)}, u32[]{:S(2)}, u32[]{:S(2)}) collective-permute-start(bf16[256,1024]{1,0:T(8,128)(2,1)} %param.4), channel_id=1, source_target_pairs={{0,1},{1,2},{2,3},{3,0},{4,5},{5,6},{6,7},{7,4},{8,9},{9,10},{10,1... | collective-permute-start | bytes 1572872 | tf_op jit(solution)/shard_map/ppermute | solution.py:64
  3.7 2.1 %collective-permute-start.1 = (bf16[256,1024]{1,0:T(8,128)(2,1)}, bf16[256,1024]{1,0:T(8,128)(2,1)}, u32[]{:S(2)}, u32[]{:S(2)}) collective-permute-start(bf16[256,1024]{1,0:T(8,128)(2,1)} %param.4), channel_id=1, source_target_pairs={{1,0},{2,1},{3,2},{0,3},{5,4},{6,5},{7,6},{4,7},{9,8},{10,9},{11,1... | collective-permute-start | bytes 1572872 | tf_op jit(solution)/shard_map/ppermute | solution.py:67
  5.8 1.9 fusion.108
  10.9 2.2 %fusion.107 = (bf16[1024,256]{1,0:T(8,128)(2,1)}, bf16[1024,256]{1,0:T(8,128)(2,1)}) fusion(bf16[1024,512]{1,0:T(8,128)(2,1)} %param.5), kind=kLoop, calls=%fused_computation.124 | loop fusion | bytes 2097152 | tf_op jit(solution)/shard_map/slice | solution.py:29
  13.4 5.4 %collective-permute-done = bf16[256,1024]{1,0:T(8,128)(2,1)} collective-permute-done((bf16[256,1024]{1,0:T(8,128)(2,1)}, bf16[256,1024]{1,0:T(8,128)(2,1)}, u32[]{:S(2)}, u32[]{:S(2)}) %collective-permute-start) | collective-permute-done | bytes 524320 | tf_op jit(solution)/shard_map/ppermute | solution.py:64
  20.0 8.9 %collective-permute-done.1 = bf16[256,1024]{1,0:T(8,128)(2,1)} collective-permute-done((bf16[256,1024]{1,0:T(8,128)(2,1)}, bf16[256,1024]{1,0:T(8,128)(2,1)}, u32[]{:S(2)}, u32[]{:S(2)}) %collective-permute-start.1) | collective-permute-done | bytes 524320 | tf_op jit(solution)/shard_map/ppermute | solution.py:67
  31.7 8.8 %collective-permute-done.2 = bf16[256,1024]{1,0:T(8,128)(2,1)} collective-permute-done((bf16[256,1024]{1,0:T(8,128)(2,1)}, bf16[256,1024]{1,0:T(8,128)(2,1)}, u32[]{:S(2)}, u32[]{:S(2)}) %collective-permute-start.2) | collective-permute-done | bytes 524320 | tf_op jit(solution)/shard_map/ppermute | solution.py:64
  44.9 8.4 %collective-permute-done.5 = bf16[1024,256]{1,0:T(8,128)(2,1)S(1)} collective-permute-done((bf16[1024,256]{1,0:T(8,128)(2,1)S(1)}, bf16[1024,256]{1,0:T(8,128)(2,1)S(1)}, u32[]{:S(2)}, u32[]{:S(2)}) %collective-permute-start.5) | collective-permute-done | bytes 524320 | tf_op jit(solution)/shard_map/ppermute | solution.py:24
  57.9 18.7 %collective-permute-done.10 = bf16[1024,256]{1,0:T(8,128)(2,1)S(1)} collective-permute-done((bf16[1024,256]{1,0:T(8,128)(2,1)}, bf16[1024,256]{1,0:T(8,128)(2,1)S(1)}, u32[]{:S(2)}, u32[]{:S(2)}) %collective-permute-start.10) | collective-permute-done | bytes 524320 | tf_op jit(solution)/shard_map/ppermute | solution.py:24
  82.3 12.0 %collective-permute-done.13 = bf16[1024,256]{1,0:T(8,128)(2,1)} collective-permute-done((bf16[1024,256]{1,0:T(8,128)(2,1)S(1)}, bf16[1024,256]{1,0:T(8,128)(2,1)}, u32[]{:S(2)}, u32[]{:S(2)}) %collective-permute-start.13) | collective-permute-done | bytes 524320 | tf_op jit(solution)/shard_map/ppermute | solution.py:24
  100.4 2.5 %collective-permute-start.32 = (bf16[256,512]{1,0:T(8,128)(2,1)S(1)}, bf16[256,512]{1,0:T(8,128)(2,1)S(1)}, u32[]{:S(2)}, u32[]{:S(2)}) collective-permute-start(bf16[256,512]{1,0:T(8,128)(2,1)S(1)} %get-tuple-element.6), channel_id=1, source_target_pairs={{24,0},{28,4},{16,8},{20,12},{8,16},{12,20},{0,24},{4,28},{25,1},{... | collective-permute-start | bytes 786440 | tf_op jit(solution)/shard_map/ppermute | solution.py:24
  103.9 8.9 %collective-permute-done.34 = bf16[128,1024]{1,0:T(8,128)(2,1)S(1)} collective-permute-done((bf16[128,1024]{1,0:T(8,128)(2,1)S(1)}, bf16[128,1024]{1,0:T(8,128)(2,1)S(1)}, u32[]{:S(2)}, u32[]{:S(2)}) %collective-permute-start.34) | collective-permute-done | bytes 262176 | tf_op jit(solution)/shard_map/ppermute | solution.py:24
  112.8 5.6 %collective-permute-done.32 = bf16[256,512]{1,0:T(8,128)(2,1)S(1)} collective-permute-done((bf16[256,512]{1,0:T(8,128)(2,1)S(1)}, bf16[256,512]{1,0:T(8,128)(2,1)S(1)}, u32[]{:S(2)}, u32[]{:S(2)}) %collective-permute-start.32) | collective-permute-done | bytes 262176 | tf_op jit(solution)/shard_map/ppermute | solution.py:24
  119.4 6.6 %collective-permute-done.33 = bf16[128,1024]{1,0:T(8,128)(2,1)S(1)} collective-permute-done((bf16[128,1024]{1,0:T(8,128)(2,1)}, bf16[128,1024]{1,0:T(8,128)(2,1)S(1)}, u32[]{:S(2)}, u32[]{:S(2)}) %collective-permute-start.33) | collective-permute-done | bytes 262176 | tf_op jit(solution)/shard_map/ppermute | solution.py:24
  127.0 5.5 %collective-permute-done.26 = bf16[256,512]{1,0:T(8,128)(2,1)S(1)} collective-permute-done((bf16[256,512]{1,0:T(8,128)(2,1)S(1)}, bf16[256,512]{1,0:T(8,128)(2,1)S(1)}, u32[]{:S(2)}, u32[]{:S(2)}) %collective-permute-start.26) | collective-permute-done | bytes 262176 | tf_op jit(solution)/shard_map/ppermute | solution.py:24
  135.0 6.8 %collective-permute-done.20 = bf16[256,512]{1,0:T(8,128)(2,1)S(1)} collective-permute-done((bf16[256,512]{1,0:T(8,128)(2,1)S(1)}, bf16[256,512]{1,0:T(8,128)(2,1)S(1)}, u32[]{:S(2)}, u32[]{:S(2)}) %collective-permute-start.20) | collective-permute-done | bytes 262176 | tf_op jit(solution)/shard_map/ppermute | solution.py:24
  144.4 6.8 %collective-permute-done.29 = bf16[256,512]{1,0:T(8,128)(2,1)S(1)} collective-permute-done((bf16[256,512]{1,0:T(8,128)(2,1)S(1)}, bf16[256,512]{1,0:T(8,128)(2,1)S(1)}, u32[]{:S(2)}, u32[]{:S(2)}) %collective-permute-start.29) | collective-permute-done | bytes 262176 | tf_op jit(solution)/shard_map/ppermute | solution.py:24
  155.6 5.0 %collective-permute-done.23 = bf16[256,512]{1,0:T(8,128)(2,1)S(1)} collective-permute-done((bf16[256,512]{1,0:T(8,128)(2,1)S(1)}, bf16[256,512]{1,0:T(8,128)(2,1)S(1)}, u32[]{:S(2)}, u32[]{:S(2)}) %collective-permute-start.23) | collective-permute-done | bytes 262176 | tf_op jit(solution)/shard_map/ppermute | solution.py:24
  162.9 1.8 fusion.31
  166.3 1.8 fusion.37
  170.0 3.9 %collective-permute-done.35 = bf16[256,512]{1,0:T(8,128)(2,1)S(1)} collective-permute-done((bf16[256,512]{1,0:T(8,128)(2,1)S(1)}, bf16[256,512]{1,0:T(8,128)(2,1)S(1)}, u32[]{:S(2)}, u32[]{:S(2)}) %collective-permute-start.35) | collective-permute-done | bytes 262176 | tf_op jit(solution)/shard_map/ppermute | solution.py:24
  176.4 8.2 %multiply_bitcast_fusion = f32[1024,512]{0,1:T(8,128)} fusion(f32[512,1024]{1,0:T(8,128)} %fusion.15, f32[512,1024]{1,0:T(8,128)S(1)} %fusion.17, f32[512,1024]{1,0:T(8,128)S(1)} %fusion.19, f32[512,1024]{1,0:T(8,128)S(1)} %fusion.21, f32[512,1024]{1,0:T(8,128)} %fusion.23, f32[512,1024]{1,0:T(8,128)S(1)} %fusion.25, f32[512,1024]{1,0:T(8,128)S(1)} %fusion.27, ...), kind=kOutput, calls=%fused_computation | convolution fusion | flops 142606336 | bytes 33947648 | tf_op jit(solution)/shard_map/dot_general | solution.py:112
  184.6 2.9 %copy.5 = f32[1024,512]{1,0:T(8,128)} copy(f32[1024,512]{0,1:T(8,128)} %multiply_bitcast_fusion) | data formatting | bytes 4194304
  188.9 2.2 %fusion.10 = bf16[256,1024]{1,0:T(8,128)(2,1)} fusion(f32[256,1024]{1,0:T(8,128)S(1)} %fusion.43, f32[256,1024]{1,0:T(8,128)S(1)} %fusion.3, bf16[1024,256]{1,0:T(8,128)(2,1)} %collective-permute-done.15, bf16[4,256,1024]{2,1,0:T(8,128)(2,1)S(1)} %bitcast_dynamic-update-slice_fusion, s32[]{:T(128)S(6)} %select_n.664, s32[]{:T(128)S(6)} %select_n.666), kind=kOutput, calls=%fused_computation.16 | convolution fusion | flops 135004160 | bytes 3276808 | tf_op jit(solution)/shard_map/dot_general | solution.py:100
  (105 shorter events, 49.9 us)
Async XLA Ops:
  0.6 18.2 %collective-permute-start = (bf16[256,1024]{1,0:T(8,128)(2,1)}, bf16[256,1024]{1,0:T(8,128)(2,1)}, u32[]{:S(2)}, u32[]{:S(2)}) collective-permute-start(bf16[256,1024]{1,0:T(8,128)(2,1)} %param.4), channel_id=1, source_target_pairs={{0,1},{1,2},{2,3},{3,0},{4,5},{5,6},{6,7},{7,4},{8,9},{9,10},{10,1... | collective-permute-start | bytes 1572872 | tf_op jit(solution)/shard_map/ppermute | solution.py:64
  3.7 25.1 %collective-permute-start.1 = (bf16[256,1024]{1,0:T(8,128)(2,1)}, bf16[256,1024]{1,0:T(8,128)(2,1)}, u32[]{:S(2)}, u32[]{:S(2)}) collective-permute-start(bf16[256,1024]{1,0:T(8,128)(2,1)} %param.4), channel_id=1, source_target_pairs={{1,0},{2,1},{3,2},{0,3},{5,4},{6,5},{7,6},{4,7},{9,8},{10,9},{11,1... | collective-permute-start | bytes 1572872 | tf_op jit(solution)/shard_map/ppermute | solution.py:67
  7.7 96.1 %collective-permute-start.21 = (bf16[128,1024]{1,0:T(8,128)(2,1)}, bf16[128,1024]{1,0:T(8,128)(2,1)}, u32[]{:S(2)}, u32[]{:S(2)}) collective-permute-start(bf16[128,1024]{1,0:T(8,128)(2,1)} %get-tuple-element.14), channel_id=1, source_target_pairs={{8,0},{12,4},{0,8},{4,12},{24,16},{28,20},{16,24},{20,28},{9,1},{1... | collective-permute-start | bytes 786440 | tf_op jit(solution)/shard_map/ppermute | solution.py:24
  9.4 123.6 %collective-permute-start.27 = (bf16[128,1024]{1,0:T(8,128)(2,1)}, bf16[128,1024]{1,0:T(8,128)(2,1)S(1)}, u32[]{:S(2)}, u32[]{:S(2)}) collective-permute-start(bf16[128,1024]{1,0:T(8,128)(2,1)} %get-tuple-element.14), channel_id=1, source_target_pairs={{16,0},{20,4},{24,8},{28,12},{0,16},{4,20},{8,24},{12,28},{17,1},{... | collective-permute-start | bytes 786440 | tf_op jit(solution)/shard_map/ppermute | solution.py:24
  13.1 30.3 %collective-permute-start.4 = (bf16[1024,256]{1,0:T(8,128)(2,1)}, bf16[1024,256]{1,0:T(8,128)(2,1)}, u32[]{:S(2)}, u32[]{:S(2)}) collective-permute-start(bf16[1024,256]{1,0:T(8,128)(2,1)} %get-tuple-element.12), channel_id=1, source_target_pairs={{4,0},{0,4},{12,8},{8,12},{20,16},{16,20},{28,24},{24,28},{5,1},{1... | collective-permute-start | bytes 1572872 | tf_op jit(solution)/shard_map/ppermute | solution.py:24
  18.8 21.6 %collective-permute-start.2 = (bf16[256,1024]{1,0:T(8,128)(2,1)}, bf16[256,1024]{1,0:T(8,128)(2,1)}, u32[]{:S(2)}, u32[]{:S(2)}) collective-permute-start(bf16[256,1024]{1,0:T(8,128)(2,1)} %collective-permute-done), channel_id=1, source_target_pairs={{0,1},{1,2},{2,3},{3,0},{4,5},{5,6},{6,7},{7,4},{8,9},{9,10},{10,1... | collective-permute-start | bytes 1572872 | tf_op jit(solution)/shard_map/ppermute | solution.py:64
  28.9 26.3 %collective-permute-start.6 = (bf16[1024,256]{1,0:T(8,128)(2,1)}, bf16[1024,256]{1,0:T(8,128)(2,1)S(1)}, u32[]{:S(2)}, u32[]{:S(2)}) collective-permute-start(bf16[1024,256]{1,0:T(8,128)(2,1)} %get-tuple-element.12), channel_id=1, source_target_pairs={{8,0},{12,4},{0,8},{4,12},{24,16},{28,20},{16,24},{20,28},{9,1},{1... | collective-permute-start | bytes 1572872 | tf_op jit(solution)/shard_map/ppermute | solution.py:24
  40.5 12.8 %collective-permute-start.5 = (bf16[1024,256]{1,0:T(8,128)(2,1)S(1)}, bf16[1024,256]{1,0:T(8,128)(2,1)S(1)}, u32[]{:S(2)}, u32[]{:S(2)}) collective-permute-start(bf16[1024,256]{1,0:T(8,128)(2,1)S(1)} %copy-done.3), channel_id=1, source_target_pairs={{8,0},{12,4},{0,8},{4,12},{24,16},{28,20},{16,24},{20,28},{9,1},{1... | collective-permute-start | bytes 1572872 | tf_op jit(solution)/shard_map/ppermute | solution.py:24
  43.4 13.0 %collective-permute-start.3 = (bf16[1024,256]{1,0:T(8,128)(2,1)S(1)}, bf16[1024,256]{1,0:T(8,128)(2,1)S(1)}, u32[]{:S(2)}, u32[]{:S(2)}) collective-permute-start(bf16[1024,256]{1,0:T(8,128)(2,1)S(1)} %copy-done.3), channel_id=1, source_target_pairs={{4,0},{0,4},{12,8},{8,12},{20,16},{16,20},{28,24},{24,28},{5,1},{1... | collective-permute-start | bytes 1572872 | tf_op jit(solution)/shard_map/ppermute | solution.py:24
  53.3 25.6 %collective-permute-start.9 = (bf16[1024,256]{1,0:T(8,128)(2,1)S(1)}, bf16[1024,256]{1,0:T(8,128)(2,1)S(1)}, u32[]{:S(2)}, u32[]{:S(2)}) collective-permute-start(bf16[1024,256]{1,0:T(8,128)(2,1)S(1)} %copy-done.3), channel_id=1, source_target_pairs={{16,0},{20,4},{24,8},{28,12},{0,16},{4,20},{8,24},{12,28},{17,1},{... | collective-permute-start | bytes 1572872 | tf_op jit(solution)/shard_map/ppermute | solution.py:24
  55.2 21.5 %collective-permute-start.10 = (bf16[1024,256]{1,0:T(8,128)(2,1)}, bf16[1024,256]{1,0:T(8,128)(2,1)S(1)}, u32[]{:S(2)}, u32[]{:S(2)}) collective-permute-start(bf16[1024,256]{1,0:T(8,128)(2,1)} %get-tuple-element.12), channel_id=1, source_target_pairs={{16,0},{20,4},{24,8},{28,12},{0,16},{4,20},{8,24},{12,28},{17,1},{... | collective-permute-start | bytes 1572872 | tf_op jit(solution)/shard_map/ppermute | solution.py:24
  56.4 22.0 %collective-permute-start.8 = (bf16[1024,256]{1,0:T(8,128)(2,1)S(1)}, bf16[1024,256]{1,0:T(8,128)(2,1)S(1)}, u32[]{:S(2)}, u32[]{:S(2)}) collective-permute-start(bf16[1024,256]{1,0:T(8,128)(2,1)S(1)} %collective-permute-done.6), channel_id=1, source_target_pairs={{4,0},{0,4},{12,8},{8,12},{20,16},{16,20},{28,24},{24,28},{5,1},{1... | collective-permute-start | bytes 1572872 | tf_op jit(solution)/shard_map/ppermute | solution.py:24
  76.6 21.3 %collective-permute-start.28 = (bf16[128,1024]{1,0:T(8,128)(2,1)S(1)}, bf16[128,1024]{1,0:T(8,128)(2,1)S(1)}, u32[]{:S(2)}, u32[]{:S(2)}) collective-permute-start(bf16[128,1024]{1,0:T(8,128)(2,1)S(1)} %copy-done.5), channel_id=1, source_target_pairs={{16,0},{20,4},{24,8},{28,12},{0,16},{4,20},{8,24},{12,28},{17,1},{... | collective-permute-start | bytes 786440 | tf_op jit(solution)/shard_map/ppermute | solution.py:24
  78.9 15.4 %collective-permute-start.13 = (bf16[1024,256]{1,0:T(8,128)(2,1)S(1)}, bf16[1024,256]{1,0:T(8,128)(2,1)}, u32[]{:S(2)}, u32[]{:S(2)}) collective-permute-start(bf16[1024,256]{1,0:T(8,128)(2,1)S(1)} %collective-permute-done.5), channel_id=1, source_target_pairs={{16,0},{20,4},{24,8},{28,12},{0,16},{4,20},{8,24},{12,28},{17,1},{... | collective-permute-start | bytes 1572872 | tf_op jit(solution)/shard_map/ppermute | solution.py:24
  80.5 15.3 %collective-permute-start.14 = (bf16[1024,256]{1,0:T(8,128)(2,1)S(1)}, bf16[1024,256]{1,0:T(8,128)(2,1)}, u32[]{:S(2)}, u32[]{:S(2)}) collective-permute-start(bf16[1024,256]{1,0:T(8,128)(2,1)S(1)} %collective-permute-done.10), channel_id=1, source_target_pairs={{8,0},{12,4},{0,8},{4,12},{24,16},{28,20},{16,24},{20,28},{9,1},{1... | collective-permute-start | bytes 1572872 | tf_op jit(solution)/shard_map/ppermute | solution.py:24
  97.9 45.2 %collective-permute-start.22 = (bf16[128,1024]{1,0:T(8,128)(2,1)S(1)}, bf16[128,1024]{1,0:T(8,128)(2,1)S(1)}, u32[]{:S(2)}, u32[]{:S(2)}) collective-permute-start(bf16[128,1024]{1,0:T(8,128)(2,1)S(1)} %copy-done.5), channel_id=1, source_target_pairs={{8,0},{12,4},{0,8},{4,12},{24,16},{28,20},{16,24},{20,28},{9,1},{1... | collective-permute-start | bytes 786440 | tf_op jit(solution)/shard_map/ppermute | solution.py:24
  99.5 13.3 %collective-permute-start.34 = (bf16[128,1024]{1,0:T(8,128)(2,1)S(1)}, bf16[128,1024]{1,0:T(8,128)(2,1)S(1)}, u32[]{:S(2)}, u32[]{:S(2)}) collective-permute-start(bf16[128,1024]{1,0:T(8,128)(2,1)S(1)} %collective-permute-done.28), channel_id=1, source_target_pairs={{8,0},{12,4},{0,8},{4,12},{24,16},{28,20},{16,24},{20,28},{9,1},{1... | collective-permute-start | bytes 786440 | tf_op jit(solution)/shard_map/ppermute | solution.py:24
  100.4 18.0 %collective-permute-start.32 = (bf16[256,512]{1,0:T(8,128)(2,1)S(1)}, bf16[256,512]{1,0:T(8,128)(2,1)S(1)}, u32[]{:S(2)}, u32[]{:S(2)}) collective-permute-start(bf16[256,512]{1,0:T(8,128)(2,1)S(1)} %get-tuple-element.6), channel_id=1, source_target_pairs={{24,0},{28,4},{16,8},{20,12},{8,16},{12,20},{0,24},{4,28},{25,1},{... | collective-permute-start | bytes 786440 | tf_op jit(solution)/shard_map/ppermute | solution.py:24
  103.8 60.9 %collective-permute-start.19 = (bf16[128,1024]{1,0:T(8,128)(2,1)S(1)}, bf16[128,1024]{1,0:T(8,128)(2,1)S(1)}, u32[]{:S(2)}, u32[]{:S(2)}) collective-permute-start(bf16[128,1024]{1,0:T(8,128)(2,1)S(1)} %copy-done.5), channel_id=1, source_target_pairs={{4,0},{0,4},{12,8},{8,12},{20,16},{16,20},{28,24},{24,28},{5,1},{1... | collective-permute-start | bytes 786440 | tf_op jit(solution)/shard_map/ppermute | solution.py:24
  112.8 55.3 %collective-permute-start.18 = (bf16[128,1024]{1,0:T(8,128)(2,1)}, bf16[128,1024]{1,0:T(8,128)(2,1)S(1)}, u32[]{:S(2)}, u32[]{:S(2)}) collective-permute-start(bf16[128,1024]{1,0:T(8,128)(2,1)} %get-tuple-element.14), channel_id=1, source_target_pairs={{4,0},{0,4},{12,8},{8,12},{20,16},{16,20},{28,24},{24,28},{5,1},{1... | collective-permute-start | bytes 786440 | tf_op jit(solution)/shard_map/ppermute | solution.py:24
  155.1 14.9 %collective-permute-start.36 = (bf16[128,1024]{1,0:T(8,128)(2,1)S(1)}, bf16[128,1024]{1,0:T(8,128)(2,1)S(1)}, u32[]{:S(2)}, u32[]{:S(2)}) collective-permute-start(bf16[128,1024]{1,0:T(8,128)(2,1)S(1)} %collective-permute-done.33), channel_id=1, source_target_pairs={{4,0},{0,4},{12,8},{8,12},{20,16},{16,20},{28,24},{24,28},{5,1},{1... | collective-permute-start | bytes 786440 | tf_op jit(solution)/shard_map/ppermute | solution.py:24
  160.6 15.8 %collective-permute-start.37 = (bf16[128,1024]{1,0:T(8,128)(2,1)S(1)}, bf16[128,1024]{1,0:T(8,128)(2,1)S(1)}, u32[]{:S(2)}, u32[]{:S(2)}) collective-permute-start(bf16[128,1024]{1,0:T(8,128)(2,1)S(1)} %collective-permute-done.34), channel_id=1, source_target_pairs={{4,0},{0,4},{12,8},{8,12},{20,16},{16,20},{28,24},{24,28},{5,1},{1... | collective-permute-start | bytes 786440 | tf_op jit(solution)/shard_map/ppermute | solution.py:24
  165.9 21.6 %collective-permute-start.16 = (bf16[1024,256]{1,0:T(8,128)(2,1)}, bf16[1024,256]{1,0:T(8,128)(2,1)}, u32[]{:S(2)}, u32[]{:S(2)}) collective-permute-start(bf16[1024,256]{1,0:T(8,128)(2,1)} %collective-permute-done.14), channel_id=1, source_target_pairs={{4,0},{0,4},{12,8},{8,12},{20,16},{16,20},{28,24},{24,28},{5,1},{1... | collective-permute-start | bytes 1572872 | tf_op jit(solution)/shard_map/ppermute | solution.py:24
  168.1 20.8 %collective-permute-start.15 = (bf16[1024,256]{1,0:T(8,128)(2,1)}, bf16[1024,256]{1,0:T(8,128)(2,1)}, u32[]{:S(2)}, u32[]{:S(2)}) collective-permute-start(bf16[1024,256]{1,0:T(8,128)(2,1)} %collective-permute-done.13), channel_id=1, source_target_pairs={{4,0},{0,4},{12,8},{8,12},{20,16},{16,20},{28,24},{24,28},{5,1},{1... | collective-permute-start | bytes 1572872 | tf_op jit(solution)/shard_map/ppermute | solution.py:24
  (20 other events, 185.8 us)

commit v2 on v0

v2 whole, which is shorter than its diff:
```python
import math

import jax
import jax.numpy as jnp
from jax import lax
from jax.sharding import PartitionSpec as P


def plane_of(outer):
    cores = 2 if outer % 2 == 0 else 1
    chips = outer // cores
    cols = max(d for d in range(1, math.isqrt(chips) + 1) if chips % d == 0)
    return chips // cols, cols, cores


def place(o, db, da, dc):
    rows, cols, cores = plane_of(lax.axis_size("outer"))
    b, a, c = o // (cols * cores), o // cores % cols, o % cores
    return ((b + db) % rows * cols + (a + da) % cols) * cores + (c + dc) % cores


def shift(array, db, da, dc=0):
    return lax.ppermute(array, "outer", [(place(o, db, da, dc), o) for o in range(lax.axis_size("outer"))])


def split(array, axis):
    half = array.shape[axis] // 2
    return [lax.slice_in_dim(array, 0, half, axis=axis), lax.slice_in_dim(array, half, 2 * half, axis=axis)]


def gather(array, axis):
    rows, cols, _ = plane_of(lax.axis_size("outer"))
    got = {(0, 0): [array]}
    for da in range(1, cols):
        got[0, da] = [shift(array, 0, da)]
    for db in range(1, rows):
        got[db, 0] = [shift(array, db, 0)]
    for db in range(1, rows):
        for da in range(1, cols):
            got[db, da] = [
                shift(split(got[0, da][0], axis)[0], db, 0),
                shift(split(got[db, 0][0], axis)[1], 0, da),
            ]
    return got


def ring(array):
    node = lax.axis_size("node")
    blocks = {0: array}
    up, down = array, array
    for step in range(1, node // 2 + 1):
        up = lax.ppermute(up, "node", [(i, (i + 1) % node) for i in range(node)])
        blocks[node - step] = up
        if 2 * step < node:
            down = lax.ppermute(down, "node", [((i + 1) % node, i) for i in range(node)])
            blocks[step] = down
    return blocks


def stacked(blocks):
    node, me = lax.axis_size("node"), lax.axis_index("node")
    whole = jnp.zeros((node,) + blocks[0].shape, blocks[0].dtype)
    for d, block in blocks.items():
        whole = lax.dynamic_update_index_in_dim(whole, block, (me + d) % node, 0)
    return whole


def body(context, grad_out, out_weight):
    outer, node = lax.axis_size("outer"), lax.axis_size("node")
    rows, cols, cores = plane_of(outer)
    tokens, held = grad_out.shape
    width = out_weight.shape[1]
    norm_scale = 1.0 / math.sqrt(tokens * outer)
    o, z = lax.axis_index("outer"), lax.axis_index("node")
    c = o % cores

    weights = gather(out_weight, 1)
    contexts = gather(context, 0)
    grad = stacked(ring(grad_out))

    def columns(o):
        first = o * width
        if held % width == 0:
            return lax.dynamic_slice(grad, (first // held, 0, first % held), (1, tokens, width))[0]
        return lax.dynamic_slice_in_dim(grad.transpose(1, 0, 2).reshape(tokens, -1), first, width, axis=1)

    def of_kind(kind):
        return jnp.stack([columns(chip * cores + kind) for chip in range(rows * cols)])

    mine = of_kind(c)
    if cores > 1:
        mine = jnp.concatenate([mine, shift(of_kind((c + 1) % cores), 0, 0, 1)], axis=1)
    context_grad = 0.0
    for at, pieces in weights.items():
        chip = place(o, *at, 0) // cores
        block = lax.dynamic_index_in_dim(mine, chip, 0, keepdims=False)
        part = width // len(pieces)
        for h, piece in enumerate(pieces):
            context_grad += lax.dot_general(
                block[:, h * part : (h + 1) * part], piece, (((1,), (1,)), ((), ())), preferred_element_type=jnp.float32
            )
    if cores > 1:
        context_grad = context_grad[:tokens] + shift(context_grad[tokens:], 0, 0, 1)

    def for_chip(db, da):
        return jnp.concatenate([columns(place(o, db, da, dc)) for dc in range(cores)], axis=1)

    weight_grad = 0.0
    for at, pieces in contexts.items():
        db, da = at
        sent = for_chip(-db, -da)
        if db and da and tokens % node == 0:
            part = tokens // node
            share = shift(lax.dynamic_slice_in_dim(sent, z * part, part, axis=0), db, da)
            block = stacked(ring(share)).reshape(tokens, -1)
        else:
            block = shift(sent, db, da) if db or da else sent
        part = tokens // len(pieces)
        for h, piece in enumerate(pieces):
            weight_grad += lax.dot_general(
                piece, block[h * part : (h + 1) * part], (((0,), (0,)), ((), ())), preferred_element_type=jnp.float32
            )
    if cores > 1:
        weight_grad = weight_grad[:, :width] + shift(weight_grad[:, width:], 0, 0, 1)
    return (context_grad.astype(jnp.bfloat16), weight_grad * norm_scale)


def solution(mesh):
    in_specs = (P("outer", "node"), P("outer", "node"), P("node", "outer"))
    out_specs = (P("outer", "node"), P("node", "outer"))
    return jax.shard_map(body, mesh=mesh, in_specs=in_specs, out_specs=out_specs, check_vma=False)
```

time: 179 us -> 109 us (0.61)
  waiting for transfers between devices: 112 us -> 59.3 us
  blocking collectives: 35.8 us -> 0 us
  starting transfers between devices: 0.12 us -> 23.9 us
  between operations: 13.7 us -> 1.59 us
  local copies, waits for them, and re-layouts: 4.43 us -> 11.3 us
  matrix products: 13.2 us -> 10.7 us
    all_gather x3 -> x0, waiting for transfers between devices: 110 us -> none  [the longest x1 51.2 us: body(): lax.all_gather(out_weight, 'outer', axis=1, tiled=True)]
    ppermute x0 -> x20, waiting for transfers between devices: none -> 59.3 us  [the longest x14 42.8 us: shift(): lax.ppermute(array, 'outer', [(place(o, db, da, dc), o) for o in range(la...]
    all_to_all x1 -> x0, blocking collectives: 35.8 us -> none  [body(): lax.all_to_all(grad_full, 'outer', split_axis=1, concat_axis=0, tiled=True)]
    ppermute x0 -> x20, starting transfers between devices: none -> 23.9 us  [the longest x14 15.5 us: shift(): lax.ppermute(array, 'outer', [(place(o, db, da, dc), o) for o in range(la...]
    slice x0 -> x7, local copies, waits for them, and re-layouts: none -> 3.42 us  [the longest x2 2.04 us: split(): lax.slice_in_dim(array, 0, half, axis=axis)]
    dynamic_update_slice x0 -> x8, local copies, waits for them, and re-layouts: none -> 3.33 us  [stacked(): whole = lax.dynamic_update_index_in_dim(whole, block, (me + d) % node, 0)]
    dot_general x2 -> x10, matrix products: 13.2 us -> 10.7 us  [the longest x5 6.25 us: body(): lax.dot_general(piece, block[h * part:(h + 1) * part], (((0,), (0,)), (()...]
    all_to_all x1 -> x0, local copies, waits for them, and re-layouts: 2.39 us -> none  [body(): lax.all_to_all(grad_full, 'outer', split_axis=1, concat_axis=0, tiled=True)]
  transfers between devices with their start and end apart: 3 -> 20, of which waited for: 3 -> 8; matrix products, arithmetic and copies ran while one was open for 5% -> 18% of each run, Pallas kernels for 0% -> 0%
where the time goes in v2:
time: 109 us
  waiting for transfers between devices  59.3 us (54%)
  starting transfers between devices  23.9 us (22%)
  local copies, waits for them, and re-layouts  11.3 us (10%)
  matrix products  10.7 us (10%)
  other arithmetic  1.77 us (2%)
  between operations  1.59 us (1%)
    ppermute x14, waiting for transfers between devices, shift(): lax.ppermute(array, 'outer', [(place(o, db, da, dc), o) for o in range(la...  42.8 us
    ppermute x14, starting transfers between devices, shift(): lax.ppermute(array, 'outer', [(place(o, db, da, dc), o) for o in range(la...  15.5 us
    ppermute x4, waiting for transfers between devices, ring(): up = lax.ppermute(up, 'node', [(i, (i + 1) % node) for i in range(node)])  12.6 us
    dot_general x5, matrix products, body(): lax.dot_general(piece, block[h * part:(h + 1) * part], (((0,), (0,)), (()...  6.25 us
    ppermute x2, starting transfers between devices, ring(): lax.ppermute(down, 'node', [((i + 1) % node, i) for i in range(node)])  5.18 us
    dot_general x5, matrix products, body(): lax.dot_general(block[:, h * part:(h + 1) * part], piece, (((1,), (1,)),...  4.46 us
    ppermute x2, waiting for transfers between devices, ring(): lax.ppermute(down, 'node', [((i + 1) % node, i) for i in range(node)])  3.93 us
    unnamed x7, local copies, waits for them, and re-layouts  3.66 us
  transfers between devices with their start and end apart: 20, of which 8 were waited for; matrix products, arithmetic and copies ran while one was open for 18% of the time, Pallas kernels for 0%

profile of v2, /device:TPU:0, one launch (start us, length us, event | category | flops | bytes accessed | tf_op | source)
XLA Modules:
  0.0 108.6 jit_solution(15158106074417384223)
XLA Ops:
  0.6 3.0 %collective-permute-start.12 = (bf16[256,1024]{1,0:T(8,128)(2,1)}, bf16[256,1024]{1,0:T(8,128)(2,1)}, u32[]{:S(2)}, u32[]{:S(2)}) collective-permute-start(bf16[256,1024]{1,0:T(8,128)(2,1)} %param.3), channel_id=1, source_target_pairs={{16,0},{20,4},{24,8},{28,12},{0,16},{4,20},{8,24},{12,28},{17,1},{... | collective-permute-start | bytes 1572872 | tf_op jit(solution)/shard_map/ppermute | solution.py:23
  3.7 1.9 %collective-permute-start.4 = (bf16[1024,512]{1,0:T(8,128)(2,1)}, bf16[1024,512]{1,0:T(8,128)(2,1)}, u32[]{:S(2)}, u32[]{:S(2)}) collective-permute-start(bf16[1024,512]{1,0:T(8,128)(2,1)} %param.5), channel_id=1, source_target_pairs={{8,0},{12,4},{0,8},{4,12},{24,16},{28,20},{16,24},{20,28},{9,1},{1... | collective-permute-start | bytes 3145736 | tf_op jit(solution)/shard_map/ppermute | solution.py:23
  5.7 1.6 %collective-permute-start = (bf16[256,1024]{1,0:T(8,128)(2,1)}, bf16[256,1024]{1,0:T(8,128)(2,1)}, u32[]{:S(2)}, u32[]{:S(2)}) collective-permute-start(bf16[256,1024]{1,0:T(8,128)(2,1)} %param.4), channel_id=1, source_target_pairs={{0,1},{1,2},{2,3},{3,0},{4,5},{5,6},{6,7},{7,4},{8,9},{9,10},{10,1... | collective-permute-start | bytes 1572872 | tf_op jit(solution)/shard_map/ppermute | solution.py:52
  7.8 9.0 %collective-permute-done.12 = bf16[256,1024]{1,0:T(8,128)(2,1)} collective-permute-done((bf16[256,1024]{1,0:T(8,128)(2,1)}, bf16[256,1024]{1,0:T(8,128)(2,1)}, u32[]{:S(2)}, u32[]{:S(2)}) %collective-permute-start.12) | collective-permute-done | bytes 524320 | tf_op jit(solution)/shard_map/ppermute | solution.py:23
  16.7 4.1 %collective-permute-start.1 = (bf16[256,1024]{1,0:T(8,128)(2,1)}, bf16[256,1024]{1,0:T(8,128)(2,1)}, u32[]{:S(2)}, u32[]{:S(2)}) collective-permute-start(bf16[256,1024]{1,0:T(8,128)(2,1)} %param.4), channel_id=1, source_target_pairs={{1,0},{2,1},{3,2},{0,3},{5,4},{6,5},{7,6},{4,7},{9,8},{10,9},{11,1... | collective-permute-start | bytes 1572872 | tf_op jit(solution)/shard_map/ppermute | solution.py:55
  23.7 16.2 %collective-permute-done.10 = bf16[256,1024]{1,0:T(8,128)(2,1)} collective-permute-done((bf16[256,1024]{1,0:T(8,128)(2,1)}, bf16[256,1024]{1,0:T(8,128)(2,1)}, u32[]{:S(2)}, u32[]{:S(2)}) %collective-permute-start.10) | collective-permute-done | bytes 524320 | tf_op jit(solution)/shard_map/ppermute | solution.py:23
  39.9 1.6 %collective-permute-start.18 = (bf16[128,1024]{1,0:T(8,128)(2,1)S(1)}, bf16[128,1024]{1,0:T(8,128)(2,1)S(1)}, u32[]{:S(2)}, u32[]{:S(2)}) collective-permute-start(bf16[128,1024]{1,0:T(8,128)(2,1)S(1)} %slice.65), channel_id=1, source_target_pairs={{8,0},{12,4},{0,8},{4,12},{24,16},{28,20},{16,24},{20,28},{9,1},{1... | collective-permute-start | bytes 786440 | tf_op jit(solution)/shard_map/ppermute | solution.py:23
  42.5 1.1 bitcast_dynamic-update-slice_fusion.2
  43.6 1.6 %collective-permute-start.17 = (bf16[128,1024]{1,0:T(8,128)(2,1)S(1)}, bf16[128,1024]{1,0:T(8,128)(2,1)S(1)}, u32[]{:S(2)}, u32[]{:S(2)}) collective-permute-start(bf16[128,1024]{1,0:T(8,128)(2,1)S(1)} %slice.63), channel_id=1, source_target_pairs={{16,0},{20,4},{24,8},{28,12},{0,16},{4,20},{8,24},{12,28},{17,1},{... | collective-permute-start | bytes 786440 | tf_op jit(solution)/shard_map/ppermute | solution.py:23
  49.9 2.7 %collective-permute-start.13 = (bf16[64,1024]{1,0:T(8,128)(2,1)S(1)}, bf16[64,1024]{1,0:T(8,128)(2,1)S(1)}, u32[]{:S(2)}, u32[]{:S(2)}) collective-permute-start(bf16[64,1024]{1,0:T(8,128)(2,1)S(1)} %fusion.23), channel_id=1, source_target_pairs={{24,0},{28,4},{16,8},{20,12},{8,16},{12,20},{0,24},{4,28},{25,1},{... | collective-permute-start | bytes 393224 | tf_op jit(solution)/shard_map/ppermute | solution.py:23
  53.0 8.7 %collective-permute-done.13 = bf16[64,1024]{1,0:T(8,128)(2,1)S(1)} collective-permute-done((bf16[64,1024]{1,0:T(8,128)(2,1)S(1)}, bf16[64,1024]{1,0:T(8,128)(2,1)S(1)}, u32[]{:S(2)}, u32[]{:S(2)}) %collective-permute-start.13) | collective-permute-done | bytes 131104 | tf_op jit(solution)/shard_map/ppermute | solution.py:23
  61.7 1.6 %collective-permute-start.14 = (bf16[64,1024]{1,0:T(8,128)(2,1)S(1)}, bf16[64,1024]{1,0:T(8,128)(2,1)S(1)}, u32[]{:S(2)}, u32[]{:S(2)}) collective-permute-start(bf16[64,1024]{1,0:T(8,128)(2,1)S(1)} %collective-permute-done.13), channel_id=1, source_target_pairs={{0,1},{1,2},{2,3},{3,0},{4,5},{5,6},{6,7},{7,4},{8,9},{9,10},{10,1... | collective-permute-start | bytes 393224 | tf_op jit(solution)/shard_map/ppermute | solution.py:52
  63.4 5.9 %collective-permute-done.14 = bf16[64,1024]{1,0:T(8,128)(2,1)S(1)} collective-permute-done((bf16[64,1024]{1,0:T(8,128)(2,1)S(1)}, bf16[64,1024]{1,0:T(8,128)(2,1)S(1)}, u32[]{:S(2)}, u32[]{:S(2)}) %collective-permute-start.14) | collective-permute-done | bytes 131104 | tf_op jit(solution)/shard_map/ppermute | solution.py:52
  70.3 3.9 %collective-permute-done.15 = bf16[64,1024]{1,0:T(8,128)(2,1)S(1)} collective-permute-done((bf16[64,1024]{1,0:T(8,128)(2,1)S(1)}, bf16[64,1024]{1,0:T(8,128)(2,1)S(1)}, u32[]{:S(2)}, u32[]{:S(2)}) %collective-permute-start.15) | collective-permute-done | bytes 131104 | tf_op jit(solution)/shard_map/ppermute | solution.py:55
  74.3 6.7 %collective-permute-done.16 = bf16[64,1024]{1,0:T(8,128)(2,1)S(1)} collective-permute-done((bf16[64,1024]{1,0:T(8,128)(2,1)S(1)}, bf16[64,1024]{1,0:T(8,128)(2,1)S(1)}, u32[]{:S(2)}, u32[]{:S(2)}) %collective-permute-start.16) | collective-permute-done | bytes 131104 | tf_op jit(solution)/shard_map/ppermute | solution.py:52
  81.0 1.2 %collective-permute-start.9 = (bf16[256,1024]{1,0:T(8,128)(2,1)S(1)}, bf16[256,1024]{1,0:T(8,128)(2,1)S(1)}, u32[]{:S(2)}, u32[]{:S(2)}) collective-permute-start(bf16[256,1024]{1,0:T(8,128)(2,1)S(1)} %pad_maximum_fusion.2), channel_id=1, source_target_pairs={{8,0},{12,4},{0,8},{4,12},{24,16},{28,20},{16,24},{20,28},{9,1},{1... | collective-permute-start | bytes 1572872 | tf_op jit(solution)/shard_map/ppermute | solution.py:23
  82.3 1.1 %collective-permute-start.11 = (bf16[256,1024]{1,0:T(8,128)(2,1)S(1)}, bf16[256,1024]{1,0:T(8,128)(2,1)S(1)}, u32[]{:S(2)}, u32[]{:S(2)}) collective-permute-start(bf16[256,1024]{1,0:T(8,128)(2,1)S(1)} %pad_maximum_fusion.3), channel_id=1, source_target_pairs={{16,0},{20,4},{24,8},{28,12},{0,16},{4,20},{8,24},{12,28},{17,1},{... | collective-permute-start | bytes 1572872 | tf_op jit(solution)/shard_map/ppermute | solution.py:23
  85.0 6.6 %collective-permute-done.11 = bf16[256,1024]{1,0:T(8,128)(2,1)S(1)} collective-permute-done((bf16[256,1024]{1,0:T(8,128)(2,1)S(1)}, bf16[256,1024]{1,0:T(8,128)(2,1)S(1)}, u32[]{:S(2)}, u32[]{:S(2)}) %collective-permute-start.11) | collective-permute-done | bytes 524320 | tf_op jit(solution)/shard_map/ppermute | solution.py:23
  91.5 1.8 %fusion.30 = f32[1024,1024]{1,0:T(8,128)S(1)} fusion(bf16[256,1024]{1,0:T(8,128)(2,1)S(1)} %collective-permute-done.11, bf16[256,1024]{1,0:T(8,128)(2,1)} %collective-permute-done.12), kind=kOutput, calls=%fused_computation.61 | convolution fusion | flops 536870912 | bytes 5242880 | tf_op jit(solution)/shard_map/dot_general | solution.py:120
  93.3 1.8 %fusion.29 = f32[1024,1024]{1,0:T(8,128)S(1)} fusion(bf16[256,1024]{1,0:T(8,128)(2,1)S(1)} %collective-permute-done.9, bf16[256,1024]{1,0:T(8,128)(2,1)} %collective-permute-done.10), kind=kOutput, calls=%fused_computation.60 | convolution fusion | flops 536870912 | bytes 5242880 | tf_op jit(solution)/shard_map/dot_general | solution.py:120
  95.2 1.2 %add_bitcast_fusion = f32[1024,1024]{0,1:T(8,128)S(1)} fusion(f32[1024,1024]{1,0:T(8,128)S(1)} %fusion.32, f32[1024,1024]{1,0:T(8,128)S(1)} %fusion.31, f32[1024,1024]{1,0:T(8,128)S(1)} %fusion.30, f32[1024,1024]{1,0:T(8,128)S(1)} %fusion.29, bf16[256,1024]{1,0:T(8,128)(2,1)S(1)} %copy-done.1, bf16[256,512]{1,0:T(8,128)(2,1)S(1)} %get-tuple-element.11, ...), kind=kOutput, calls=%fused_computation | convolution fusion | flops 542113792 | bytes 22020096 | tf_op jit(solution)/shard_map/dot_general | solution.py:120
  99.4 2.0 %fusion.10 = f32[512,1024]{1,0:T(8,128)S(1)} fusion(bf16[1024,512]{1,0:T(8,128)(2,1)} %collective-permute-done.4, bf16[4,512,512]{2,1,0:T(8,128)(2,1)S(1)} %pad_maximum_fusion, s32[]{:T(128)S(6)} %select_n.506), kind=kOutput, calls=%fused_computation.18 | convolution fusion | flops 536870912 | bytes 3670020 | tf_op jit(solution)/shard_map/dot_general | solution.py:99
  103.1 2.3 %collective-permute-done.8 = f32[256,1024]{1,0:T(8,128)S(1)} collective-permute-done((f32[256,1024]{1,0:T(8,128)S(1)}, f32[256,1024]{1,0:T(8,128)S(1)}, u32[]{:S(2)}, u32[]{:S(2)}) %collective-permute-start.8) | collective-permute-done | bytes 1048608 | tf_op jit(solution)/shard_map/ppermute | solution.py:23
  106.8 1.8 %copy.5 = f32[1024,512]{1,0:T(8,128)} copy(f32[1024,512]{0,1:T(8,128)S(1)} %fusion) | data formatting | bytes 4194304
  (60 shorter events, 17.6 us)
Async XLA Ops:
  0.6 16.1 %collective-permute-start.12 = (bf16[256,1024]{1,0:T(8,128)(2,1)}, bf16[256,1024]{1,0:T(8,128)(2,1)}, u32[]{:S(2)}, u32[]{:S(2)}) collective-permute-start(bf16[256,1024]{1,0:T(8,128)(2,1)} %param.3), channel_id=1, source_target_pairs={{16,0},{20,4},{24,8},{28,12},{0,16},{4,20},{8,24},{12,28},{17,1},{... | collective-permute-start | bytes 1572872 | tf_op jit(solution)/shard_map/ppermute | solution.py:23
  3.7 42.6 %collective-permute-start.5 = (bf16[1024,512]{1,0:T(8,128)(2,1)}, bf16[1024,512]{1,0:T(8,128)(2,1)S(1)}, u32[]{:S(2)}, u32[]{:S(2)}) collective-permute-start(bf16[1024,512]{1,0:T(8,128)(2,1)} %param.5), channel_id=1, source_target_pairs={{16,0},{20,4},{24,8},{28,12},{0,16},{4,20},{8,24},{12,28},{17,1},{... | collective-permute-start | bytes 3145736 | tf_op jit(solution)/shard_map/ppermute | solution.py:23
  3.7 43.2 %collective-permute-start.4 = (bf16[1024,512]{1,0:T(8,128)(2,1)}, bf16[1024,512]{1,0:T(8,128)(2,1)}, u32[]{:S(2)}, u32[]{:S(2)}) collective-permute-start(bf16[1024,512]{1,0:T(8,128)(2,1)} %param.5), channel_id=1, source_target_pairs={{8,0},{12,4},{0,8},{4,12},{24,16},{28,20},{16,24},{20,28},{9,1},{1... | collective-permute-start | bytes 3145736 | tf_op jit(solution)/shard_map/ppermute | solution.py:23
  5.7 16.3 %collective-permute-start = (bf16[256,1024]{1,0:T(8,128)(2,1)}, bf16[256,1024]{1,0:T(8,128)(2,1)}, u32[]{:S(2)}, u32[]{:S(2)}) collective-permute-start(bf16[256,1024]{1,0:T(8,128)(2,1)} %param.4), channel_id=1, source_target_pairs={{0,1},{1,2},{2,3},{3,0},{4,5},{5,6},{6,7},{7,4},{8,9},{9,10},{10,1... | collective-permute-start | bytes 1572872 | tf_op jit(solution)/shard_map/ppermute | solution.py:52
  7.2 32.7 %collective-permute-start.10 = (bf16[256,1024]{1,0:T(8,128)(2,1)}, bf16[256,1024]{1,0:T(8,128)(2,1)}, u32[]{:S(2)}, u32[]{:S(2)}) collective-permute-start(bf16[256,1024]{1,0:T(8,128)(2,1)} %param.3), channel_id=1, source_target_pairs={{8,0},{12,4},{0,8},{4,12},{24,16},{28,20},{16,24},{20,28},{9,1},{1... | collective-permute-start | bytes 1572872 | tf_op jit(solution)/shard_map/ppermute | solution.py:23
  16.7 26.9 %collective-permute-start.1 = (bf16[256,1024]{1,0:T(8,128)(2,1)}, bf16[256,1024]{1,0:T(8,128)(2,1)}, u32[]{:S(2)}, u32[]{:S(2)}) collective-permute-start(bf16[256,1024]{1,0:T(8,128)(2,1)} %param.4), channel_id=1, source_target_pairs={{1,0},{2,1},{3,2},{0,3},{5,4},{6,5},{7,6},{4,7},{9,8},{10,9},{11,1... | collective-permute-start | bytes 1572872 | tf_op jit(solution)/shard_map/ppermute | solution.py:55
  20.9 1.1 copy-start.2
  22.0 26.4 %collective-permute-start.2 = (bf16[256,1024]{1,0:T(8,128)(2,1)}, bf16[256,1024]{1,0:T(8,128)(2,1)}, u32[]{:S(2)}, u32[]{:S(2)}) collective-permute-start(bf16[256,1024]{1,0:T(8,128)(2,1)} %collective-permute-done), channel_id=1, source_target_pairs={{0,1},{1,2},{2,3},{3,0},{4,5},{5,6},{6,7},{7,4},{8,9},{9,10},{10,1... | collective-permute-start | bytes 1572872 | tf_op jit(solution)/shard_map/ppermute | solution.py:52
  39.9 42.4 %collective-permute-start.18 = (bf16[128,1024]{1,0:T(8,128)(2,1)S(1)}, bf16[128,1024]{1,0:T(8,128)(2,1)S(1)}, u32[]{:S(2)}, u32[]{:S(2)}) collective-permute-start(bf16[128,1024]{1,0:T(8,128)(2,1)S(1)} %slice.65), channel_id=1, source_target_pairs={{8,0},{12,4},{0,8},{4,12},{24,16},{28,20},{16,24},{20,28},{9,1},{1... | collective-permute-start | bytes 786440 | tf_op jit(solution)/shard_map/ppermute | solution.py:23
  43.6 40.5 %collective-permute-start.17 = (bf16[128,1024]{1,0:T(8,128)(2,1)S(1)}, bf16[128,1024]{1,0:T(8,128)(2,1)S(1)}, u32[]{:S(2)}, u32[]{:S(2)}) collective-permute-start(bf16[128,1024]{1,0:T(8,128)(2,1)S(1)} %slice.63), channel_id=1, source_target_pairs={{16,0},{20,4},{24,8},{28,12},{0,16},{4,20},{8,24},{12,28},{17,1},{... | collective-permute-start | bytes 786440 | tf_op jit(solution)/shard_map/ppermute | solution.py:23
  46.3 55.5 %collective-permute-start.7 = (bf16[1024,256]{1,0:T(8,128)(2,1)S(1)}, bf16[1024,256]{1,0:T(8,128)(2,1)S(1)}, u32[]{:S(2)}, u32[]{:S(2)}) collective-permute-start(bf16[1024,256]{1,0:T(8,128)(2,1)S(1)} %slice.59), channel_id=1, source_target_pairs={{8,0},{12,4},{0,8},{4,12},{24,16},{28,20},{16,24},{20,28},{9,1},{1... | collective-permute-start | bytes 1572872 | tf_op jit(solution)/shard_map/ppermute | solution.py:23
  48.0 53.4 %collective-permute-start.6 = (bf16[1024,256]{1,0:T(8,128)(2,1)S(1)}, bf16[1024,256]{1,0:T(8,128)(2,1)S(1)}, u32[]{:S(2)}, u32[]{:S(2)}) collective-permute-start(bf16[1024,256]{1,0:T(8,128)(2,1)S(1)} %slice.57), channel_id=1, source_target_pairs={{16,0},{20,4},{24,8},{28,12},{0,16},{4,20},{8,24},{12,28},{17,1},{... | collective-permute-start | bytes 1572872 | tf_op jit(solution)/shard_map/ppermute | solution.py:23
  49.9 11.9 %collective-permute-start.13 = (bf16[64,1024]{1,0:T(8,128)(2,1)S(1)}, bf16[64,1024]{1,0:T(8,128)(2,1)S(1)}, u32[]{:S(2)}, u32[]{:S(2)}) collective-permute-start(bf16[64,1024]{1,0:T(8,128)(2,1)S(1)} %fusion.23), channel_id=1, source_target_pairs={{24,0},{28,4},{16,8},{20,12},{8,16},{12,20},{0,24},{4,28},{25,1},{... | collective-permute-start | bytes 393224 | tf_op jit(solution)/shard_map/ppermute | solution.py:23
  61.7 7.5 %collective-permute-start.14 = (bf16[64,1024]{1,0:T(8,128)(2,1)S(1)}, bf16[64,1024]{1,0:T(8,128)(2,1)S(1)}, u32[]{:S(2)}, u32[]{:S(2)}) collective-permute-start(bf16[64,1024]{1,0:T(8,128)(2,1)S(1)} %collective-permute-done.13), channel_id=1, source_target_pairs={{0,1},{1,2},{2,3},{3,0},{4,5},{5,6},{6,7},{7,4},{8,9},{9,10},{10,1... | collective-permute-start | bytes 393224 | tf_op jit(solution)/shard_map/ppermute | solution.py:52
  69.3 5.0 %collective-permute-start.15 = (bf16[64,1024]{1,0:T(8,128)(2,1)S(1)}, bf16[64,1024]{1,0:T(8,128)(2,1)S(1)}, u32[]{:S(2)}, u32[]{:S(2)}) collective-permute-start(bf16[64,1024]{1,0:T(8,128)(2,1)S(1)} %collective-permute-done.13), channel_id=1, source_target_pairs={{1,0},{2,1},{3,2},{0,3},{5,4},{6,5},{7,6},{4,7},{9,8},{10,9},{11,1... | collective-permute-start | bytes 393224 | tf_op jit(solution)/shard_map/ppermute | solution.py:55
  74.2 6.8 %collective-permute-start.16 = (bf16[64,1024]{1,0:T(8,128)(2,1)S(1)}, bf16[64,1024]{1,0:T(8,128)(2,1)S(1)}, u32[]{:S(2)}, u32[]{:S(2)}) collective-permute-start(bf16[64,1024]{1,0:T(8,128)(2,1)S(1)} %collective-permute-done.14), channel_id=1, source_target_pairs={{0,1},{1,2},{2,3},{3,0},{4,5},{5,6},{6,7},{7,4},{8,9},{9,10},{10,1... | collective-permute-start | bytes 393224 | tf_op jit(solution)/shard_map/ppermute | solution.py:52
  81.0 12.3 %collective-permute-start.9 = (bf16[256,1024]{1,0:T(8,128)(2,1)S(1)}, bf16[256,1024]{1,0:T(8,128)(2,1)S(1)}, u32[]{:S(2)}, u32[]{:S(2)}) collective-permute-start(bf16[256,1024]{1,0:T(8,128)(2,1)S(1)} %pad_maximum_fusion.2), channel_id=1, source_target_pairs={{8,0},{12,4},{0,8},{4,12},{24,16},{28,20},{16,24},{20,28},{9,1},{1... | collective-permute-start | bytes 1572872 | tf_op jit(solution)/shard_map/ppermute | solution.py:23
  82.3 9.2 %collective-permute-start.11 = (bf16[256,1024]{1,0:T(8,128)(2,1)S(1)}, bf16[256,1024]{1,0:T(8,128)(2,1)S(1)}, u32[]{:S(2)}, u32[]{:S(2)}) collective-permute-start(bf16[256,1024]{1,0:T(8,128)(2,1)S(1)} %pad_maximum_fusion.3), channel_id=1, source_target_pairs={{16,0},{20,4},{24,8},{28,12},{0,16},{4,20},{8,24},{12,28},{17,1},{... | collective-permute-start | bytes 1572872 | tf_op jit(solution)/shard_map/ppermute | solution.py:23
  84.2 12.5 %collective-permute-start.3 = (bf16[4,256,512]{2,1,0:T(8,128)(2,1)S(1)}, bf16[4,256,512]{2,1,0:T(8,128)(2,1)S(1)}, u32[]{:S(2)}, u32[]{:S(2)}) collective-permute-start(bf16[4,256,512]{2,1,0:T(8,128)(2,1)S(1)} %pad_maximum_fusion.1), channel_id=1, source_target_pairs={{4,0},{0,4},{12,8},{8,12},{20,16},{16,20},{28,24},{24,28},{5,1},{1... | collective-permute-start | bytes 3145736 | tf_op jit(solution)/shard_map/ppermute | solution.py:23
  93.3 1.9 %copy-start.1 = (bf16[256,1024]{1,0:T(8,128)(2,1)S(1)}, bf16[256,1024]{1,0:T(8,128)(2,1)}, u32[]{:S(2)}) copy-start(bf16[256,1024]{1,0:T(8,128)(2,1)} %param.3) | copy-start | bytes 1572868
  96.6 9.7 %collective-permute-start.19 = (f32[1024,512]{0,1:T(8,128)S(1)}, f32[1024,512]{0,1:T(8,128)S(1)}, u32[]{:S(2)}, u32[]{:S(2)}) collective-permute-start(f32[1024,512]{0,1:T(8,128)S(1)} %slice.67), channel_id=1, source_target_pairs={{4,0},{0,4},{12,8},{8,12},{20,16},{16,20},{28,24},{24,28},{5,1},{1... | collective-permute-start | bytes 6291464 | tf_op jit(solution)/shard_map/ppermute | solution.py:23
  96.7 1.2 %copy-start = (bf16[1024,512]{1,0:T(8,128)(2,1)S(1)}, bf16[1024,512]{1,0:T(8,128)(2,1)}, u32[]{:S(2)}) copy-start(bf16[1024,512]{1,0:T(8,128)(2,1)} %param.5) | copy-start | bytes 3145732
  102.5 2.8 %collective-permute-start.8 = (f32[256,1024]{1,0:T(8,128)S(1)}, f32[256,1024]{1,0:T(8,128)S(1)}, u32[]{:S(2)}, u32[]{:S(2)}) collective-permute-start(f32[256,1024]{1,0:T(8,128)S(1)} %slice.61), channel_id=1, source_target_pairs={{4,0},{0,4},{12,8},{8,12},{20,16},{16,20},{28,24},{24,28},{5,1},{1... | collective-permute-start | bytes 3145736 | tf_op jit(solution)/shard_map/ppermute | solution.py:23

commit v3 on v2

v3 whole, which is shorter than its diff:
```python
import functools
import math

import jax
import jax.numpy as jnp
from jax import lax
from jax.experimental import pallas as pl
from jax.experimental.pallas import tpu as pltpu
from jax.sharding import PartitionSpec as P


def plane_of(outer):
    cores = 2 if outer % 2 == 0 else 1
    chips = outer // cores
    cols = max(d for d in range(1, math.isqrt(chips) + 1) if chips % d == 0)
    return chips // cols, cols, cores


def place(o, db, da, dc):
    rows, cols, cores = plane_of(lax.axis_size("outer"))
    b, a, c = o // (cols * cores), o // cores % cols, o % cores
    return ((b + db) % rows * cols + (a + da) % cols) * cores + (c + dc) % cores


def shift(array, db, da, dc=0):
    return lax.ppermute(array, "outer", [(place(o, db, da, dc), o) for o in range(lax.axis_size("outer"))])


def sibling(array):
    return shift(array, 0, 0, 1)


def along_node(array, d):
    node = lax.axis_size("node")
    return lax.ppermute(array, "node", [((i + d) % node, i) for i in range(node)])


def after(arrays, done):
    return lax.optimization_barrier((arrays, done))[0]


def ring(array):
    node = lax.axis_size("node")
    blocks = {0: array}
    up, down = array, array
    for step in range(1, node // 2 + 1):
        up = along_node(up, -1)
        blocks[node - step] = up
        if 2 * step < node:
            down = along_node(down, 1)
            blocks[step] = down
    return blocks


def stacked(blocks):
    node, me = lax.axis_size("node"), lax.axis_index("node")
    whole = jnp.zeros((node,) + blocks[0].shape, blocks[0].dtype)
    for d, block in blocks.items():
        whole = lax.dynamic_update_index_in_dim(whole, block, (me + d) % node, 0)
    return whole


def pack_kernel(weight, context, out):
    taken, width = weight.shape
    tokens = context.shape[0]
    half = taken // 2
    out[:half] = weight[:half]
    for i in range(taken // width):
        out[half + i * tokens : half + (i + 1) * tokens] = context[:, i * width : (i + 1) * width]
    out[-half:] = weight[half:]


def packed(weight, context):
    taken, width = weight.shape
    high = taken + taken // width * context.shape[0]
    return pl.pallas_call(
        pack_kernel,
        out_shape=jax.ShapeDtypeStruct((high, width), weight.dtype),
        in_specs=[pl.BlockSpec(memory_space=pltpu.VMEM)] * 2,
        out_specs=pl.BlockSpec(memory_space=pltpu.VMEM),
        compiler_params=pltpu.CompilerParams(vmem_limit_bytes=16 * 2**20),
        cost_estimate=pl.CostEstimate(flops=0, bytes_accessed=4 * high * width, transcendentals=0),
    )(weight, context)


def body(context, grad_out, out_weight):
    outer, node = lax.axis_size("outer"), lax.axis_size("node")
    rows, cols, cores = plane_of(outer)
    tokens, held = grad_out.shape
    taken, width = out_weight.shape
    norm_scale = 1.0 / math.sqrt(tokens * outer)
    o, z = lax.axis_index("outer"), lax.axis_index("node")
    c = o % cores
    row = [(0, da) for da in range(1, cols)]
    column = [(db, 0) for db in range(1, rows)]
    across = [(db, da) for db in range(1, rows) for da in range(1, cols)]
    half, slabs = taken // 2, taken // width
    high = taken + slabs * tokens

    def dot(left, right, dim):
        return lax.dot_general(left, right, (((dim,), (dim,)), ((), ())), preferred_element_type=jnp.float32)

    def both(array):
        return [array, sibling(array)] if cores > 1 else [array]

    def wide(slab):
        return jnp.concatenate([slab[i * tokens : (i + 1) * tokens] for i in range(slabs)], axis=1)

    around = ring(grad_out)
    pack = packed(out_weight, context)
    packs = {at: shift(pack, *at) for at in row + column}
    contexts = {(0, 0): both(context)}
    grad = stacked(around)

    def columns(o):
        first = o * width
        if held % width == 0:
            return lax.dynamic_slice(grad, (first // held, 0, first % held), (1, tokens, width))[0]
        return lax.dynamic_slice_in_dim(grad.transpose(1, 0, 2).reshape(tokens, -1), first, width, axis=1)

    def of_kind(kind):
        return jnp.stack([columns(chip * cores + kind) for chip in range(rows * cols)])

    def for_chip(db, da):
        return jnp.concatenate([columns(place(o, db, da, dc)) for dc in range(cores)], axis=1)

    upper = {(db, da): shift(packs[0, da][: high // 2], db, 0) for db, da in across}
    lower = {(db, da): shift(packs[db, 0][high // 2 :], 0, da) for db, da in across}

    pair = 2 if node % 2 == 0 else 1
    part = tokens // pair
    shares = {
        (db, da): lax.dynamic_slice_in_dim(for_chip(-db, -da), z % pair * part, part, axis=0) for db, da in across
    }
    shares = {at: shift(share, *at) for at, share in after(shares, packs).items()}
    mine = of_kind(c)
    if cores > 1:
        mine = jnp.concatenate([mine, sibling(after(of_kind((c + 1) % cores), packs))], axis=1)
    sent = {(db, da): for_chip(-db, -da) for db, da in row + column}
    blocks = {at: shift(block, *at) for at, block in after(sent, (shares, mine)).items()}
    for at, share in shares.items():
        if pair > 1:
            other = lax.ppermute(share, "node", [(i ^ 1, i) for i in range(node)])
            share = jnp.where(z % 2 == 0, jnp.concatenate([share, other]), jnp.concatenate([other, share]))
        blocks[at] = share
    near = jnp.stack([wide(packs[at][half : half + slabs * tokens]) for at in row + column])
    for at, pair in zip(row + column, zip(*both(after(near, [blocks[at] for at in across])))):
        contexts[at] = pair
    for at in across:
        contexts[at] = both(wide(jnp.concatenate([upper[at][half:], lower[at][: high // 2 - half]], axis=0)))

    sides = []
    weights = {(0, 0): (out_weight[:half], out_weight[half:])}
    weights |= {at: (packs[at][:half], packs[at][-half:]) for at in row + column}
    weights |= {at: (upper[at][:half], lower[at][-half:]) for at in across}
    for h in range(2):
        side = 0.0
        for at, pair in weights.items():
            side += dot(lax.dynamic_index_in_dim(mine, place(o, *at, 0) // cores, 0, keepdims=False), pair[h], 1)
        sides.append(side)
    context_grad = jnp.concatenate([side[:tokens] for side in sides], axis=1)
    if cores > 1:
        theirs = jnp.concatenate([side[tokens:] for side in sides], axis=1)
        blocks |= after({at: blocks[at] for at in row + column}, theirs)
        context_grad += sibling(theirs)

    own = lax.dynamic_index_in_dim(mine, o // cores, 0, keepdims=False)
    cotangents = {(0, 0): [own[i * tokens : (i + 1) * tokens] for i in range(cores)]}
    for at in across + row + column:
        cotangents[at] = [blocks[at][:, :width]]
        if cores > 1:
            cotangents[at].append(sibling(blocks[at][:, width:]))
    weight_grad = 0.0
    for group in ([(0, 0)], across, row + column):
        if group:
            left = jnp.concatenate([x for at in group for x in contexts[at]], axis=0)
            right = jnp.concatenate([x for at in group for x in cotangents[at]], axis=0)
            weight_grad += dot(left, right, 0)
    return (context_grad.astype(jnp.bfloat16), weight_grad * norm_scale)


def solution(mesh):
    in_specs = (P("outer", "node"), P("outer", "node"), P("node", "outer"))
    out_specs = (P("outer", "node"), P("node", "outer"))
    return jax.shard_map(body, mesh=mesh, in_specs=in_specs, out_specs=out_specs, check_vma=False)
```

time: 109 us -> 92.5 us (0.85)
  waiting for transfers between devices: 59.3 us -> 44.1 us
  starting transfers between devices: 23.9 us -> 17.1 us
  local copies, waits for them, and re-layouts: 11.3 us -> 16.3 us
  Pallas kernels: 0 us -> 1.14 us
    ppermute x14 -> x15, waiting for transfers between devices: 42.8 us -> 16 us  [shift(): lax.ppermute(array, 'outer', [(place(o, db, da, dc), o) for o in range(la...]
    ppermute x6 -> x4, waiting for transfers between devices: 16.5 us -> 28.1 us  [the longest x3 22.9 us: along_node(): lax.ppermute(array, 'node', [((i + d) % node, i) for i in range(node)])]
    ppermute x14 -> x15, starting transfers between devices: 15.5 us -> 10.6 us  [shift(): lax.ppermute(array, 'outer', [(place(o, db, da, dc), o) for o in range(la...]
    dynamic_update_slice x8 -> x4, local copies, waits for them, and re-layouts: 3.33 us -> 6.46 us  [stacked(): whole = lax.dynamic_update_index_in_dim(whole, block, (me + d) % node, 0)]
    ppermute x6 -> x4, starting transfers between devices: 8.39 us -> 6.49 us  [the longest x3 5.17 us: along_node(): lax.ppermute(array, 'node', [((i + d) % node, i) for i in range(node)])]
    squeeze x1, local copies, waits for them, and re-layouts: 0.31 us -> 1.83 us  [columns(): lax.dynamic_slice(grad, (first // held, 0, first % held), (1, tokens, wid...]
    unnamed x7, local copies, waits for them, and re-layouts: 3.66 us -> 2.24 us
    broadcast_in_dim x2 -> x1, local copies, waits for them, and re-layouts: 0.3 us -> 1.58 us  [stacked(): whole = jnp.zeros((node,) + blocks[0].shape, blocks[0].dtype)]
  transfers between devices with their start and end apart: 20 -> 19, of which waited for: 8 -> 11; matrix products, arithmetic and copies ran while one was open for 18% -> 29% of each run, Pallas kernels for 0% -> 1%
where the time goes in v3:
time: 92.5 us; the launch traced here: 91.9 us
  waiting for transfers between devices  44.1 us (48%)
  starting transfers between devices  17.1 us (18%)
  local copies, waits for them, and re-layouts  16.3 us (18%)
  matrix products  11.3 us (12%)
  Pallas kernels  1.14 us (1%)
  other arithmetic  1.06 us (1%)
  between operations  0.95 us (1%)
    ppermute x3, waiting for transfers between devices, along_node(): lax.ppermute(array, 'node', [((i + d) % node, i) for i in range(node)])  22.9 us
    ppermute x15, waiting for transfers between devices, shift(): lax.ppermute(array, 'outer', [(place(o, db, da, dc), o) for o in range(la...  16 us
    dot_general x11, matrix products, dot(): lax.dot_general(left, right, (((dim,), (dim,)), ((), ())), preferred_elem...  11.3 us
    ppermute x15, starting transfers between devices, shift(): lax.ppermute(array, 'outer', [(place(o, db, da, dc), o) for o in range(la...  10.6 us
    dynamic_update_slice x4, local copies, waits for them, and re-layouts, stacked(): whole = lax.dynamic_update_index_in_dim(whole, block, (me + d) % node, 0)  6.46 us
    ppermute x1, waiting for transfers between devices, body(): other = lax.ppermute(share, 'node', [(i ^ 1, i) for i in range(node)])  5.18 us
    ppermute x3, starting transfers between devices, along_node(): lax.ppermute(array, 'node', [((i + d) % node, i) for i in range(node)])  5.17 us
    unnamed x7, local copies, waits for them, and re-layouts  2.24 us
  transfers between devices with their start and end apart: 19, of which 11 were waited for; matrix products, arithmetic and copies ran while one was open for 29% of the time, Pallas kernels for 1%

profile of v3, /device:TPU:0, one launch (start us, length us, event | category | flops | bytes accessed | tf_op | source)
XLA Modules:
  0.0 91.9 jit_solution(4011459715079613488)
XLA Ops:
  0.6 3.1 %collective-permute-start = (bf16[256,1024]{1,0:T(8,128)(2,1)}, bf16[256,1024]{1,0:T(8,128)(2,1)}, u32[]{:S(2)}, u32[]{:S(2)}) collective-permute-start(bf16[256,1024]{1,0:T(8,128)(2,1)} %param.4), channel_id=1, source_target_pairs={{3,0},{0,1},{1,2},{2,3},{7,4},{4,5},{5,6},{6,7},{11,8},{8,9},{9,10... | collective-permute-start | bytes 1572872 | tf_op jit(solution)/shard_map/ppermute | solution.py:35
  3.7 2.1 %collective-permute-start.1 = (bf16[256,1024]{1,0:T(8,128)(2,1)}, bf16[256,1024]{1,0:T(8,128)(2,1)}, u32[]{:S(2)}, u32[]{:S(2)}) collective-permute-start(bf16[256,1024]{1,0:T(8,128)(2,1)} %param.4), channel_id=1, source_target_pairs={{1,0},{2,1},{3,2},{0,3},{5,4},{6,5},{7,6},{4,7},{9,8},{10,9},{11,1... | collective-permute-start | bytes 1572872 | tf_op jit(solution)/shard_map/ppermute | solution.py:35
  8.2 1.7 %collective-permute-start.3 = (bf16[1536,512]{1,0:T(8,128)(2,1)S(1)}, bf16[1536,512]{1,0:T(8,128)(2,1)S(1)}, u32[]{:S(2)}, u32[]{:S(2)}) collective-permute-start(bf16[1536,512]{1,0:T(8,128)(2,1)S(1)} %shard_map.50), channel_id=1, source_target_pairs={{8,0},{12,4},{0,8},{4,12},{24,16},{28,20},{16,24},{20,28},{9,1},{1... | collective-permute-start | bytes 4718600 | tf_op jit(solution)/shard_map/ppermute | solution.py:26
  9.9 1.5 %collective-permute-start.4 = (bf16[1536,512]{1,0:T(8,128)(2,1)S(1)}, bf16[1536,512]{1,0:T(8,128)(2,1)}, u32[]{:S(2)}, u32[]{:S(2)}) collective-permute-start(bf16[1536,512]{1,0:T(8,128)(2,1)S(1)} %shard_map.50), channel_id=1, source_target_pairs={{16,0},{20,4},{24,8},{28,12},{0,16},{4,20},{8,24},{12,28},{17,1},{... | collective-permute-start | bytes 4718600 | tf_op jit(solution)/shard_map/ppermute | solution.py:26
  11.4 1.6 %broadcast_in_dim.16 = bf16[4,256,1024]{2,1,0:T(8,128)(2,1)} broadcast(bf16[]{:T(256)} %constant.509.clone.1), dimensions={} | broadcast | bytes 2097154 | tf_op jit(solution)/shard_map/broadcast_in_dim | solution.py:57
  13.8 5.0 %collective-permute-done = bf16[256,1024]{1,0:T(8,128)(2,1)} collective-permute-done((bf16[256,1024]{1,0:T(8,128)(2,1)}, bf16[256,1024]{1,0:T(8,128)(2,1)}, u32[]{:S(2)}, u32[]{:S(2)}) %collective-permute-start) | collective-permute-done | bytes 524320 | tf_op jit(solution)/shard_map/ppermute | solution.py:35
  18.9 1.9 %bitcast_dynamic-update-slice_fusion.2 = bf16[4,256,1024]{2,1,0:T(8,128)(2,1)} fusion(bf16[4,256,1024]{2,1,0:T(8,128)(2,1)} %bitcast_dynamic-update-slice_fusion.3, s32[]{:T(128)S(6)} %select_n.468, bf16[256,1024]{1,0:T(8,128)(2,1)} %collective-permute-done), kind=kLoop, calls=%fused_computation.76 | loop fusion | bytes 1048580 | tf_op jit(solution)/shard_map/jit(dynamic_update_index_in_dim)/dynamic_update_slice | solution.py:59
  20.8 8.1 %collective-permute-done.1 = bf16[256,1024]{1,0:T(8,128)(2,1)} collective-permute-done((bf16[256,1024]{1,0:T(8,128)(2,1)}, bf16[256,1024]{1,0:T(8,128)(2,1)}, u32[]{:S(2)}, u32[]{:S(2)}) %collective-permute-start.1) | collective-permute-done | bytes 524320 | tf_op jit(solution)/shard_map/ppermute | solution.py:35
  28.9 1.9 %bitcast_dynamic-update-slice_fusion.1 = bf16[4,256,1024]{2,1,0:T(8,128)(2,1)} fusion(bf16[4,256,1024]{2,1,0:T(8,128)(2,1)} %bitcast_dynamic-update-slice_fusion.2, s32[]{:T(128)S(6)} %select_n.470, bf16[256,1024]{1,0:T(8,128)(2,1)} %collective-permute-done.1), kind=kLoop, calls=%fused_computation.75 | loop fusion | bytes 1048580 | tf_op jit(solution)/shard_map/jit(dynamic_update_index_in_dim)/dynamic_update_slice | solution.py:59
  30.7 9.8 %collective-permute-done.2 = bf16[256,1024]{1,0:T(8,128)(2,1)} collective-permute-done((bf16[256,1024]{1,0:T(8,128)(2,1)}, bf16[256,1024]{1,0:T(8,128)(2,1)}, u32[]{:S(2)}, u32[]{:S(2)}) %collective-permute-start.2) | collective-permute-done | bytes 524320 | tf_op jit(solution)/shard_map/ppermute | solution.py:35
  40.5 1.9 %bitcast_dynamic-update-slice_fusion = bf16[4,256,1024]{2,1,0:T(8,128)(2,1)} fusion(bf16[4,256,1024]{2,1,0:T(8,128)(2,1)} %bitcast_dynamic-update-slice_fusion.1, s32[]{:T(128)S(6)} %select_n.472, bf16[256,1024]{1,0:T(8,128)(2,1)} %collective-permute-done.2), kind=kLoop, calls=%fused_computation.74 | loop fusion | bytes 1048580 | tf_op jit(solution)/shard_map/jit(dynamic_update_index_in_dim)/dynamic_update_slice | solution.py:59
  42.4 1.8 %dynamic-slice_bitcast_fusion.3 = (bf16[256,512]{1,0:T(8,128)(2,1)S(1)}, bf16[256,512]{1,0:T(8,128)(2,1)S(1)}, bf16[256,512]{1,0:T(8,128)(2,1)S(1)}, bf16[256,51...) fusion(bf16[4,256,1024]{2,1,0:T(8,128)(2,1)} %bitcast_dynamic-u, ...), kind=kLoop, calls=%fused_computation.94 | loop fusion | bytes 4718664 | tf_op jit(solution)/shard_map/squeeze | solution.py:118
  44.4 1.4 %constant_dynamic-slice_fusion.7 = (bf16[1,256,512]{2,1,0:T(8,128)(2,1)S(1)}, bf16[1,256,512]{2,1,0:T(8,128)(2,1)S(1)}, bf16[1,256,512]{2,1,0:T(8,128)(2,1)S(1)}...) fusion(bf16[4,256,1024]{2,1,0:T(8,128)(2,1)} %bitcast_dynamic-update-slice_fusion, s32[]{:T(128)S(6)} %select_n.475, ...), kind=kLoop, calls=%fused_computation.114 | loop fusion | bytes 2621480 | tf_op jit(solution)/shard_map/dynamic_slice | solution.py:118
  45.9 2.5 %collective-permute-start.11 = (bf16[128,1024]{1,0:T(8,128)(2,1)S(1)}, bf16[128,1024]{1,0:T(8,128)(2,1)S(1)}, u32[]{:S(2)}, u32[]{:S(2)}) collective-permute-start(bf16[128,1024]{1,0:T(8,128)(2,1)S(1)} %fusion.70), channel_id=1, source_target_pairs={{24,0},{28,4},{16,8},{20,12},{8,16},{12,20},{0,24},{4,28},{25,1},{... | collective-permute-start | bytes 786440 | tf_op jit(solution)/shard_map/ppermute | solution.py:26
  51.9 1.5 %collective-permute-done.11 = bf16[128,1024]{1,0:T(8,128)(2,1)S(1)} collective-permute-done((bf16[128,1024]{1,0:T(8,128)(2,1)S(1)}, bf16[128,1024]{1,0:T(8,128)(2,1)S(1)}, u32[]{:S(2)}, u32[]{:S(2)}) %collective-permute-start.11) | collective-permute-done | bytes 262176 | tf_op jit(solution)/shard_map/ppermute | solution.py:26
  53.4 1.3 %collective-permute-start.12 = (bf16[128,1024]{1,0:T(8,128)(2,1)S(1)}, bf16[128,1024]{1,0:T(8,128)(2,1)S(1)}, u32[]{:S(2)}, u32[]{:S(2)}) collective-permute-start(bf16[128,1024]{1,0:T(8,128)(2,1)S(1)} %collective-permute-done.11), channel_id=1, source_target_pairs={{1,0},{0,1},{3,2},{2,3},{5,4},{4,5},{7,6},{6,7},{9,8},{8,9},{11,10... | collective-permute-start | bytes 786440 | tf_op jit(solution)/shard_map/ppermute | solution.py:143
  55.0 5.2 %collective-permute-done.12 = bf16[128,1024]{1,0:T(8,128)(2,1)S(1)} collective-permute-done((bf16[128,1024]{1,0:T(8,128)(2,1)S(1)}, bf16[128,1024]{1,0:T(8,128)(2,1)S(1)}, u32[]{:S(2)}, u32[]{:S(2)}) %collective-permute-start.12) | collective-permute-done | bytes 262176 | tf_op jit(solution)/shard_map/ppermute | solution.py:143
  60.5 9.6 %collective-permute-done.6 = bf16[768,512]{1,0:T(8,128)(2,1)S(1)} collective-permute-done((bf16[768,512]{1,0:T(8,128)(2,1)S(1)}, bf16[768,512]{1,0:T(8,128)(2,1)S(1)}, u32[]{:S(2)}, u32[]{:S(2)}) %collective-permute-start.6) | collective-permute-done | bytes 786464 | tf_op jit(solution)/shard_map/ppermute | solution.py:26
  70.5 1.6 %collective-permute-start.15 = (bf16[256,1024]{1,0:T(8,128)(2,1)S(1)}, bf16[256,1024]{1,0:T(8,128)(2,1)S(1)}, u32[]{:S(2)}, u32[]{:S(2)}) collective-permute-start(bf16[256,1024]{1,0:T(8,128)(2,1)S(1)} %get-tuple-element.12), channel_id=1, source_target_pairs={{8,0},{12,4},{0,8},{4,12},{24,16},{28,20},{16,24},{20,28},{9,1},{1... | collective-permute-start | bytes 1572872 | tf_op jit(solution)/shard_map/ppermute | solution.py:26
  73.3 1.6 %fusion.42 = f32[512,512]{0,1:T(8,128)S(1)} fusion(bf16[1536,512]{1,0:T(8,128)(2,1)} %collective-permute-done.4, bf16[4,512,512]{2,1,0:T(8,128)(2,1)S(1)} %pad_maximum_fusion, s32[]{:T(128)S(6)} %select_n.520), kind=kOutput, calls=%fused_computation.48 | convolution fusion | flops 268435456 | bytes 2097156 | tf_op jit(solution)/shard_map/dot_general | solution.py:101
  76.4 1.5 %fusion.36 = f32[512,512]{0,1:T(8,128)S(1)} fusion(bf16[1536,512]{1,0:T(8,128)(2,1)} %collective-permute-done.4, bf16[4,512,512]{2,1,0:T(8,128)(2,1)S(1)} %pad_maximum_fusion, s32[]{:T(128)S(6)} %select_n.520), kind=kOutput, calls=%fused_computation.42 | convolution fusion | flops 268435456 | bytes 2097156 | tf_op jit(solution)/shard_map/dot_general | solution.py:101
  79.2 2.0 %fusion.13 = f32[1024,512]{1,0:T(8,128)S(1)} fusion(bf16[256,1024]{1,0:T(8,128)(2,1)} %collective-permute-done.9, bf16[256,1024]{1,0:T(8,128)(2,1)} %context.1, bf16[256,512]{1,0:T(8,128)(2,1)S(1)} %get-tuple-element.28, bf16[256,512]{1,0:T(8,128)(2,1)S(1)} %get-tuple-element.27), kind=kOutput, calls=%fused_computation.20 | convolution fusion | flops 540016640 | bytes 3670016 | tf_op jit(solution)/shard_map/dot_general | solution.py:101
  82.5 2.4 %collective-permute-done.15 = bf16[256,1024]{1,0:T(8,128)(2,1)S(1)} collective-permute-done((bf16[256,1024]{1,0:T(8,128)(2,1)S(1)}, bf16[256,1024]{1,0:T(8,128)(2,1)S(1)}, u32[]{:S(2)}, u32[]{:S(2)}) %collective-permute-start.15) | collective-permute-done | bytes 524320 | tf_op jit(solution)/shard_map/ppermute | solution.py:26
  88.1 2.6 %add_multiply_fusion = f32[1024,512]{1,0:T(8,128)} fusion(f32[1024,512]{1,0:T(8,128)S(1)} %fusion.13, f32[1024,512]{1,0:T(8,128)S(1)} %fusion.17, bf16[256,1024]{1,0:T(8,128)(2,1)S(1)} %get-tuple-element.41, bf16[256,1024]{1,0:T(8,128)(2,1)S(1)} %get-tuple-element.39, bf16[256,1024]{1,0:T(8,128)(2,1)S(1)} %get-tuple-element.40, ...), kind=kOutput, calls=%fused_computation.9 | convolution fusion | flops 1087897600 | bytes 9437184 | tf_op jit(solution)/shard_map/dot_general | solution.py:101
  (64 shorter events, 17.5 us)
Async XLA Ops:
  0.6 18.2 %collective-permute-start = (bf16[256,1024]{1,0:T(8,128)(2,1)}, bf16[256,1024]{1,0:T(8,128)(2,1)}, u32[]{:S(2)}, u32[]{:S(2)}) collective-permute-start(bf16[256,1024]{1,0:T(8,128)(2,1)} %param.4), channel_id=1, source_target_pairs={{3,0},{0,1},{1,2},{2,3},{7,4},{4,5},{5,6},{6,7},{11,8},{8,9},{9,10... | collective-permute-start | bytes 1572872 | tf_op jit(solution)/shard_map/ppermute | solution.py:35
  3.7 25.1 %collective-permute-start.1 = (bf16[256,1024]{1,0:T(8,128)(2,1)}, bf16[256,1024]{1,0:T(8,128)(2,1)}, u32[]{:S(2)}, u32[]{:S(2)}) collective-permute-start(bf16[256,1024]{1,0:T(8,128)(2,1)} %param.4), channel_id=1, source_target_pairs={{1,0},{2,1},{3,2},{0,3},{5,4},{6,5},{7,6},{4,7},{9,8},{10,9},{11,1... | collective-permute-start | bytes 1572872 | tf_op jit(solution)/shard_map/ppermute | solution.py:35
  5.8 1.2 %copy-start = (bf16[1024,512]{1,0:T(8,128)(2,1)S(1)}, bf16[1024,512]{1,0:T(8,128)(2,1)}, u32[]{:S(2)}) copy-start(bf16[1024,512]{1,0:T(8,128)(2,1)} %weight.1) | copy-start | bytes 3145732
  8.2 37.7 %collective-permute-start.3 = (bf16[1536,512]{1,0:T(8,128)(2,1)S(1)}, bf16[1536,512]{1,0:T(8,128)(2,1)S(1)}, u32[]{:S(2)}, u32[]{:S(2)}) collective-permute-start(bf16[1536,512]{1,0:T(8,128)(2,1)S(1)} %shard_map.50), channel_id=1, source_target_pairs={{8,0},{12,4},{0,8},{4,12},{24,16},{28,20},{16,24},{20,28},{9,1},{1... | collective-permute-start | bytes 4718600 | tf_op jit(solution)/shard_map/ppermute | solution.py:26
  9.9 36.0 %collective-permute-start.4 = (bf16[1536,512]{1,0:T(8,128)(2,1)S(1)}, bf16[1536,512]{1,0:T(8,128)(2,1)}, u32[]{:S(2)}, u32[]{:S(2)}) collective-permute-start(bf16[1536,512]{1,0:T(8,128)(2,1)S(1)} %shard_map.50), channel_id=1, source_target_pairs={{16,0},{20,4},{24,8},{28,12},{0,16},{4,20},{8,24},{12,28},{17,1},{... | collective-permute-start | bytes 4718600 | tf_op jit(solution)/shard_map/ppermute | solution.py:26
  11.4 67.7 %collective-permute-start.9 = (bf16[256,1024]{1,0:T(8,128)(2,1)}, bf16[256,1024]{1,0:T(8,128)(2,1)}, u32[]{:S(2)}, u32[]{:S(2)}) collective-permute-start(bf16[256,1024]{1,0:T(8,128)(2,1)} %context.1), channel_id=1, source_target_pairs={{4,0},{0,4},{12,8},{8,12},{20,16},{16,20},{28,24},{24,28},{5,1},{1... | collective-permute-start | bytes 1572872 | tf_op jit(solution)/shard_map/ppermute | solution.py:26
  11.4 1.6 %copy-start.2 = (bf16[256,1024]{1,0:T(8,128)(2,1)S(1)}, bf16[256,1024]{1,0:T(8,128)(2,1)}, u32[]{:S(2)}) copy-start(bf16[256,1024]{1,0:T(8,128)(2,1)} %param.4) | copy-start | bytes 1572868
  18.8 21.6 %collective-permute-start.2 = (bf16[256,1024]{1,0:T(8,128)(2,1)}, bf16[256,1024]{1,0:T(8,128)(2,1)}, u32[]{:S(2)}, u32[]{:S(2)}) collective-permute-start(bf16[256,1024]{1,0:T(8,128)(2,1)} %collective-permute-done), channel_id=1, source_target_pairs={{3,0},{0,1},{1,2},{2,3},{7,4},{4,5},{5,6},{6,7},{11,8},{8,9},{9,10... | collective-permute-start | bytes 1572872 | tf_op jit(solution)/shard_map/ppermute | solution.py:35
  45.9 7.5 %collective-permute-start.11 = (bf16[128,1024]{1,0:T(8,128)(2,1)S(1)}, bf16[128,1024]{1,0:T(8,128)(2,1)S(1)}, u32[]{:S(2)}, u32[]{:S(2)}) collective-permute-start(bf16[128,1024]{1,0:T(8,128)(2,1)S(1)} %fusion.70), channel_id=1, source_target_pairs={{24,0},{28,4},{16,8},{20,12},{8,16},{12,20},{0,24},{4,28},{25,1},{... | collective-permute-start | bytes 786440 | tf_op jit(solution)/shard_map/ppermute | solution.py:26
  48.4 22.0 %collective-permute-start.5 = (bf16[4,256,512]{2,1,0:T(8,128)(2,1)S(1)}, bf16[4,256,512]{2,1,0:T(8,128)(2,1)S(1)}, u32[]{:S(2)}, u32[]{:S(2)}) collective-permute-start(bf16[4,256,512]{2,1,0:T(8,128)(2,1)S(1)} %pad_maximum_fusion.1), channel_id=1, source_target_pairs={{4,0},{0,4},{12,8},{8,12},{20,16},{16,20},{28,24},{24,28},{5,1},{1... | collective-permute-start | bytes 3145736 | tf_op jit(solution)/shard_map/ppermute | solution.py:26
  48.5 21.6 %collective-permute-start.6 = (bf16[768,512]{1,0:T(8,128)(2,1)S(1)}, bf16[768,512]{1,0:T(8,128)(2,1)S(1)}, u32[]{:S(2)}, u32[]{:S(2)}) collective-permute-start(bf16[768,512]{1,0:T(8,128)(2,1)S(1)} %slice.128), channel_id=1, source_target_pairs={{16,0},{20,4},{24,8},{28,12},{0,16},{4,20},{8,24},{12,28},{17,1},{... | collective-permute-start | bytes 2359304 | tf_op jit(solution)/shard_map/ppermute | solution.py:26
  50.2 20.0 %collective-permute-start.7 = (bf16[768,512]{1,0:T(8,128)(2,1)S(1)}, bf16[768,512]{1,0:T(8,128)(2,1)S(1)}, u32[]{:S(2)}, u32[]{:S(2)}) collective-permute-start(bf16[768,512]{1,0:T(8,128)(2,1)S(1)} %slice.133), channel_id=1, source_target_pairs={{8,0},{12,4},{0,8},{4,12},{24,16},{28,20},{16,24},{20,28},{9,1},{1... | collective-permute-start | bytes 2359304 | tf_op jit(solution)/shard_map/ppermute | solution.py:26
  53.4 6.7 %collective-permute-start.12 = (bf16[128,1024]{1,0:T(8,128)(2,1)S(1)}, bf16[128,1024]{1,0:T(8,128)(2,1)S(1)}, u32[]{:S(2)}, u32[]{:S(2)}) collective-permute-start(bf16[128,1024]{1,0:T(8,128)(2,1)S(1)} %collective-permute-done.11), channel_id=1, source_target_pairs={{1,0},{0,1},{3,2},{2,3},{5,4},{4,5},{7,6},{6,7},{9,8},{8,9},{11,10... | collective-permute-start | bytes 786440 | tf_op jit(solution)/shard_map/ppermute | solution.py:143
  60.3 26.5 %collective-permute-start.14 = (bf16[2,256,1024]{2,1,0:T(8,128)(2,1)S(1)}, bf16[2,256,1024]{2,1,0:T(8,128)(2,1)S(1)}, u32[]{:S(2)}, u32[]{:S(2)}) collective-permute-start(bf16[2,256,1024]{2,1,0:T(8,128)(2,1)S(1)} %pad_maximum_fusion.3), channel_id=1, source_target_pairs={{4,0},{0,4},{12,8},{8,12},{20,16},{16,20},{28,24},{24,28},{5,1},{1... | collective-permute-start | bytes 3145736 | tf_op jit(solution)/shard_map/ppermute | solution.py:26
  70.3 11.5 %collective-permute-start.10 = (bf16[256,1024]{1,0:T(8,128)(2,1)S(1)}, bf16[256,1024]{1,0:T(8,128)(2,1)S(1)}, u32[]{:S(2)}, u32[]{:S(2)}) collective-permute-start(bf16[256,1024]{1,0:T(8,128)(2,1)S(1)} %pad_maximum_fusion.4), channel_id=1, source_target_pairs={{4,0},{0,4},{12,8},{8,12},{20,16},{16,20},{28,24},{24,28},{5,1},{1... | collective-permute-start | bytes 1572872 | tf_op jit(solution)/shard_map/ppermute | solution.py:26
  70.5 14.4 %collective-permute-start.15 = (bf16[256,1024]{1,0:T(8,128)(2,1)S(1)}, bf16[256,1024]{1,0:T(8,128)(2,1)S(1)}, u32[]{:S(2)}, u32[]{:S(2)}) collective-permute-start(bf16[256,1024]{1,0:T(8,128)(2,1)S(1)} %get-tuple-element.12), channel_id=1, source_target_pairs={{8,0},{12,4},{0,8},{4,12},{24,16},{28,20},{16,24},{20,28},{9,1},{1... | collective-permute-start | bytes 1572872 | tf_op jit(solution)/shard_map/ppermute | solution.py:26
  72.1 14.0 %collective-permute-start.16 = (bf16[256,1024]{1,0:T(8,128)(2,1)S(1)}, bf16[256,1024]{1,0:T(8,128)(2,1)S(1)}, u32[]{:S(2)}, u32[]{:S(2)}) collective-permute-start(bf16[256,1024]{1,0:T(8,128)(2,1)S(1)} %get-tuple-element.13), channel_id=1, source_target_pairs={{16,0},{20,4},{24,8},{28,12},{0,16},{4,20},{8,24},{12,28},{17,1},{... | collective-permute-start | bytes 1572872 | tf_op jit(solution)/shard_map/ppermute | solution.py:26
  73.3 2.1 %copy-start.1 = (bf16[1024,512]{1,0:T(8,128)(2,1)S(1)}, bf16[1024,512]{1,0:T(8,128)(2,1)}, u32[]{:S(2)}) copy-start(bf16[1024,512]{1,0:T(8,128)(2,1)} %weight.1) | copy-start | bytes 3145732
  79.1 2.1 %collective-permute-start.13 = (bf16[256,512]{1,0:T(8,128)(2,1)S(1)}, bf16[256,512]{1,0:T(8,128)(2,1)S(1)}, u32[]{:S(2)}, u32[]{:S(2)}) collective-permute-start(bf16[256,512]{1,0:T(8,128)(2,1)S(1)} %get-tuple-element.51), channel_id=1, source_target_pairs={{4,0},{0,4},{12,8},{8,12},{20,16},{16,20},{28,24},{24,28},{5,1},{1... | collective-permute-start | bytes 786440 | tf_op jit(solution)/shard_map/ppermute | solution.py:26
  81.2 9.5 %collective-permute-start.8 = (f32[256,1024]{0,1:T(8,128)S(1)}, f32[256,1024]{0,1:T(8,128)S(1)}, u32[]{:S(2)}, u32[]{:S(2)}) collective-permute-start(f32[256,1024]{0,1:T(8,128)S(1)} %pad_maximum_fusion.2), channel_id=1, source_target_pairs={{4,0},{0,4},{12,8},{8,12},{20,16},{16,20},{28,24},{24,28},{5,1},{1... | collective-permute-start | bytes 3145736 | tf_op jit(solution)/shard_map/ppermute | solution.py:26
  86.1 1.6 %collective-permute-start.17 = (bf16[256,512]{1,0:T(8,128)(2,1)S(1)}, bf16[256,512]{1,0:T(8,128)(2,1)S(1)}, u32[]{:S(2)}, u32[]{:S(2)}) collective-permute-start(bf16[256,512]{1,0:T(8,128)(2,1)S(1)} %get-tuple-element.47), channel_id=1, source_target_pairs={{4,0},{0,4},{12,8},{8,12},{20,16},{16,20},{28,24},{24,28},{5,1},{1... | collective-permute-start | bytes 786440 | tf_op jit(solution)/shard_map/ppermute | solution.py:26
  86.3 1.9 %collective-permute-start.18 = (bf16[256,512]{1,0:T(8,128)(2,1)S(1)}, bf16[256,512]{1,0:T(8,128)(2,1)S(1)}, u32[]{:S(2)}, u32[]{:S(2)}) collective-permute-start(bf16[256,512]{1,0:T(8,128)(2,1)S(1)} %get-tuple-element.49), channel_id=1, source_target_pairs={{4,0},{0,4},{12,8},{8,12},{20,16},{16,20},{28,24},{24,28},{5,1},{1... | collective-permute-start | bytes 786440 | tf_op jit(solution)/shard_map/ppermute | solution.py:26

commit v4 on v0

v4 whole, which is shorter than its diff:
```python
import functools
import math

import jax
import jax.numpy as jnp
from jax import lax
from jax.experimental import pallas as pl
from jax.experimental.pallas import tpu as pltpu
from jax.sharding import PartitionSpec as P

F32, BF16 = jnp.float32, jnp.bfloat16
VMEM = pl.BlockSpec(memory_space=pltpu.VMEM)


def plane_of(outer):
    cores = 2 if outer % 2 == 0 else 1
    chips = outer // cores
    cols = max(d for d in range(1, math.isqrt(chips) + 1) if chips % d == 0)
    return chips // cols, cols, cores


def place(o, db, da, dc):
    rows, cols, cores = plane_of(lax.axis_size("outer"))
    b, a, c = o // (cols * cores), o // cores % cols, o % cores
    return ((b + db) % rows * cols + (a + da) % cols) * cores + (c + dc) % cores


def chip_at(db, da):
    rows, cols, cores = plane_of(lax.axis_size("outer"))
    chip = lax.div(lax.axis_index("outer"), jnp.int32(cores))
    b, a = lax.div(chip, jnp.int32(cols)), lax.rem(chip, jnp.int32(cols))
    return lax.rem(b + db % rows, jnp.int32(rows)) * cols + lax.rem(a + da % cols, jnp.int32(cols))


def kind_at(dc):
    cores = plane_of(lax.axis_size("outer"))[2]
    return lax.rem(lax.axis_index("outer") + dc, jnp.int32(cores))


def shift(array, db, da, dc=0):
    return lax.ppermute(array, "outer", [(place(o, db, da, dc), o) for o in range(lax.axis_size("outer"))])


def sibling(array):
    return shift(array, 0, 0, 1)


def along_node(array, d):
    node = lax.axis_size("node")
    return lax.ppermute(array, "node", [((i + d) % node, i) for i in range(node)])


def after(arrays, done):
    return lax.optimization_barrier((arrays, done))[0]


def ring(array):
    node = lax.axis_size("node")
    blocks = {0: array}
    up, down = array, array
    for step in range(1, node // 2 + 1):
        up = along_node(up, -1)
        blocks[node - step] = up
        if 2 * step < node:
            down = along_node(down, 1)
            blocks[step] = down
    return [blocks[d] for d in range(node)]


def call(kernel, out, *args, scratch=(), grid=None, in_specs=None, out_specs=None, vmem=40):
    return pl.pallas_call(
        kernel,
        out_shape=out,
        in_specs=in_specs or [VMEM] * len(args),
        out_specs=out_specs or jax.tree.map(lambda _: VMEM, out),
        scratch_shapes=scratch,
        compiler_params=pltpu.CompilerParams(vmem_limit_bytes=vmem * 2**20),
        cost_estimate=pl.CostEstimate(flops=0, bytes_accessed=0, transcendentals=0),
        **({"grid": grid} if grid else {}),
    )(*args)


class Sizes:
    def __init__(self, context, grad_out, out_weight):
        self.outer, self.node = lax.axis_size("outer"), lax.axis_size("node")
        self.rows, self.cols, self.cores = plane_of(self.outer)
        self.chips = self.rows * self.cols
        self.tokens, self.held = grad_out.shape
        self.taken, self.width = out_weight.shape
        self.row = [(0, da) for da in range(1, self.cols)]
        self.column = [(db, 0) for db in range(1, self.rows)]
        self.across = [(db, da) for db in range(1, self.rows) for da in range(1, self.cols)]
        self.half, self.slabs = self.taken // 2, self.taken // self.width
        self.high = self.taken + self.slabs * self.tokens
        self.fits = self.width % 128 == 0 and self.held % (self.width * self.cores) == 0 and self.node % 2 == 0


def pack_kernel(s, weight, context, out, sems):
    moves = [(weight, 0, 0, s.half, 0)]
    moves += [(context, 0, i * s.width, s.tokens, s.half + i * s.tokens) for i in range(s.slabs)]
    moves += [(weight, s.half, 0, s.half, s.high - s.half)]
    copies = []
    for i, (source, row, column, height, to) in enumerate(moves):
        rows = source.at[pl.ds(row, height), pl.ds(column, s.width)]
        copies.append(pltpu.make_async_copy(rows, out.at[pl.ds(to, height)], sems.at[i]))
        copies[-1].start()
    for copy in copies:
        copy.wait()


def route_kernel(s, *refs):
    blocks, (mine, other, whole) = refs[: s.node], refs[s.node :]
    for d, block in enumerate(blocks):
        whole[lax.rem(lax.axis_index("node") + d, jnp.int32(s.node))] = block[...]
    for out, kind in ((mine, kind_at(0)), (other, kind_at(1))):
        for chip in range(s.chips):
            first = chip * s.cores * s.width
            at = pl.multiple_of(first % s.held + kind * s.width, 128)
            out[chip] = whole[first // s.held, :, pl.ds(at, s.width)]


def pick_kernel(s, mine, theirs, *sent):
    odd = lax.rem(lax.axis_index("node"), jnp.int32(2))
    for source, here in ((mine, odd == 0), (theirs, odd == 1)):

        @pl.when(here)
        def _(source=source):
            for (db, da), out in zip(s.across + s.row + s.column, sent):
                out[...] = source[chip_at(-db, -da)]


def put(s, packed, slot, n, share, second):
    odd = lax.rem(lax.axis_index("node"), jnp.int32(2))
    for block, half in ((share, odd), (second, 1 - odd)):
        at = pl.multiple_of((half * n + slot) * s.tokens, 128)
        packed[pl.ds(at, s.tokens)] = block[...]


def turn_kernel(s, context, *refs):
    *refs, out = refs
    n = len(s.row + s.column)
    slabs = [[pack[s.half + i * s.tokens : s.half + (i + 1) * s.tokens] for i in range(s.slabs)] for pack in refs[:n]]
    for upper, lower in zip(refs[n::2], refs[n + 1 :: 2]):
        slab = jnp.concatenate([upper[...], lower[...]], axis=0)
        slabs.append([slab[i * s.tokens : (i + 1) * s.tokens] for i in range(s.slabs)])
    out[:, : s.tokens] = context[...].T
    for k, parts in enumerate(slabs):
        to = slice((1 + k) * s.tokens, (2 + k) * s.tokens)
        for i, part in enumerate(parts):
            out[i * s.width : (i + 1) * s.width, to] = part.T


def over_chips(s, mine, theirs, pieces):
    total = 0.0
    for at, piece in pieces:
        chip = chip_at(*at)
        left = jnp.concatenate([mine[chip], theirs[chip]], axis=0)
        total += lax.dot_general(left, piece, (((1,), (1,)), ((), ())), preferred_element_type=F32)
    return total


def context_kernel(s, mine, theirs, weight, *refs):
    *packs, own, others = refs
    for h in range(2):
        side = slice(h * s.half, (h + 1) * s.half)
        pieces = [((0, 0), weight[side])]
        pieces += [(at, pack[: s.half] if h == 0 else pack[-s.half :]) for at, pack in zip(s.row + s.column, packs)]
        total = over_chips(s, mine, theirs, pieces)
        own[:, side] = total[: s.tokens]
        others[:, side] = total[s.tokens :]


def context_far_kernel(s, mine, other, near, near_theirs, *refs):
    *halves, out = refs
    quarter = len(halves) // 2
    for h in range(2):
        side = slice(h * s.half, (h + 1) * s.half)
        total = near[:, side] + near_theirs[:, side]
        for k, at in enumerate(s.across):
            for left, pairs in ((mine, halves[:quarter]), (other, halves[quarter:])):
                piece = pairs[2 * k + h][...]
                total += lax.dot_general(
                    left[chip_at(*at)], piece, (((1,), (1,)), ((), ())), preferred_element_type=F32
                )
        out[:, side] = total.astype(BF16)


def near_kernel(s, turned, theirs, mine, other, *refs):
    *blocks, out, packed = refs
    n = 1 + len(blocks) // 2
    packed[: s.tokens] = mine[chip_at(0, 0)]
    packed[n * s.tokens : (n + 1) * s.tokens] = other[chip_at(0, 0)]
    for k in range(1, n):
        put(s, packed, k, n, *blocks[2 * k - 2 : 2 * k])
    left = jnp.concatenate([turned[:, : n * s.tokens], theirs[:, : n * s.tokens]], axis=1)
    out[...] = jnp.dot(left, packed[...], preferred_element_type=F32)


def far_kernel(s, scale, near, turned, theirs, *refs):
    *blocks, out, packed = refs
    n = len(blocks) // 2
    for k in range(n):
        put(s, packed, k, n, *blocks[2 * k : 2 * k + 2])
    at = (1 + len(s.row + s.column)) * s.tokens
    left = jnp.concatenate([turned[:, at:], theirs[:, at:]], axis=1)
    out[...] = (near[...] + jnp.dot(left, packed[...], preferred_element_type=F32)) * scale


def body(context, grad_out, out_weight):
    s = Sizes(context, grad_out, out_weight)
    if not s.fits or s.cores == 1:
        return plain(context, grad_out, out_weight)
    shape = lambda *dims, dtype=BF16: jax.ShapeDtypeStruct(dims, dtype)
    scale = 1.0 / math.sqrt(s.tokens * s.outer)
    near = s.row + s.column

    around = ring(grad_out)
    pack = call(
        functools.partial(pack_kernel, s), shape(s.high, s.width), out_weight, context,
        in_specs=[pl.BlockSpec(memory_space=pl.ANY)] * 2, scratch=[pltpu.SemaphoreType.DMA((s.slabs + 2,))], vmem=60,
    )
    packs = {at: shift(pack, *at) for at in near}

    def forward(packs, first, count):
        pairs = []
        for db, da in s.across:
            pairs.append(shift(packs[0, da][first : first + count], db, 0))
            pairs.append(shift(packs[db, 0][s.high - first - count : s.high - first], 0, da))
        return pairs

    packs = after(packs, around)
    slabs = forward(packs, s.half, s.high // 2 - s.half)

    columns = shape(s.chips, s.tokens, s.width)
    mine, other = call(
        functools.partial(route_kernel, s), [columns] * 2, *around,
        scratch=[pltpu.VMEM((s.node, s.tokens, s.held), BF16)],
    )
    theirs = after(sibling(other), packs)

    chips = s.across + near
    sent = call(functools.partial(pick_kernel, s), [shape(s.tokens, s.width)] * len(chips), mine, theirs)
    shares = [shift(x, *at) for x, at in zip(sent, chips)]
    seconds = [lax.ppermute(x, "node", [(i ^ 1, i) for i in range(s.node)]) for x in shares]
    blocks = {at: two for at, two in zip(chips, zip(shares, seconds))}
    turned = call(
        functools.partial(turn_kernel, s), shape(s.taken, s.chips * s.tokens),
        *after([context, *[packs[at] for at in near], *slabs], shares),
    )
    turned_other = sibling(turned)

    packs = after(packs, shares)
    pairs = forward(packs, 0, s.half)
    packs = [packs[at] for at in near]

    def by_rows(x):
        return pl.BlockSpec((s.taken // 4, x.shape[1]), lambda i: (i, 0))

    result = shape(s.taken, s.width, dtype=F32)
    lefts = [turned, turned_other]
    rights = [mine, theirs, *[x for at in near for x in blocks[at]]]
    sums = call(
        functools.partial(near_kernel, s), result, *lefts, *rights,
        grid=(4,), in_specs=[by_rows(x) for x in lefts] + [VMEM] * len(rights), out_specs=by_rows(result),
        scratch=[pltpu.VMEM((2 * (1 + len(near)) * s.tokens, s.width), BF16)],
    )
    lefts = [sums, turned, turned_other]
    rights = [x for at in s.across for x in blocks[at]]
    weight_grad = call(
        functools.partial(far_kernel, s, scale), result, *lefts, *rights,
        grid=(4,), in_specs=[by_rows(x) for x in lefts] + [VMEM] * len(rights), out_specs=by_rows(result),
        scratch=[pltpu.VMEM((len(rights) * s.tokens, s.width), BF16)],
    )

    half_sums = shape(s.tokens, s.taken, dtype=F32)
    own, others = call(functools.partial(context_kernel, s), [half_sums] * 2, mine, theirs, out_weight, *after(packs, turned_other))
    pairs_other = [sibling(x) for x in after(pairs, (sums, seconds))]
    context_grad = call(
        functools.partial(context_far_kernel, s), shape(s.tokens, s.taken),
        mine, other, own, sibling(others), *pairs, *pairs_other,
    )
    return (context_grad, weight_grad)


def plain(context, grad_out, out_weight):
    grad_full = lax.all_gather(grad_out, "node", axis=1, tiled=True)
    weight = lax.all_gather(out_weight, "outer", axis=1, tiled=True)
    context_grad = lax.dot_general(grad_full, weight, (((1,), (1,)), ((), ())), preferred_element_type=F32)
    scale = 1.0 / math.sqrt(grad_full.shape[0] * lax.axis_size("outer"))
    owner_cols = lax.all_to_all(grad_full, "outer", split_axis=1, concat_axis=0, tiled=True)
    context = lax.all_gather(context, "outer", axis=0, tiled=True)
    weight_grad = lax.dot_general(context, owner_cols, (((0,), (0,)), ((), ())), preferred_element_type=F32)
    return (context_grad.astype(BF16), weight_grad * scale)


def solution(mesh):
    in_specs = (P("outer", "node"), P("outer", "node"), P("node", "outer"))
    out_specs = (P("outer", "node"), P("node", "outer"))
    return jax.shard_map(body, mesh=mesh, in_specs=in_specs, out_specs=out_specs, check_vma=False)
```

time: 179 us -> 88.8 us (0.50)
  waiting for transfers between devices: 112 us -> 54.8 us
  blocking collectives: 35.8 us -> 0 us
  starting transfers between devices: 0.12 us -> 21 us
  matrix products: 13.2 us -> 0 us
  between operations: 13.7 us -> 0.76 us
  Pallas kernels: 0 us -> 12 us
  local copies, waits for them, and re-layouts: 4.43 us -> 0.12 us
    all_gather x3 -> x0, waiting for transfers between devices: 110 us -> none  [the longest x1 51.2 us: body(): lax.all_gather(out_weight, 'outer', axis=1, tiled=True)]
    ppermute x0 -> x20, waiting for transfers between devices: none -> 54.8 us  [the longest x3 28.8 us: along_node(): lax.ppermute(array, 'node', [((i + d) % node, i) for i in range(node)])]
    all_to_all x1 -> x0, blocking collectives: 35.8 us -> none  [body(): lax.all_to_all(grad_full, 'outer', split_axis=1, concat_axis=0, tiled=True)]
    ppermute x0 -> x20, starting transfers between devices: none -> 21 us  [the longest x14 10.9 us: shift(): lax.ppermute(array, 'outer', [(place(o, db, da, dc), o) for o in range(la...]
    dot_general x2 -> x0, matrix products: 13.2 us -> none  [the longest x1 6.68 us: body(): lax.dot_general(lax.all_gather(context, 'outer', axis=0, tiled=True), own...]
    pallas_call x0 -> x8, Pallas kernels: none -> 12 us  [call(): pl.pallas_call(kernel, out_shape=out, in_specs=in_specs or [VMEM] * len(a...]
    all_to_all x1 -> x0, local copies, waits for them, and re-layouts: 2.39 us -> none  [body(): lax.all_to_all(grad_full, 'outer', split_axis=1, concat_axis=0, tiled=True)]
    unnamed x3 -> x6, local copies, waits for them, and re-layouts: 2.04 us -> 0.02 us
  transfers between devices with their start and end apart: 3 -> 20, of which waited for: 3 -> 12; matrix products, arithmetic and copies ran while one was open for 5% -> 0% of each run, Pallas kernels for 0% -> 11%
where the time goes in v4:
time: 88.8 us; the launch traced here: 88.6 us
  waiting for transfers between devices  54.8 us (62%)
  starting transfers between devices  21 us (24%)
  Pallas kernels  12 us (14%)
    ppermute x3, waiting for transfers between devices, along_node(): lax.ppermute(array, 'node', [((i + d) % node, i) for i in range(node)])  28.8 us
    ppermute x14, waiting for transfers between devices, shift(): lax.ppermute(array, 'outer', [(place(o, db, da, dc), o) for o in range(la...  17.5 us
    pallas_call x8, Pallas kernels, call(): pl.pallas_call(kernel, out_shape=out, in_specs=in_specs or [VMEM] * len(a...  12 us
    ppermute x14, starting transfers between devices, shift(): lax.ppermute(array, 'outer', [(place(o, db, da, dc), o) for o in range(la...  10.9 us
    ppermute x3, waiting for transfers between devices, body(): lax.ppermute(x, 'node', [(i ^ 1, i) for i in range(s.node)])  8.52 us
    ppermute x3, starting transfers between devices, along_node(): lax.ppermute(array, 'node', [((i + d) % node, i) for i in range(node)])  5.33 us
    ppermute x3, starting transfers between devices, body(): lax.ppermute(x, 'node', [(i ^ 1, i) for i in range(s.node)])  4.75 us
  transfers between devices with their start and end apart: 20, of which 12 were waited for; matrix products, arithmetic and copies ran while one was open for 0% of the time, Pallas kernels for 11%

profile of v4, /device:TPU:0, one launch (start us, length us, event | category | flops | bytes accessed | tf_op | source)
XLA Modules:
  0.0 88.6 jit_solution(3627812631772086386)
XLA Ops:
  0.6 3.1 %collective-permute-start.1 = (bf16[256,1024]{1,0:T(8,128)(2,1)}, bf16[256,1024]{1,0:T(8,128)(2,1)S(1)}, u32[]{:S(2)}, u32[]{:S(2)}) collective-permute-start(bf16[256,1024]{1,0:T(8,128)(2,1)} %refs_0_.1), channel_id=1, source_target_pairs={{3,0},{0,1},{1,2},{2,3},{7,4},{4,5},{5,6},{6,7},{11,8},{8,9},{9,10... | collective-permute-start | bytes 1572872 | tf_op jit(solution)/shard_map/ppermute | solution.py:50
  3.7 2.5 %shard_map.51 = bf16[1536,512]{1,0:T(8,128)(2,1)} custom-call(bf16[1024,512]{1,0:T(8,128)(2,1)} %weight.3, bf16[256,1024]{1,0:T(8,128)(2,1)} %context.2), custom_call_target="tpu_custom_call" | custom-call | tf_op jit(solution)/shard_map/pallas_call | solution.py:71
  6.3 1.6 %collective-permute-start.4 = (bf16[1536,512]{1,0:T(8,128)(2,1)}, bf16[1536,512]{1,0:T(8,128)(2,1)S(1)}, u32[]{:S(2)}, u32[]{:S(2)}) collective-permute-start(bf16[1536,512]{1,0:T(8,128)(2,1)} %shard_map.51), channel_id=1, source_target_pairs={{8,0},{12,4},{0,8},{4,12},{24,16},{28,20},{16,24},{20,28},{9,1},{1... | collective-permute-start | bytes 4718600 | tf_op jit(solution)/shard_map/ppermute | solution.py:41
  7.8 1.5 %collective-permute-start.5 = (bf16[1536,512]{1,0:T(8,128)(2,1)}, bf16[1536,512]{1,0:T(8,128)(2,1)S(1)}, u32[]{:S(2)}, u32[]{:S(2)}) collective-permute-start(bf16[1536,512]{1,0:T(8,128)(2,1)} %shard_map.51), channel_id=1, source_target_pairs={{16,0},{20,4},{24,8},{28,12},{0,16},{4,20},{8,24},{12,28},{17,1},{... | collective-permute-start | bytes 4718600 | tf_op jit(solution)/shard_map/ppermute | solution.py:41
  9.3 2.2 %collective-permute-start = (bf16[256,1024]{1,0:T(8,128)(2,1)S(1)}, bf16[256,1024]{1,0:T(8,128)(2,1)S(1)}, u32[]{:S(2)}, u32[]{:S(2)}) collective-permute-start(bf16[256,1024]{1,0:T(8,128)(2,1)S(1)} %copy-done.2), channel_id=1, source_target_pairs={{1,0},{2,1},{3,2},{0,3},{5,4},{6,5},{7,6},{4,7},{9,8},{10,9},{11,1... | collective-permute-start | bytes 1572872 | tf_op jit(solution)/shard_map/ppermute | solution.py:50
  11.6 7.2 %collective-permute-done.1.refs_3_ = bf16[256,1024]{1,0:T(8,128)(2,1)S(1)} collective-permute-done((bf16[256,1024]{1,0:T(8,128)(2,1)}, bf16[256,1024]{1,0:T(8,128)(2,1)S(1)}, u32[]{:S(2)}, u32[]{:S(2)}) %collective-permute-start.1) | collective-permute-done | bytes 524320 | tf_op jit(solution)/shard_map/ppermute | solution.py:50
  18.8 11.1 %collective-permute-done.refs_1_ = bf16[256,1024]{1,0:T(8,128)(2,1)S(1)} collective-permute-done((bf16[256,1024]{1,0:T(8,128)(2,1)S(1)}, bf16[256,1024]{1,0:T(8,128)(2,1)S(1)}, u32[]{:S(2)}, u32[]{:S(2)}) %collective-permute-start) | collective-permute-done | bytes 524320 | tf_op jit(solution)/shard_map/ppermute | solution.py:50
  29.9 10.5 %collective-permute-done.2.refs_2_ = bf16[256,1024]{1,0:T(8,128)(2,1)S(1)} collective-permute-done((bf16[256,1024]{1,0:T(8,128)(2,1)S(1)}, bf16[256,1024]{1,0:T(8,128)(2,1)S(1)}, u32[]{:S(2)}, u32[]{:S(2)}) %collective-permute-start.2) | collective-permute-done | bytes 524320 | tf_op jit(solution)/shard_map/ppermute | solution.py:50
  40.8 1.6 %collective-permute-done.4.refs_0_ = bf16[1536,512]{1,0:T(8,128)(2,1)S(1)} collective-permute-done((bf16[1536,512]{1,0:T(8,128)(2,1)}, bf16[1536,512]{1,0:T(8,128)(2,1)S(1)}, u32[]{:S(2)}, u32[]{:S(2)}) %collective-permute-start.4) | collective-permute-done | bytes 1572896 | tf_op jit(solution)/shard_map/ppermute | solution.py:41
  43.6 1.6 %collective-permute-start.9 = (bf16[256,512]{1,0:T(8,128)(2,1)S(1)}, bf16[256,512]{1,0:T(8,128)(2,1)S(1)}, u32[]{:S(2)}, u32[]{:S(2)}) collective-permute-start(bf16[256,512]{1,0:T(8,128)(2,1)S(1)} %slice.12), channel_id=1, source_target_pairs={{16,0},{20,4},{24,8},{28,12},{0,16},{4,20},{8,24},{12,28},{17,1},{... | collective-permute-start | bytes 786440 | tf_op jit(solution)/shard_map/ppermute | solution.py:41
  45.9 1.5 %collective-permute-start.6 = (bf16[256,512]{1,0:T(8,128)(2,1)S(1)}, bf16[256,512]{1,0:T(8,128)(2,1)S(1)}, u32[]{:S(2)}, u32[]{:S(2)}) collective-permute-start(bf16[256,512]{1,0:T(8,128)(2,1)S(1)} %get-tuple-element.28), channel_id=1, source_target_pairs={{24,0},{28,4},{16,8},{20,12},{8,16},{12,20},{0,24},{4,28},{25,1},{... | collective-permute-start | bytes 786440 | tf_op jit(solution)/shard_map/ppermute | solution.py:41
  47.9 1.5 %collective-permute-start.8 = (bf16[256,512]{1,0:T(8,128)(2,1)S(1)}, bf16[256,512]{1,0:T(8,128)(2,1)S(1)}, u32[]{:S(2)}, u32[]{:S(2)}) collective-permute-start(bf16[256,512]{1,0:T(8,128)(2,1)S(1)} %get-tuple-element.30), channel_id=1, source_target_pairs={{16,0},{20,4},{24,8},{28,12},{0,16},{4,20},{8,24},{12,28},{17,1},{... | collective-permute-start | bytes 786440 | tf_op jit(solution)/shard_map/ppermute | solution.py:41
  49.4 5.2 %collective-permute-done.9.refs_2_ = bf16[256,512]{1,0:T(8,128)(2,1)S(1)} collective-permute-done((bf16[256,512]{1,0:T(8,128)(2,1)S(1)}, bf16[256,512]{1,0:T(8,128)(2,1)S(1)}, u32[]{:S(2)}, u32[]{:S(2)}) %collective-permute-start.9) | collective-permute-done | bytes 262176 | tf_op jit(solution)/shard_map/ppermute | solution.py:41
  54.6 5.3 %collective-permute-done.6.refs_0_ = bf16[256,512]{1,0:T(8,128)(2,1)S(1)} collective-permute-done((bf16[256,512]{1,0:T(8,128)(2,1)S(1)}, bf16[256,512]{1,0:T(8,128)(2,1)S(1)}, u32[]{:S(2)}, u32[]{:S(2)}) %collective-permute-start.6) | collective-permute-done | bytes 262176 | tf_op jit(solution)/shard_map/ppermute | solution.py:41
  60.0 2.8 %collective-permute-done.7.refs_0_ = bf16[256,512]{1,0:T(8,128)(2,1)S(1)} collective-permute-done((bf16[256,512]{1,0:T(8,128)(2,1)S(1)}, bf16[256,512]{1,0:T(8,128)(2,1)S(1)}, u32[]{:S(2)}, u32[]{:S(2)}) %collective-permute-start.7) | collective-permute-done | bytes 262176 | tf_op jit(solution)/shard_map/ppermute | solution.py:41
  64.2 1.6 %collective-permute-start.15 = (bf16[256,512]{1,0:T(8,128)(2,1)S(1)}, bf16[256,512]{1,0:T(8,128)(2,1)S(1)}, u32[]{:S(2)}, u32[]{:S(2)}) collective-permute-start(bf16[256,512]{1,0:T(8,128)(2,1)S(1)} %collective-permute-done.7.refs_0_), channel_id=1, source_target_pairs={{1,0},{0,1},{3,2},{2,3},{5,4},{4,5},{7,6},{6,7},{9,8},{8,9},{11,10... | collective-permute-start | bytes 786440 | tf_op jit(solution)/shard_map/ppermute | solution.py:244
  67.7 1.8 %shard_map.54 = (f32[256,1024]{1,0:T(8,128)S(1)}, f32[256,1024]{1,0:T(8,128)S(1)}) custom-call(bf16[4,256,512]{2,1,0:T(8,128)(2,1)S(1)} %get-tuple-element.23.mine, bf16[4,256,512]{2,1,0:T(8,128)(2,1)S(1)} %collective-permute-done.3.theirs.other, bf16[1024,512]{1,0:T(8,128)(2,1)S(1)} %copy-done, bf16[1536,512]{1,0:T(8,128)(2,1)S(1)} %collective-permute-done.4.refs_0_, ...), custom_call_target="tpu_custom_call" | custom-call | tf_op jit(solution)/shard_map/pallas_call | solution.py:71
  69.7 1.6 %collective-permute-start.16 = (bf16[256,512]{1,0:T(8,128)(2,1)S(1)}, bf16[256,512]{1,0:T(8,128)(2,1)S(1)}, u32[]{:S(2)}, u32[]{:S(2)}) collective-permute-start(bf16[256,512]{1,0:T(8,128)(2,1)S(1)} %collective-permute-done.8.refs_2_), channel_id=1, source_target_pairs={{1,0},{0,1},{3,2},{2,3},{5,4},{4,5},{7,6},{6,7},{9,8},{8,9},{11,10... | collective-permute-start | bytes 786440 | tf_op jit(solution)/shard_map/ppermute | solution.py:244
  72.6 1.6 %collective-permute-start.17 = (bf16[256,512]{1,0:T(8,128)(2,1)S(1)}, bf16[256,512]{1,0:T(8,128)(2,1)S(1)}, u32[]{:S(2)}, u32[]{:S(2)}) collective-permute-start(bf16[256,512]{1,0:T(8,128)(2,1)S(1)} %collective-permute-done.6.refs_0_), channel_id=1, source_target_pairs={{1,0},{0,1},{3,2},{2,3},{5,4},{4,5},{7,6},{6,7},{9,8},{8,9},{11,10... | collective-permute-start | bytes 786440 | tf_op jit(solution)/shard_map/ppermute | solution.py:244
  74.2 4.7 %collective-permute-done.16.refs_3_ = bf16[256,512]{1,0:T(8,128)(2,1)S(1)} collective-permute-done((bf16[256,512]{1,0:T(8,128)(2,1)S(1)}, bf16[256,512]{1,0:T(8,128)(2,1)S(1)}, u32[]{:S(2)}, u32[]{:S(2)}) %collective-permute-start.16) | collective-permute-done | bytes 262176 | tf_op jit(solution)/shard_map/ppermute | solution.py:244
  78.9 2.5 %shard_map.55.near = f32[1024,512]{1,0:T(8,128)S(1)} custom-call(bf16[1024,1024]{1,0:T(8,128)(2,1)S(1)} %shard_map.53.turned, bf16[1024,1024]{1,0:T(8,128)(2,1)S(1)} %collective-permute-done.11.theirs, bf16[4,256,512]{2,1,0:T(8,128)(2,1)S(1)} %get-tuple-element.23.mine, bf16[4,256,512]{2,1,0:T(8,128)(2,1)S(1)} %collective-permute-done.3.theirs.other, ...), custom_call_target="tpu_custom_call" | custom-call | tf_op jit(solution)/shard_map/pallas_call | solution.py:71
  81.4 2.6 %collective-permute-done.17.refs_1_ = bf16[256,512]{1,0:T(8,128)(2,1)S(1)} collective-permute-done((bf16[256,512]{1,0:T(8,128)(2,1)S(1)}, bf16[256,512]{1,0:T(8,128)(2,1)S(1)}, u32[]{:S(2)}, u32[]{:S(2)}) %collective-permute-start.17) | collective-permute-done | bytes 262176 | tf_op jit(solution)/shard_map/ppermute | solution.py:244
  84.4 2.6 %shard_map.57 = f32[1024,512]{1,0:T(8,128)} custom-call(f32[1024,512]{1,0:T(8,128)S(1)} %shard_map.55.near, bf16[1024,1024]{1,0:T(8,128)(2,1)S(1)} %shard_map.53.turned, bf16[1024,1024]{1,0:T(8,128)(2,1)S(1)} %collective-permute-done.11.theirs, bf16[256,512]{1,0:T(8,128)(2,1)S(1)} %collective-permute-done.6.refs_0_, ...), custom_call_target="tpu_custom_call" | custom-call | tf_op jit(solution)/shard_map/pallas_call | solution.py:71
  87.1 1.5 %shard_map.56 = bf16[256,1024]{1,0:T(8,128)(2,1)} custom-call(bf16[4,256,512]{2,1,0:T(8,128)(2,1)S(1)} %get-tuple-element.23.mine, bf16[4,256,512]{2,1,0:T(8,128)(2,1)S(1)} %get-tuple-element.24.other, f32[256,1024]{1,0:T(8,128)S(1)} %get-tuple-element.40.near, f32[256,1024]{1,0:T(8,128)S(1)} %collective-permute-done.12.near_theirs, ...), custom_call_target="tpu_custom_call" | custom-call | tf_op jit(solution)/shard_map/pallas_call | solution.py:71
  (34 shorter events, 8.1 us)
Async XLA Ops:
  0.6 8.7 %copy-start.2 = (bf16[256,1024]{1,0:T(8,128)(2,1)S(1)}, bf16[256,1024]{1,0:T(8,128)(2,1)}, u32[]{:S(2)}) copy-start(bf16[256,1024]{1,0:T(8,128)(2,1)} %refs_0_.1) | copy-start | bytes 1572868
  0.6 18.1 %collective-permute-start.1 = (bf16[256,1024]{1,0:T(8,128)(2,1)}, bf16[256,1024]{1,0:T(8,128)(2,1)S(1)}, u32[]{:S(2)}, u32[]{:S(2)}) collective-permute-start(bf16[256,1024]{1,0:T(8,128)(2,1)} %refs_0_.1), channel_id=1, source_target_pairs={{3,0},{0,1},{1,2},{2,3},{7,4},{4,5},{5,6},{6,7},{11,8},{8,9},{9,10... | collective-permute-start | bytes 1572872 | tf_op jit(solution)/shard_map/ppermute | solution.py:50
  6.3 36.1 %collective-permute-start.4 = (bf16[1536,512]{1,0:T(8,128)(2,1)}, bf16[1536,512]{1,0:T(8,128)(2,1)S(1)}, u32[]{:S(2)}, u32[]{:S(2)}) collective-permute-start(bf16[1536,512]{1,0:T(8,128)(2,1)} %shard_map.51), channel_id=1, source_target_pairs={{8,0},{12,4},{0,8},{4,12},{24,16},{28,20},{16,24},{20,28},{9,1},{1... | collective-permute-start | bytes 4718600 | tf_op jit(solution)/shard_map/ppermute | solution.py:41
  7.8 35.8 %collective-permute-start.5 = (bf16[1536,512]{1,0:T(8,128)(2,1)}, bf16[1536,512]{1,0:T(8,128)(2,1)S(1)}, u32[]{:S(2)}, u32[]{:S(2)}) collective-permute-start(bf16[1536,512]{1,0:T(8,128)(2,1)} %shard_map.51), channel_id=1, source_target_pairs={{16,0},{20,4},{24,8},{28,12},{0,16},{4,20},{8,24},{12,28},{17,1},{... | collective-permute-start | bytes 4718600 | tf_op jit(solution)/shard_map/ppermute | solution.py:41
  9.3 20.6 %collective-permute-start = (bf16[256,1024]{1,0:T(8,128)(2,1)S(1)}, bf16[256,1024]{1,0:T(8,128)(2,1)S(1)}, u32[]{:S(2)}, u32[]{:S(2)}) collective-permute-start(bf16[256,1024]{1,0:T(8,128)(2,1)S(1)} %copy-done.2), channel_id=1, source_target_pairs={{1,0},{2,1},{3,2},{0,3},{5,4},{6,5},{7,6},{4,7},{9,8},{10,9},{11,1... | collective-permute-start | bytes 1572872 | tf_op jit(solution)/shard_map/ppermute | solution.py:50
  18.8 21.6 %collective-permute-start.2 = (bf16[256,1024]{1,0:T(8,128)(2,1)S(1)}, bf16[256,1024]{1,0:T(8,128)(2,1)S(1)}, u32[]{:S(2)}, u32[]{:S(2)}) collective-permute-start(bf16[256,1024]{1,0:T(8,128)(2,1)S(1)} %collective-permute-done.1.refs_3_), channel_id=1, source_target_pairs={{3,0},{0,1},{1,2},{2,3},{7,4},{4,5},{5,6},{6,7},{11,8},{8,9},{9,10... | collective-permute-start | bytes 1572872 | tf_op jit(solution)/shard_map/ppermute | solution.py:50
  40.7 22.1 %copy-start.1 = (bf16[256,1024]{1,0:T(8,128)(2,1)S(1)}, bf16[256,1024]{1,0:T(8,128)(2,1)}, u32[]{:S(2)}) copy-start(bf16[256,1024]{1,0:T(8,128)(2,1)} %context.2) | copy-start | bytes 1572868
  40.7 5.1 %collective-permute-start.3 = (bf16[4,256,512]{2,1,0:T(8,128)(2,1)S(1)}, bf16[4,256,512]{2,1,0:T(8,128)(2,1)S(1)}, u32[]{:S(2)}, u32[]{:S(2)}) collective-permute-start(bf16[4,256,512]{2,1,0:T(8,128)(2,1)S(1)} %get-tuple-element.24.other), channel_id=1, source_target_pairs={{4,0},{0,4},{12,8},{8,12},{20,16},{16,20},{28,24},{24,28},{5,1},{1... | collective-permute-start | bytes 3145736 | tf_op jit(solution)/shard_map/ppermute | solution.py:41
  43.6 11.0 %collective-permute-start.9 = (bf16[256,512]{1,0:T(8,128)(2,1)S(1)}, bf16[256,512]{1,0:T(8,128)(2,1)S(1)}, u32[]{:S(2)}, u32[]{:S(2)}) collective-permute-start(bf16[256,512]{1,0:T(8,128)(2,1)S(1)} %slice.12), channel_id=1, source_target_pairs={{16,0},{20,4},{24,8},{28,12},{0,16},{4,20},{8,24},{12,28},{17,1},{... | collective-permute-start | bytes 786440 | tf_op jit(solution)/shard_map/ppermute | solution.py:41
  45.2 9.4 %collective-permute-start.10 = (bf16[256,512]{1,0:T(8,128)(2,1)S(1)}, bf16[256,512]{1,0:T(8,128)(2,1)S(1)}, u32[]{:S(2)}, u32[]{:S(2)}) collective-permute-start(bf16[256,512]{1,0:T(8,128)(2,1)S(1)} %slice.13), channel_id=1, source_target_pairs={{8,0},{12,4},{0,8},{4,12},{24,16},{28,20},{16,24},{20,28},{9,1},{1... | collective-permute-start | bytes 786440 | tf_op jit(solution)/shard_map/ppermute | solution.py:41
  45.9 14.1 %collective-permute-start.6 = (bf16[256,512]{1,0:T(8,128)(2,1)S(1)}, bf16[256,512]{1,0:T(8,128)(2,1)S(1)}, u32[]{:S(2)}, u32[]{:S(2)}) collective-permute-start(bf16[256,512]{1,0:T(8,128)(2,1)S(1)} %get-tuple-element.28), channel_id=1, source_target_pairs={{24,0},{28,4},{16,8},{20,12},{8,16},{12,20},{0,24},{4,28},{25,1},{... | collective-permute-start | bytes 786440 | tf_op jit(solution)/shard_map/ppermute | solution.py:41
  47.4 15.4 %collective-permute-start.7 = (bf16[256,512]{1,0:T(8,128)(2,1)S(1)}, bf16[256,512]{1,0:T(8,128)(2,1)S(1)}, u32[]{:S(2)}, u32[]{:S(2)}) collective-permute-start(bf16[256,512]{1,0:T(8,128)(2,1)S(1)} %get-tuple-element.29), channel_id=1, source_target_pairs={{8,0},{12,4},{0,8},{4,12},{24,16},{28,20},{16,24},{20,28},{9,1},{1... | collective-permute-start | bytes 786440 | tf_op jit(solution)/shard_map/ppermute | solution.py:41
  47.9 14.9 %collective-permute-start.8 = (bf16[256,512]{1,0:T(8,128)(2,1)S(1)}, bf16[256,512]{1,0:T(8,128)(2,1)S(1)}, u32[]{:S(2)}, u32[]{:S(2)}) collective-permute-start(bf16[256,512]{1,0:T(8,128)(2,1)S(1)} %get-tuple-element.30), channel_id=1, source_target_pairs={{16,0},{20,4},{24,8},{28,12},{0,16},{4,20},{8,24},{12,28},{17,1},{... | collective-permute-start | bytes 786440 | tf_op jit(solution)/shard_map/ppermute | solution.py:41
  63.5 4.2 %copy-start = (bf16[1024,512]{1,0:T(8,128)(2,1)S(1)}, bf16[1024,512]{1,0:T(8,128)(2,1)}, u32[]{:S(2)}) copy-start(bf16[1024,512]{1,0:T(8,128)(2,1)} %weight.3) | copy-start | bytes 3145732
  63.5 4.2 %collective-permute-start.11 = (bf16[1024,1024]{1,0:T(8,128)(2,1)S(1)}, bf16[1024,1024]{1,0:T(8,128)(2,1)S(1)}, u32[]{:S(2)}, u32[]{:S(2)}) collective-permute-start(bf16[1024,1024]{1,0:T(8,128)(2,1)S(1)} %shard_map.53.turned), channel_id=1, source_target_pairs={{4,0},{0,4},{12,8},{8,12},{20,16},{16,20},{28,24},{24,28},{5,1},{1... | collective-permute-start | bytes 6291464 | tf_op jit(solution)/shard_map/ppermute | solution.py:41
  63.6 20.3 %collective-permute-start.13 = (bf16[512,512]{1,0:T(8,128)(2,1)S(1)}, bf16[512,512]{1,0:T(8,128)(2,1)S(1)}, u32[]{:S(2)}, u32[]{:S(2)}) collective-permute-start(bf16[512,512]{1,0:T(8,128)(2,1)S(1)} %slice.14), channel_id=1, source_target_pairs={{16,0},{20,4},{24,8},{28,12},{0,16},{4,20},{8,24},{12,28},{17,1},{... | collective-permute-start | bytes 1572872 | tf_op jit(solution)/shard_map/ppermute | solution.py:41
  64.2 8.4 %collective-permute-start.15 = (bf16[256,512]{1,0:T(8,128)(2,1)S(1)}, bf16[256,512]{1,0:T(8,128)(2,1)S(1)}, u32[]{:S(2)}, u32[]{:S(2)}) collective-permute-start(bf16[256,512]{1,0:T(8,128)(2,1)S(1)} %collective-permute-done.7.refs_0_), channel_id=1, source_target_pairs={{1,0},{0,1},{3,2},{2,3},{5,4},{4,5},{7,6},{6,7},{9,8},{8,9},{11,10... | collective-permute-start | bytes 786440 | tf_op jit(solution)/shard_map/ppermute | solution.py:244
  65.8 18.2 %collective-permute-start.14 = (bf16[512,512]{1,0:T(8,128)(2,1)S(1)}, bf16[512,512]{1,0:T(8,128)(2,1)S(1)}, u32[]{:S(2)}, u32[]{:S(2)}) collective-permute-start(bf16[512,512]{1,0:T(8,128)(2,1)S(1)} %slice.15), channel_id=1, source_target_pairs={{8,0},{12,4},{0,8},{4,12},{24,16},{28,20},{16,24},{20,28},{9,1},{1... | collective-permute-start | bytes 1572872 | tf_op jit(solution)/shard_map/ppermute | solution.py:41
  69.5 17.6 %collective-permute-start.12 = (f32[256,1024]{1,0:T(8,128)S(1)}, f32[256,1024]{1,0:T(8,128)S(1)}, u32[]{:S(2)}, u32[]{:S(2)}) collective-permute-start(f32[256,1024]{1,0:T(8,128)S(1)} %get-tuple-element.41), channel_id=1, source_target_pairs={{4,0},{0,4},{12,8},{8,12},{20,16},{16,20},{28,24},{24,28},{5,1},{1... | collective-permute-start | bytes 3145736 | tf_op jit(solution)/shard_map/ppermute | solution.py:41
  69.7 9.1 %collective-permute-start.16 = (bf16[256,512]{1,0:T(8,128)(2,1)S(1)}, bf16[256,512]{1,0:T(8,128)(2,1)S(1)}, u32[]{:S(2)}, u32[]{:S(2)}) collective-permute-start(bf16[256,512]{1,0:T(8,128)(2,1)S(1)} %collective-permute-done.8.refs_2_), channel_id=1, source_target_pairs={{1,0},{0,1},{3,2},{2,3},{5,4},{4,5},{7,6},{6,7},{9,8},{8,9},{11,10... | collective-permute-start | bytes 786440 | tf_op jit(solution)/shard_map/ppermute | solution.py:244
  72.6 11.3 %collective-permute-start.17 = (bf16[256,512]{1,0:T(8,128)(2,1)S(1)}, bf16[256,512]{1,0:T(8,128)(2,1)S(1)}, u32[]{:S(2)}, u32[]{:S(2)}) collective-permute-start(bf16[256,512]{1,0:T(8,128)(2,1)S(1)} %collective-permute-done.6.refs_0_), channel_id=1, source_target_pairs={{1,0},{0,1},{3,2},{2,3},{5,4},{4,5},{7,6},{6,7},{9,8},{8,9},{11,10... | collective-permute-start | bytes 786440 | tf_op jit(solution)/shard_map/ppermute | solution.py:244
  83.9 3.2 %collective-permute-start.18 = (bf16[512,512]{1,0:T(8,128)(2,1)S(1)}, bf16[512,512]{1,0:T(8,128)(2,1)S(1)}, u32[]{:S(2)}, u32[]{:S(2)}) collective-permute-start(bf16[512,512]{1,0:T(8,128)(2,1)S(1)} %collective-permute-done.13.refs_0_), channel_id=1, source_target_pairs={{4,0},{0,4},{12,8},{8,12},{20,16},{16,20},{28,24},{24,28},{5,1},{1... | collective-permute-start | bytes 1572872 | tf_op jit(solution)/shard_map/ppermute | solution.py:41
  83.9 3.2 %collective-permute-start.19 = (bf16[512,512]{1,0:T(8,128)(2,1)S(1)}, bf16[512,512]{1,0:T(8,128)(2,1)S(1)}, u32[]{:S(2)}, u32[]{:S(2)}) collective-permute-start(bf16[512,512]{1,0:T(8,128)(2,1)S(1)} %collective-permute-done.14.refs_1_), channel_id=1, source_target_pairs={{4,0},{0,4},{12,8},{8,12},{20,16},{16,20},{28,24},{24,28},{5,1},{1... | collective-permute-start | bytes 1572872 | tf_op jit(solution)/shard_map/ppermute | solution.py:41

commit v5 on v4

v5 whole, which is shorter than its diff:
```python
import functools
import math

import jax
import jax.numpy as jnp
from jax import lax
from jax.experimental import pallas as pl
from jax.experimental.pallas import tpu as pltpu
from jax.sharding import PartitionSpec as P

F32, BF16 = jnp.float32, jnp.bfloat16
VMEM = pl.BlockSpec(memory_space=pltpu.VMEM)


def plane_of(outer):
    cores = 2 if outer % 2 == 0 else 1
    chips = outer // cores
    cols = max(d for d in range(1, math.isqrt(chips) + 1) if chips % d == 0)
    return chips // cols, cols, cores


def place(o, db, da, dc):
    rows, cols, cores = plane_of(lax.axis_size("outer"))
    b, a, c = o // (cols * cores), o // cores % cols, o % cores
    return ((b + db) % rows * cols + (a + da) % cols) * cores + (c + dc) % cores


def chip_at(db, da):
    rows, cols, cores = plane_of(lax.axis_size("outer"))
    chip = lax.div(lax.axis_index("outer"), jnp.int32(cores))
    b, a = lax.div(chip, jnp.int32(cols)), lax.rem(chip, jnp.int32(cols))
    return lax.rem(b + db % rows, jnp.int32(rows)) * cols + lax.rem(a + da % cols, jnp.int32(cols))


def kind_at(dc):
    cores = plane_of(lax.axis_size("outer"))[2]
    return lax.rem(lax.axis_index("outer") + dc, jnp.int32(cores))


def shift(array, db, da, dc=0):
    return lax.ppermute(array, "outer", [(place(o, db, da, dc), o) for o in range(lax.axis_size("outer"))])


def sibling(array, cuts=()):
    at = [0] + [int(array.shape[0] * cut) for cut in cuts] + [array.shape[0]]
    pieces = [shift(array[i:j], 0, 0, 1) for i, j in zip(at, at[1:])]
    return pieces[0] if len(pieces) == 1 else jnp.concatenate(pieces)


def along_node(array, d):
    node = lax.axis_size("node")
    return lax.ppermute(array, "node", [((i + d) % node, i) for i in range(node)])


def after(arrays, done):
    return lax.optimization_barrier((arrays, done))[0]


def call(kernel, out, *args, scratch=(), grid=None, in_specs=None, out_specs=None, vmem=40):
    return pl.pallas_call(
        kernel,
        out_shape=out,
        in_specs=in_specs or [VMEM] * len(args),
        out_specs=out_specs or jax.tree.map(lambda _: VMEM, out),
        scratch_shapes=scratch,
        compiler_params=pltpu.CompilerParams(vmem_limit_bytes=vmem * 2**20),
        cost_estimate=pl.CostEstimate(flops=0, bytes_accessed=0, transcendentals=0),
        **({"grid": grid} if grid else {}),
    )(*args)


class Sizes:
    def __init__(self, context, grad_out, out_weight):
        self.outer, self.node = lax.axis_size("outer"), lax.axis_size("node")
        self.rows, self.cols, self.cores = plane_of(self.outer)
        self.chips = self.rows * self.cols
        self.tokens, self.held = grad_out.shape
        self.taken, self.width = out_weight.shape
        self.row = [(0, da) for da in range(1, self.cols)]
        self.column = [(db, 0) for db in range(1, self.rows)]
        self.across = [(db, da) for db in range(1, self.rows) for da in range(1, self.cols)]
        self.half = self.taken // 2
        self.fits = self.width % 128 == 0 and self.held % (self.width * self.cores) == 0 and self.node % 2 == 0 and self.node > 2


def route_kernel(s, *refs):
    blocks, (mine, other, whole) = refs[: s.node], refs[s.node :]
    for d, block in enumerate(blocks):
        whole[lax.rem(lax.axis_index("node") + d, jnp.int32(s.node))] = block[...]
    for out, kind in ((mine, kind_at(0)), (other, kind_at(1))):
        for chip in range(s.chips):
            first = chip * s.cores * s.width
            at = pl.multiple_of(first % s.held + kind * s.width, 128)
            out[chip] = whole[first // s.held, :, pl.ds(at, s.width)]


def pick_kernel(s, mine, theirs, *sent):
    odd = lax.rem(lax.axis_index("node"), jnp.int32(2))
    for (db, da), out in zip(s.row + s.column, sent):
        out[: s.tokens] = mine[chip_at(-db, -da)]
        out[s.tokens :] = theirs[chip_at(-db, -da)]
    for source, here in ((mine, odd == 0), (theirs, odd == 1)):

        @pl.when(here)
        def _(source=source):
            for (db, da), out in zip(s.across, sent[len(s.row + s.column) :]):
                out[...] = source[chip_at(-db, -da)]


def put(s, packed, slot, n, share, second):
    odd = lax.rem(lax.axis_index("node"), jnp.int32(2))
    for block, half in ((share, odd), (second, 1 - odd)):
        at = pl.multiple_of((half * n + slot) * s.tokens, 128)
        packed[pl.ds(at, s.tokens)] = block[...]


def turn_kernel(s, *refs):
    *blocks, out = refs
    at = 0
    for block in blocks:
        out[:, at : at + block.shape[0]] = block[...].T
        at += block.shape[0]


def over_chips(s, mine, theirs, pieces):
    total = 0.0
    for at, piece in pieces:
        chip = chip_at(*at)
        left = jnp.concatenate([mine[chip], theirs[chip]], axis=0)
        total += lax.dot_general(left, piece, (((1,), (1,)), ((), ())), preferred_element_type=F32)
    return total


def context_kernel(s, mine, theirs, *refs):
    *weights, out = refs
    for h in range(2):
        side = slice(h * s.half, (h + 1) * s.half)
        pieces = [(at, weight[side]) for at, weight in zip([(0, 0)] + s.row + s.column, weights)]
        out[:, side] = over_chips(s, mine, theirs, pieces)


def context_far_kernel(s, mine, theirs, near, *refs):
    *pairs, own, others = refs
    for h in range(2):
        side = slice(h * s.half, (h + 1) * s.half)
        total = near[:, side] + over_chips(s, mine, theirs, [(at, pairs[2 * k + h][...]) for k, at in enumerate(s.across)])
        own[:, side] = total[: s.tokens]
        others[:, side] = total[s.tokens :]


def early_kernel(s, turned, theirs, far, far_theirs, mine, other, *refs):
    *blocks, out, packed = refs
    n = 1 + len(blocks) // 2
    packed[: s.tokens] = mine[chip_at(0, 0)]
    packed[n * s.tokens : (n + 1) * s.tokens] = other[chip_at(0, 0)]
    for k in range(1, n):
        put(s, packed, k, n, *blocks[2 * k - 2 : 2 * k])
    left = [turned[:, : s.tokens], far[...], theirs[:, : s.tokens], far_theirs[...]]
    out[...] = jnp.dot(jnp.concatenate(left, axis=1), packed[...], preferred_element_type=F32)


def late_kernel(s, scale, early, turned, theirs, *refs):
    *blocks, out, packed = refs
    n = len(blocks)
    for k, block in enumerate(blocks):
        packed[k * s.tokens : (k + 1) * s.tokens] = block[: s.tokens]
        packed[(n + k) * s.tokens : (n + k + 1) * s.tokens] = block[s.tokens :]
    left = jnp.concatenate([turned[:, s.tokens :], theirs[:, s.tokens :]], axis=1)
    out[...] = (early[...] + jnp.dot(left, packed[...], preferred_element_type=F32)) * scale


def body(context, grad_out, out_weight):
    s = Sizes(context, grad_out, out_weight)
    if not s.fits or s.cores == 1:
        return plain(context, grad_out, out_weight)
    shape = lambda *dims, dtype=BF16: jax.ShapeDtypeStruct(dims, dtype)
    scale = 1.0 / math.sqrt(s.tokens * s.outer)
    near = s.row + s.column

    def straight(block):
        return {at: shift(block, *at) for at in near}

    def diagonal(blocks):
        half = next(iter(blocks.values())).shape[0] // 2
        pairs = []
        for db, da in s.across:
            pairs.append(shift(blocks[0, da][:half], db, 0))
            pairs.append(shift(blocks[db, 0][half:], 0, da))
        return pairs

    weights = straight(out_weight)
    around = {0: grad_out, s.node - 1: along_node(grad_out, -1), 1: along_node(grad_out, 1)}
    contexts = {at: shift(context, *at) for at in s.row}
    contexts |= {at: shift(after(context, around[s.node - 1]), *at) for at in s.column}
    weights, around = lax.optimization_barrier((weights, around))
    for step in range(2, s.node // 2 + 1):
        around[s.node - step] = along_node(around[s.node - step + 1], -1)
        if 2 * step < s.node:
            around[step] = along_node(around[step - 1], 1)
    weights_far = diagonal(weights)
    contexts_far = diagonal(contexts)
    turn = functools.partial(turn_kernel, s)
    turned = call(turn, shape(s.taken, (1 + len(near)) * s.tokens), context, *contexts.values())
    turned_other = sibling(turned)
    turned_far = call(turn, shape(s.taken, len(s.across) * s.tokens), *contexts_far)
    turned_far_other = sibling(turned_far, ())

    columns = shape(s.chips, s.tokens, s.width)
    mine, other = call(
        functools.partial(route_kernel, s), [columns] * 2, *[around[d] for d in range(s.node)],
        scratch=[pltpu.VMEM((s.node, s.tokens, s.held), BF16)],
    )
    theirs = sibling(after(other, weights_far))

    outs = [shape(s.cores * s.tokens, s.width)] * len(near) + [shape(s.tokens, s.width)] * len(s.across)
    sent = call(functools.partial(pick_kernel, s), outs, mine, after(theirs, turned_other))
    shares = [shift(x, *at) for x, at in zip(sent[len(near) :], s.across)]
    blocks = [shift(x, *at) for x, at in zip(sent, near)]
    far = [(x, lax.ppermute(x, "node", [(i ^ 1, i) for i in range(s.node)])) for x in shares]

    half_sums = shape(s.tokens, s.taken, dtype=F32)
    sums = call(
        functools.partial(context_kernel, s), shape(s.cores * s.tokens, s.taken, dtype=F32),
        mine, theirs, out_weight, *weights.values(),
    )
    own, others = call(functools.partial(context_far_kernel, s), [half_sums] * 2, mine, theirs, sums, *weights_far)
    context_grad = (own + sibling(others, (0.25, 0.5, 0.75))).astype(BF16)

    def by_rows(x):
        return pl.BlockSpec((s.taken // 4, x.shape[1]), lambda i: (i, 0))

    result = shape(s.taken, s.width, dtype=F32)
    lefts = [turned, turned_other, turned_far, turned_far_other]
    rights = [mine, theirs, *[x for two in far for x in two]]
    early = call(
        functools.partial(early_kernel, s), result, *lefts, *rights,
        grid=(4,), in_specs=[by_rows(x) for x in lefts] + [VMEM] * len(rights), out_specs=by_rows(result),
        scratch=[pltpu.VMEM((2 * (1 + len(far)) * s.tokens, s.width), BF16)],
    )
    lefts = [early, turned, turned_other]
    weight_grad = call(
        functools.partial(late_kernel, s, scale), result, *lefts, *blocks,
        grid=(4,), in_specs=[by_rows(x) for x in lefts] + [VMEM] * len(blocks), out_specs=by_rows(result),
        scratch=[pltpu.VMEM((2 * len(blocks) * s.tokens, s.width), BF16)],
    )
    return (context_grad, weight_grad)


def plain(context, grad_out, out_weight):
    grad_full = lax.all_gather(grad_out, "node", axis=1, tiled=True)
    weight = lax.all_gather(out_weight, "outer", axis=1, tiled=True)
    context_grad = lax.dot_general(grad_full, weight, (((1,), (1,)), ((), ())), preferred_element_type=F32)
    scale = 1.0 / math.sqrt(grad_full.shape[0] * lax.axis_size("outer"))
    owner_cols = lax.all_to_all(grad_full, "outer", split_axis=1, concat_axis=0, tiled=True)
    context = lax.all_gather(context, "outer", axis=0, tiled=True)
    weight_grad = lax.dot_general(context, owner_cols, (((0,), (0,)), ((), ())), preferred_element_type=F32)
    return (context_grad.astype(BF16), weight_grad * scale)


def solution(mesh):
    in_specs = (P("outer", "node"), P("outer", "node"), P("node", "outer"))
    out_specs = (P("outer", "node"), P("node", "outer"))
    return jax.shard_map(body, mesh=mesh, in_specs=in_specs, out_specs=out_specs, check_vma=False)
```

time: 88.8 us -> 83 us (0.935)
  Pallas kernels: 12 us -> 8.37 us
  waiting for transfers between devices: 54.8 us -> 51.9 us
  other arithmetic: 0 us -> 0.93 us
    ppermute x14 -> x18, waiting for transfers between devices: 17.5 us -> 22.8 us  [shift(): lax.ppermute(array, 'outer', [(place(o, db, da, dc), o) for o in range(la...]
    ppermute x3 -> x1, waiting for transfers between devices: 8.52 us -> 3.86 us  [body(): lax.ppermute(x, 'node', [(i ^ 1, i) for i in range(s.node)])]
    pallas_call x8, Pallas kernels: 12 us -> 8.37 us  [call(): pl.pallas_call(kernel, out_shape=out, in_specs=in_specs or [VMEM] * len(a...]
    ppermute x3, waiting for transfers between devices: 28.8 us -> 25.2 us  [along_node(): lax.ppermute(array, 'node', [((i + d) % node, i) for i in range(node)])]
    ppermute x14 -> x18, starting transfers between devices: 10.9 us -> 14.1 us  [shift(): lax.ppermute(array, 'outer', [(place(o, db, da, dc), o) for o in range(la...]
    ppermute x3 -> x1, starting transfers between devices: 4.75 us -> 1.58 us  [body(): lax.ppermute(x, 'node', [(i ^ 1, i) for i in range(s.node)])]
    convert_element_type x0 -> x1, other arithmetic: none -> 0.93 us  [body(): context_grad = (own + sibling(others, (0.25, 0.5, 0.75))).astype(BF16)]
  transfers between devices with their start and end apart: 20 -> 22, of which waited for: 12 -> 12; matrix products, arithmetic and copies ran while one was open for 0% -> 1% of each run, Pallas kernels for 11% -> 7%
where the time goes in v5:
time: 83 us; the launch traced here: 82.8 us
  waiting for transfers between devices  51.9 us (63%)
  starting transfers between devices  20.6 us (25%)
  Pallas kernels  8.37 us (10%)
  other arithmetic  0.93 us (1%)
    ppermute x3, waiting for transfers between devices, along_node(): lax.ppermute(array, 'node', [((i + d) % node, i) for i in range(node)])  25.2 us
    ppermute x18, waiting for transfers between devices, shift(): lax.ppermute(array, 'outer', [(place(o, db, da, dc), o) for o in range(la...  22.8 us
    ppermute x18, starting transfers between devices, shift(): lax.ppermute(array, 'outer', [(place(o, db, da, dc), o) for o in range(la...  14.1 us
    pallas_call x8, Pallas kernels, call(): pl.pallas_call(kernel, out_shape=out, in_specs=in_specs or [VMEM] * len(a...  8.37 us
    ppermute x3, starting transfers between devices, along_node(): lax.ppermute(array, 'node', [((i + d) % node, i) for i in range(node)])  4.95 us
    ppermute x1, waiting for transfers between devices, body(): lax.ppermute(x, 'node', [(i ^ 1, i) for i in range(s.node)])  3.86 us
  transfers between devices with their start and end apart: 22, of which 12 were waited for; matrix products, arithmetic and copies ran while one was open for 1% of the time, Pallas kernels for 7%

profile of v5, /device:TPU:0, one launch (start us, length us, event | category | flops | bytes accessed | tf_op | source)
XLA Modules:
  0.0 82.8 jit_solution(5253124342154477923)
XLA Ops:
  0.6 3.0 %collective-permute-start = (bf16[1024,512]{1,0:T(8,128)(2,1)}, bf16[1024,512]{1,0:T(8,128)(2,1)S(1)}, u32[]{:S(2)}, u32[]{:S(2)}) collective-permute-start(bf16[1024,512]{1,0:T(8,128)(2,1)} %refs_0_.3), channel_id=1, source_target_pairs={{8,0},{12,4},{0,8},{4,12},{24,16},{28,20},{16,24},{20,28},{9,1},{1... | collective-permute-start | bytes 3145736 | tf_op jit(solution)/shard_map/ppermute | solution.py:41
  3.6 1.5 %collective-permute-start.1 = (bf16[1024,512]{1,0:T(8,128)(2,1)}, bf16[1024,512]{1,0:T(8,128)(2,1)S(1)}, u32[]{:S(2)}, u32[]{:S(2)}) collective-permute-start(bf16[1024,512]{1,0:T(8,128)(2,1)} %refs_0_.3), channel_id=1, source_target_pairs={{16,0},{20,4},{24,8},{28,12},{0,16},{4,20},{8,24},{12,28},{17,1},{... | collective-permute-start | bytes 3145736 | tf_op jit(solution)/shard_map/ppermute | solution.py:41
  5.2 1.6 %collective-permute-start.3 = (bf16[256,1024]{1,0:T(8,128)(2,1)}, bf16[256,1024]{1,0:T(8,128)(2,1)S(1)}, u32[]{:S(2)}, u32[]{:S(2)}) collective-permute-start(bf16[256,1024]{1,0:T(8,128)(2,1)} %refs_0_.2), channel_id=1, source_target_pairs={{3,0},{0,1},{1,2},{2,3},{7,4},{4,5},{5,6},{6,7},{11,8},{8,9},{9,10... | collective-permute-start | bytes 1572872 | tf_op jit(solution)/shard_map/ppermute | solution.py:52
  6.7 2.2 %collective-permute-start.2 = (bf16[256,1024]{1,0:T(8,128)(2,1)}, bf16[256,1024]{1,0:T(8,128)(2,1)S(1)}, u32[]{:S(2)}, u32[]{:S(2)}) collective-permute-start(bf16[256,1024]{1,0:T(8,128)(2,1)} %refs_0_.2), channel_id=1, source_target_pairs={{1,0},{2,1},{3,2},{0,3},{5,4},{6,5},{7,6},{4,7},{9,8},{10,9},{11,1... | collective-permute-start | bytes 1572872 | tf_op jit(solution)/shard_map/ppermute | solution.py:52
  9.5 12.6 %collective-permute-done.3.refs_3_ = bf16[256,1024]{1,0:T(8,128)(2,1)S(1)} collective-permute-done((bf16[256,1024]{1,0:T(8,128)(2,1)}, bf16[256,1024]{1,0:T(8,128)(2,1)S(1)}, u32[]{:S(2)}, u32[]{:S(2)}) %collective-permute-start.3) | collective-permute-done | bytes 524320 | tf_op jit(solution)/shard_map/ppermute | solution.py:52
  22.6 8.4 %collective-permute-done.2.refs_1_ = bf16[256,1024]{1,0:T(8,128)(2,1)S(1)} collective-permute-done((bf16[256,1024]{1,0:T(8,128)(2,1)}, bf16[256,1024]{1,0:T(8,128)(2,1)S(1)}, u32[]{:S(2)}, u32[]{:S(2)}) %collective-permute-start.2) | collective-permute-done | bytes 524320 | tf_op jit(solution)/shard_map/ppermute | solution.py:52
  31.0 1.1 %collective-permute-start.4 = (bf16[256,1024]{1,0:T(8,128)(2,1)S(1)}, bf16[256,1024]{1,0:T(8,128)(2,1)S(1)}, u32[]{:S(2)}, u32[]{:S(2)}) collective-permute-start(bf16[256,1024]{1,0:T(8,128)(2,1)S(1)} %collective-permute-done.3.refs_3_), channel_id=1, source_target_pairs={{3,0},{0,1},{1,2},{2,3},{7,4},{4,5},{5,6},{6,7},{11,8},{8,9},{9,10... | collective-permute-start | bytes 1572872 | tf_op jit(solution)/shard_map/ppermute | solution.py:52
  33.7 5.3 %collective-permute-done.12.refs_1_ = bf16[256,1024]{1,0:T(8,128)(2,1)S(1)} collective-permute-done((bf16[256,1024]{1,0:T(8,128)(2,1)}, bf16[256,1024]{1,0:T(8,128)(2,1)S(1)}, u32[]{:S(2)}, u32[]{:S(2)}) %collective-permute-start.12) | collective-permute-done | bytes 524320 | tf_op jit(solution)/shard_map/ppermute | solution.py:41
  39.1 2.1 %collective-permute-done.13.refs_2_ = bf16[256,1024]{1,0:T(8,128)(2,1)S(1)} collective-permute-done((bf16[256,1024]{1,0:T(8,128)(2,1)}, bf16[256,1024]{1,0:T(8,128)(2,1)S(1)}, u32[]{:S(2)}, u32[]{:S(2)}) %collective-permute-start.13) | collective-permute-done | bytes 524320 | tf_op jit(solution)/shard_map/ppermute | solution.py:41
  41.7 4.3 %collective-permute-done.4.refs_2_ = bf16[256,1024]{1,0:T(8,128)(2,1)S(1)} collective-permute-done((bf16[256,1024]{1,0:T(8,128)(2,1)S(1)}, bf16[256,1024]{1,0:T(8,128)(2,1)S(1)}, u32[]{:S(2)}, u32[]{:S(2)}) %collective-permute-start.4) | collective-permute-done | bytes 524320 | tf_op jit(solution)/shard_map/ppermute | solution.py:52
  46.3 3.2 %collective-permute-done.6.refs_1_ = bf16[512,512]{1,0:T(8,128)(2,1)S(1)} collective-permute-done((bf16[512,512]{1,0:T(8,128)(2,1)S(1)}, bf16[512,512]{1,0:T(8,128)(2,1)S(1)}, u32[]{:S(2)}, u32[]{:S(2)}) %collective-permute-start.6) | collective-permute-done | bytes 524320 | tf_op jit(solution)/shard_map/ppermute | solution.py:41
  49.5 1.5 %collective-permute-done.5.refs_0_ = bf16[512,512]{1,0:T(8,128)(2,1)S(1)} collective-permute-done((bf16[512,512]{1,0:T(8,128)(2,1)S(1)}, bf16[512,512]{1,0:T(8,128)(2,1)S(1)}, u32[]{:S(2)}, u32[]{:S(2)}) %collective-permute-start.5) | collective-permute-done | bytes 524320 | tf_op jit(solution)/shard_map/ppermute | solution.py:41
  51.0 1.6 %collective-permute-start.15 = (bf16[128,1024]{1,0:T(8,128)(2,1)S(1)}, bf16[128,1024]{1,0:T(8,128)(2,1)S(1)}, u32[]{:S(2)}, u32[]{:S(2)}) collective-permute-start(bf16[128,1024]{1,0:T(8,128)(2,1)S(1)} %slice.32), channel_id=1, source_target_pairs={{16,0},{20,4},{24,8},{28,12},{0,16},{4,20},{8,24},{12,28},{17,1},{... | collective-permute-start | bytes 786440 | tf_op jit(solution)/shard_map/ppermute | solution.py:41
  53.6 1.8 %shard_map.51.near = f32[512,1024]{1,0:T(8,128)S(1)} custom-call(bf16[4,256,512]{2,1,0:T(8,128)(2,1)S(1)} %get-tuple-element.20.mine, bf16[4,256,512]{2,1,0:T(8,128)(2,1)S(1)} %collective-permute-done.7.theirs.other, bf16[1024,512]{1,0:T(8,128)(2,1)S(1)} %copy-done, bf16[1024,512]{1,0:T(8,128)(2,1)S(1)} %collective-permute-done.refs_1_, ...), custom_call_target="tpu_custom_call" | custom-call | tf_op jit(solution)/shard_map/pallas_call | solution.py:60
  57.1 2.7 %collective-permute-done.15.refs_0_ = bf16[128,1024]{1,0:T(8,128)(2,1)S(1)} collective-permute-done((bf16[128,1024]{1,0:T(8,128)(2,1)S(1)}, bf16[128,1024]{1,0:T(8,128)(2,1)S(1)}, u32[]{:S(2)}, u32[]{:S(2)}) %collective-permute-start.15) | collective-permute-done | bytes 262176 | tf_op jit(solution)/shard_map/ppermute | solution.py:41
  59.8 1.5 %collective-permute-start.18 = (bf16[256,512]{1,0:T(8,128)(2,1)S(1)}, bf16[256,512]{1,0:T(8,128)(2,1)S(1)}, u32[]{:S(2)}, u32[]{:S(2)}) collective-permute-start(bf16[256,512]{1,0:T(8,128)(2,1)S(1)} %get-tuple-element.29), channel_id=1, source_target_pairs={{24,0},{28,4},{16,8},{20,12},{8,16},{12,20},{0,24},{4,28},{25,1},{... | collective-permute-start | bytes 786440 | tf_op jit(solution)/shard_map/ppermute | solution.py:41
  62.0 1.5 %collective-permute-start.20 = (bf16[512,512]{1,0:T(8,128)(2,1)S(1)}, bf16[512,512]{1,0:T(8,128)(2,1)S(1)}, u32[]{:S(2)}, u32[]{:S(2)}) collective-permute-start(bf16[512,512]{1,0:T(8,128)(2,1)S(1)} %get-tuple-element.30), channel_id=1, source_target_pairs={{8,0},{12,4},{0,8},{4,12},{24,16},{28,20},{16,24},{20,28},{9,1},{1... | collective-permute-start | bytes 1572872 | tf_op jit(solution)/shard_map/ppermute | solution.py:41
  64.0 5.8 %collective-permute-done.18.refs_0_ = bf16[256,512]{1,0:T(8,128)(2,1)S(1)} collective-permute-done((bf16[256,512]{1,0:T(8,128)(2,1)S(1)}, bf16[256,512]{1,0:T(8,128)(2,1)S(1)}, u32[]{:S(2)}, u32[]{:S(2)}) %collective-permute-start.18) | collective-permute-done | bytes 262176 | tf_op jit(solution)/shard_map/ppermute | solution.py:41
  69.9 1.6 %collective-permute-start.19 = (bf16[256,512]{1,0:T(8,128)(2,1)S(1)}, bf16[256,512]{1,0:T(8,128)(2,1)S(1)}, u32[]{:S(2)}, u32[]{:S(2)}) collective-permute-start(bf16[256,512]{1,0:T(8,128)(2,1)S(1)} %collective-permute-done.18.refs_0_), channel_id=1, source_target_pairs={{1,0},{0,1},{3,2},{2,3},{5,4},{4,5},{7,6},{6,7},{9,8},{8,9},{11,10... | collective-permute-start | bytes 786440 | tf_op jit(solution)/shard_map/ppermute | solution.py:219
  71.4 0.9 %fusion = bf16[256,1024]{1,0:T(8,128)(2,1)} fusion(f32[256,1024]{1,0:T(8,128)S(1)} %get-tuple-element.25, f32[64,1024]{1,0:T(8,128)S(1)} %collective-permute-done.11, f32[64,1024]{1,0:T(8,128)S(1)} %collective-permute-done.10, f32[64,1024]{1,0:T(8,128)S(1)} %collective-permute-done.9, f32[64,1024]{1,0:T(8,128)S(1)} %collective-permute-done.8), kind=kLoop, calls=%fused_computation.1 | loop fusion | flops 1310720 | bytes 2621440 | tf_op jit(solution)/shard_map/convert_element_type | solution.py:227
  72.4 3.9 %collective-permute-done.19.refs_1_ = bf16[256,512]{1,0:T(8,128)(2,1)S(1)} collective-permute-done((bf16[256,512]{1,0:T(8,128)(2,1)S(1)}, bf16[256,512]{1,0:T(8,128)(2,1)S(1)}, u32[]{:S(2)}, u32[]{:S(2)}) %collective-permute-start.19) | collective-permute-done | bytes 262176 | tf_op jit(solution)/shard_map/ppermute | solution.py:219
  76.2 1.9 %shard_map.56.early = f32[1024,512]{1,0:T(8,128)S(1)} custom-call(bf16[1024,768]{1,0:T(8,128)(2,1)S(1)} %shard_map.53.turned, bf16[1024,768]{1,0:T(8,128)(2,1)S(1)} %collective-permute-done.14.theirs, bf16[1024,256]{1,0:T(8,128)(2,1)S(1)} %shard_map.54.far, bf16[1024,256]{1,0:T(8,128)(2,1)S(1)} %collective-permute-done.17.far_theirs, ...), custom_call_target="tpu_custom_call" | custom-call | tf_op jit(solution)/shard_map/pallas_call | solution.py:60
  78.1 1.8 %collective-permute-done.20.refs_0_ = bf16[512,512]{1,0:T(8,128)(2,1)S(1)} collective-permute-done((bf16[512,512]{1,0:T(8,128)(2,1)S(1)}, bf16[512,512]{1,0:T(8,128)(2,1)S(1)}, u32[]{:S(2)}, u32[]{:S(2)}) %collective-permute-start.20) | collective-permute-done | bytes 524320 | tf_op jit(solution)/shard_map/ppermute | solution.py:41
  79.9 2.9 %shard_map.57 = f32[1024,512]{1,0:T(8,128)} custom-call(f32[1024,512]{1,0:T(8,128)S(1)} %shard_map.56.early, bf16[1024,768]{1,0:T(8,128)(2,1)S(1)} %shard_map.53.turned, bf16[1024,768]{1,0:T(8,128)(2,1)S(1)} %collective-permute-done.14.theirs, bf16[512,512]{1,0:T(8,128)(2,1)S(1)} %collective-permute-done.20.refs_0_, ...), custom_call_target="tpu_custom_call" | custom-call | tf_op jit(solution)/shard_map/pallas_call | solution.py:60
  (40 shorter events, 7.4 us)
Async XLA Ops:
  0.6 40.5 %copy-start.1 = (bf16[256,1024]{1,0:T(8,128)(2,1)S(1)}, bf16[256,1024]{1,0:T(8,128)(2,1)}, u32[]{:S(2)}) copy-start(bf16[256,1024]{1,0:T(8,128)(2,1)} %refs_0_.4) | copy-start | bytes 1572868
  0.6 30.4 %collective-permute-start = (bf16[1024,512]{1,0:T(8,128)(2,1)}, bf16[1024,512]{1,0:T(8,128)(2,1)S(1)}, u32[]{:S(2)}, u32[]{:S(2)}) collective-permute-start(bf16[1024,512]{1,0:T(8,128)(2,1)} %refs_0_.3), channel_id=1, source_target_pairs={{8,0},{12,4},{0,8},{4,12},{24,16},{28,20},{16,24},{20,28},{9,1},{1... | collective-permute-start | bytes 3145736 | tf_op jit(solution)/shard_map/ppermute | solution.py:41
  3.6 27.4 %collective-permute-start.1 = (bf16[1024,512]{1,0:T(8,128)(2,1)}, bf16[1024,512]{1,0:T(8,128)(2,1)S(1)}, u32[]{:S(2)}, u32[]{:S(2)}) collective-permute-start(bf16[1024,512]{1,0:T(8,128)(2,1)} %refs_0_.3), channel_id=1, source_target_pairs={{16,0},{20,4},{24,8},{28,12},{0,16},{4,20},{8,24},{12,28},{17,1},{... | collective-permute-start | bytes 3145736 | tf_op jit(solution)/shard_map/ppermute | solution.py:41
  5.2 16.9 %collective-permute-start.3 = (bf16[256,1024]{1,0:T(8,128)(2,1)}, bf16[256,1024]{1,0:T(8,128)(2,1)S(1)}, u32[]{:S(2)}, u32[]{:S(2)}) collective-permute-start(bf16[256,1024]{1,0:T(8,128)(2,1)} %refs_0_.2), channel_id=1, source_target_pairs={{3,0},{0,1},{1,2},{2,3},{7,4},{4,5},{5,6},{6,7},{11,8},{8,9},{9,10... | collective-permute-start | bytes 1572872 | tf_op jit(solution)/shard_map/ppermute | solution.py:52
  6.7 24.3 %collective-permute-start.2 = (bf16[256,1024]{1,0:T(8,128)(2,1)}, bf16[256,1024]{1,0:T(8,128)(2,1)S(1)}, u32[]{:S(2)}, u32[]{:S(2)}) collective-permute-start(bf16[256,1024]{1,0:T(8,128)(2,1)} %refs_0_.2), channel_id=1, source_target_pairs={{1,0},{2,1},{3,2},{0,3},{5,4},{6,5},{7,6},{4,7},{9,8},{10,9},{11,1... | collective-permute-start | bytes 1572872 | tf_op jit(solution)/shard_map/ppermute | solution.py:52
  9.0 30.1 %collective-permute-start.12 = (bf16[256,1024]{1,0:T(8,128)(2,1)}, bf16[256,1024]{1,0:T(8,128)(2,1)S(1)}, u32[]{:S(2)}, u32[]{:S(2)}) collective-permute-start(bf16[256,1024]{1,0:T(8,128)(2,1)} %refs_0_.4), channel_id=1, source_target_pairs={{8,0},{12,4},{0,8},{4,12},{24,16},{28,20},{16,24},{20,28},{9,1},{1... | collective-permute-start | bytes 1572872 | tf_op jit(solution)/shard_map/ppermute | solution.py:41
  22.1 19.1 %collective-permute-start.13 = (bf16[256,1024]{1,0:T(8,128)(2,1)}, bf16[256,1024]{1,0:T(8,128)(2,1)S(1)}, u32[]{:S(2)}, u32[]{:S(2)}) collective-permute-start(bf16[256,1024]{1,0:T(8,128)(2,1)} %refs_0_.4), channel_id=1, source_target_pairs={{16,0},{20,4},{24,8},{28,12},{0,16},{4,20},{8,24},{12,28},{17,1},{... | collective-permute-start | bytes 1572872 | tf_op jit(solution)/shard_map/ppermute | solution.py:41
  31.0 15.0 %collective-permute-start.4 = (bf16[256,1024]{1,0:T(8,128)(2,1)S(1)}, bf16[256,1024]{1,0:T(8,128)(2,1)S(1)}, u32[]{:S(2)}, u32[]{:S(2)}) collective-permute-start(bf16[256,1024]{1,0:T(8,128)(2,1)S(1)} %collective-permute-done.3.refs_3_), channel_id=1, source_target_pairs={{3,0},{0,1},{1,2},{2,3},{7,4},{4,5},{5,6},{6,7},{11,8},{8,9},{9,10... | collective-permute-start | bytes 1572872 | tf_op jit(solution)/shard_map/ppermute | solution.py:52
  32.2 13.8 %copy-start.2 = (bf16[256,1024]{1,0:T(8,128)(2,1)S(1)}, bf16[256,1024]{1,0:T(8,128)(2,1)}, u32[]{:S(2)}) copy-start(bf16[256,1024]{1,0:T(8,128)(2,1)} %refs_0_.2) | copy-start | bytes 1572868
  32.2 17.2 %collective-permute-start.6 = (bf16[512,512]{1,0:T(8,128)(2,1)S(1)}, bf16[512,512]{1,0:T(8,128)(2,1)S(1)}, u32[]{:S(2)}, u32[]{:S(2)}) collective-permute-start(bf16[512,512]{1,0:T(8,128)(2,1)S(1)} %slice.25), channel_id=1, source_target_pairs={{8,0},{12,4},{0,8},{4,12},{24,16},{28,20},{16,24},{20,28},{9,1},{1... | collective-permute-start | bytes 1572872 | tf_op jit(solution)/shard_map/ppermute | solution.py:41
  32.8 18.1 %collective-permute-start.5 = (bf16[512,512]{1,0:T(8,128)(2,1)S(1)}, bf16[512,512]{1,0:T(8,128)(2,1)S(1)}, u32[]{:S(2)}, u32[]{:S(2)}) collective-permute-start(bf16[512,512]{1,0:T(8,128)(2,1)S(1)} %slice.24), channel_id=1, source_target_pairs={{16,0},{20,4},{24,8},{28,12},{0,16},{4,20},{8,24},{12,28},{17,1},{... | collective-permute-start | bytes 1572872 | tf_op jit(solution)/shard_map/ppermute | solution.py:41
  41.6 15.2 %collective-permute-start.14 = (bf16[1024,768]{1,0:T(8,128)(2,1)S(1)}, bf16[1024,768]{1,0:T(8,128)(2,1)S(1)}, u32[]{:S(2)}, u32[]{:S(2)}) collective-permute-start(bf16[1024,768]{1,0:T(8,128)(2,1)S(1)} %shard_map.53.turned), channel_id=1, source_target_pairs={{4,0},{0,4},{12,8},{8,12},{20,16},{16,20},{28,24},{24,28},{5,1},{1... | collective-permute-start | bytes 4718600 | tf_op jit(solution)/shard_map/ppermute | solution.py:41
  50.9 2.7 %collective-permute-start.7 = (bf16[4,256,512]{2,1,0:T(8,128)(2,1)S(1)}, bf16[4,256,512]{2,1,0:T(8,128)(2,1)S(1)}, u32[]{:S(2)}, u32[]{:S(2)}) collective-permute-start(bf16[4,256,512]{2,1,0:T(8,128)(2,1)S(1)} %get-tuple-element.24), channel_id=1, source_target_pairs={{4,0},{0,4},{12,8},{8,12},{20,16},{16,20},{28,24},{24,28},{5,1},{1... | collective-permute-start | bytes 3145736 | tf_op jit(solution)/shard_map/ppermute | solution.py:41
  51.0 8.8 %collective-permute-start.15 = (bf16[128,1024]{1,0:T(8,128)(2,1)S(1)}, bf16[128,1024]{1,0:T(8,128)(2,1)S(1)}, u32[]{:S(2)}, u32[]{:S(2)}) collective-permute-start(bf16[128,1024]{1,0:T(8,128)(2,1)S(1)} %slice.32), channel_id=1, source_target_pairs={{16,0},{20,4},{24,8},{28,12},{0,16},{4,20},{8,24},{12,28},{17,1},{... | collective-permute-start | bytes 786440 | tf_op jit(solution)/shard_map/ppermute | solution.py:41
  52.6 8.7 %collective-permute-start.16 = (bf16[128,1024]{1,0:T(8,128)(2,1)S(1)}, bf16[128,1024]{1,0:T(8,128)(2,1)S(1)}, u32[]{:S(2)}, u32[]{:S(2)}) collective-permute-start(bf16[128,1024]{1,0:T(8,128)(2,1)S(1)} %slice.33), channel_id=1, source_target_pairs={{8,0},{12,4},{0,8},{4,12},{24,16},{28,20},{16,24},{20,28},{9,1},{1... | collective-permute-start | bytes 786440 | tf_op jit(solution)/shard_map/ppermute | solution.py:41
  56.3 5.2 %collective-permute-start.8 = (f32[64,1024]{1,0:T(8,128)S(1)}, f32[64,1024]{1,0:T(8,128)S(1)}, u32[]{:S(2)}, u32[]{:S(2)}) collective-permute-start(f32[64,1024]{1,0:T(8,128)S(1)} %get-tuple-element.32), channel_id=1, source_target_pairs={{4,0},{0,4},{12,8},{8,12},{20,16},{16,20},{28,24},{24,28},{5,1},{1... | collective-permute-start | bytes 786440 | tf_op jit(solution)/shard_map/ppermute | solution.py:41
  56.5 5.5 %collective-permute-start.11 = (f32[64,1024]{1,0:T(8,128)S(1)}, f32[64,1024]{1,0:T(8,128)S(1)}, u32[]{:S(2)}, u32[]{:S(2)}) collective-permute-start(f32[64,1024]{1,0:T(8,128)S(1)} %get-tuple-element.33), channel_id=1, source_target_pairs={{4,0},{0,4},{12,8},{8,12},{20,16},{16,20},{28,24},{24,28},{5,1},{1... | collective-permute-start | bytes 786440 | tf_op jit(solution)/shard_map/ppermute | solution.py:41
  56.9 6.7 %collective-permute-start.10 = (f32[64,1024]{1,0:T(8,128)S(1)}, f32[64,1024]{1,0:T(8,128)S(1)}, u32[]{:S(2)}, u32[]{:S(2)}) collective-permute-start(f32[64,1024]{1,0:T(8,128)S(1)} %get-tuple-element.34), channel_id=1, source_target_pairs={{4,0},{0,4},{12,8},{8,12},{20,16},{16,20},{28,24},{24,28},{5,1},{1... | collective-permute-start | bytes 786440 | tf_op jit(solution)/shard_map/ppermute | solution.py:41
  59.8 10.1 %collective-permute-start.18 = (bf16[256,512]{1,0:T(8,128)(2,1)S(1)}, bf16[256,512]{1,0:T(8,128)(2,1)S(1)}, u32[]{:S(2)}, u32[]{:S(2)}) collective-permute-start(bf16[256,512]{1,0:T(8,128)(2,1)S(1)} %get-tuple-element.29), channel_id=1, source_target_pairs={{24,0},{28,4},{16,8},{20,12},{8,16},{12,20},{0,24},{4,28},{25,1},{... | collective-permute-start | bytes 786440 | tf_op jit(solution)/shard_map/ppermute | solution.py:41
  61.2 10.2 %collective-permute-start.9 = (f32[64,1024]{1,0:T(8,128)S(1)}, f32[64,1024]{1,0:T(8,128)S(1)}, u32[]{:S(2)}, u32[]{:S(2)}) collective-permute-start(f32[64,1024]{1,0:T(8,128)S(1)} %get-tuple-element.35), channel_id=1, source_target_pairs={{4,0},{0,4},{12,8},{8,12},{20,16},{16,20},{28,24},{24,28},{5,1},{1... | collective-permute-start | bytes 786440 | tf_op jit(solution)/shard_map/ppermute | solution.py:41
  61.5 10.9 %collective-permute-start.17 = (bf16[1024,256]{1,0:T(8,128)(2,1)S(1)}, bf16[1024,256]{1,0:T(8,128)(2,1)S(1)}, u32[]{:S(2)}, u32[]{:S(2)}) collective-permute-start(bf16[1024,256]{1,0:T(8,128)(2,1)S(1)} %shard_map.54.far), channel_id=1, source_target_pairs={{4,0},{0,4},{12,8},{8,12},{20,16},{16,20},{28,24},{24,28},{5,1},{1... | collective-permute-start | bytes 1572872 | tf_op jit(solution)/shard_map/ppermute | solution.py:41
  62.0 17.9 %collective-permute-start.20 = (bf16[512,512]{1,0:T(8,128)(2,1)S(1)}, bf16[512,512]{1,0:T(8,128)(2,1)S(1)}, u32[]{:S(2)}, u32[]{:S(2)}) collective-permute-start(bf16[512,512]{1,0:T(8,128)(2,1)S(1)} %get-tuple-element.30), channel_id=1, source_target_pairs={{8,0},{12,4},{0,8},{4,12},{24,16},{28,20},{16,24},{20,28},{9,1},{1... | collective-permute-start | bytes 1572872 | tf_op jit(solution)/shard_map/ppermute | solution.py:41
  63.5 16.4 %collective-permute-start.21 = (bf16[512,512]{1,0:T(8,128)(2,1)S(1)}, bf16[512,512]{1,0:T(8,128)(2,1)S(1)}, u32[]{:S(2)}, u32[]{:S(2)}) collective-permute-start(bf16[512,512]{1,0:T(8,128)(2,1)S(1)} %get-tuple-element.31), channel_id=1, source_target_pairs={{16,0},{20,4},{24,8},{28,12},{0,16},{4,20},{8,24},{12,28},{17,1},{... | collective-permute-start | bytes 1572872 | tf_op jit(solution)/shard_map/ppermute | solution.py:41
  69.9 6.4 %collective-permute-start.19 = (bf16[256,512]{1,0:T(8,128)(2,1)S(1)}, bf16[256,512]{1,0:T(8,128)(2,1)S(1)}, u32[]{:S(2)}, u32[]{:S(2)}) collective-permute-start(bf16[256,512]{1,0:T(8,128)(2,1)S(1)} %collective-permute-done.18.refs_0_), channel_id=1, source_target_pairs={{1,0},{0,1},{3,2},{2,3},{5,4},{4,5},{7,6},{6,7},{9,8},{8,9},{11,10... | collective-permute-start | bytes 786440 | tf_op jit(solution)/shard_map/ppermute | solution.py:219
  (1 other events, 12.0 us)

commit v6 on v5

--- a/solution.py
+++ b/solution.py
@@ -56,16 +56,15 @@
     return lax.optimization_barrier((arrays, done))[0]
 
 
-def call(kernel, out, *args, scratch=(), grid=None, in_specs=None, out_specs=None, vmem=40):
+def call(kernel, out, *args, scratch=(), out_specs=None):
     return pl.pallas_call(
         kernel,
         out_shape=out,
-        in_specs=in_specs or [VMEM] * len(args),
+        in_specs=[VMEM] * len(args),
         out_specs=out_specs or jax.tree.map(lambda _: VMEM, out),
         scratch_shapes=scratch,
-        compiler_params=pltpu.CompilerParams(vmem_limit_bytes=vmem * 2**20),
+        compiler_params=pltpu.CompilerParams(vmem_limit_bytes=40 * 2**20),
         cost_estimate=pl.CostEstimate(flops=0, bytes_accessed=0, transcendentals=0),
-        **({"grid": grid} if grid else {}),
     )(*args)
 
 
@@ -148,6 +147,10 @@
         others[:, side] = total[s.tokens :]
 
 
+def blocks_of(rows):
+    return [slice(i * rows // 4, (i + 1) * rows // 4) for i in range(4)]
+
+
 def early_kernel(s, turned, theirs, far, far_theirs, mine, other, *refs):
     *blocks, out, packed = refs
     n = 1 + len(blocks) // 2
@@ -155,18 +158,25 @@
     packed[n * s.tokens : (n + 1) * s.tokens] = other[chip_at(0, 0)]
     for k in range(1, n):
         put(s, packed, k, n, *blocks[2 * k - 2 : 2 * k])
-    left = [turned[:, : s.tokens], far[...], theirs[:, : s.tokens], far_theirs[...]]
-    out[...] = jnp.dot(jnp.concatenate(left, axis=1), packed[...], preferred_element_type=F32)
+    for rows in blocks_of(s.taken):
+        left = [turned[rows, : s.tokens], far[rows], theirs[rows, : s.tokens], far_theirs[rows]]
+        out[rows] = jnp.dot(jnp.concatenate(left, axis=1), packed[...], preferred_element_type=F32)
 
 
 def late_kernel(s, scale, early, turned, theirs, *refs):
-    *blocks, out, packed = refs
+    *blocks, out, packed, sums, sems = refs
     n = len(blocks)
     for k, block in enumerate(blocks):
         packed[k * s.tokens : (k + 1) * s.tokens] = block[: s.tokens]
         packed[(n + k) * s.tokens : (n + k + 1) * s.tokens] = block[s.tokens :]
-    left = jnp.concatenate([turned[:, s.tokens :], theirs[:, s.tokens :]], axis=1)
-    out[...] = (early[...] + jnp.dot(left, packed[...], preferred_element_type=F32)) * scale
+    copies = []
+    for i, rows in enumerate(blocks_of(s.taken)):
+        left = jnp.concatenate([turned[rows, s.tokens :], theirs[rows, s.tokens :]], axis=1)
+        sums[rows] = (early[rows] + jnp.dot(left, packed[...], preferred_element_type=F32)) * scale
+        copies.append(pltpu.make_async_copy(sums.at[rows], out.at[rows], sems.at[i]))
+        copies[-1].start()
+    for copy in copies:
+        copy.wait()
 
 
 def body(context, grad_out, out_weight):
@@ -226,22 +236,20 @@
     own, others = call(functools.partial(context_far_kernel, s), [half_sums] * 2, mine, theirs, sums, *weights_far)
     context_grad = (own + sibling(others, (0.25, 0.5, 0.75))).astype(BF16)
 
-    def by_rows(x):
-        return pl.BlockSpec((s.taken // 4, x.shape[1]), lambda i: (i, 0))
-
     result = shape(s.taken, s.width, dtype=F32)
-    lefts = [turned, turned_other, turned_far, turned_far_other]
-    rights = [mine, theirs, *[x for two in far for x in two]]
     early = call(
-        functools.partial(early_kernel, s), result, *lefts, *rights,
-        grid=(4,), in_specs=[by_rows(x) for x in lefts] + [VMEM] * len(rights), out_specs=by_rows(result),
+        functools.partial(early_kernel, s), result,
+        turned, turned_other, turned_far, turned_far_other, mine, theirs, *[x for two in far for x in two],
         scratch=[pltpu.VMEM((2 * (1 + len(far)) * s.tokens, s.width), BF16)],
     )
-    lefts = [early, turned, turned_other]
     weight_grad = call(
-        functools.partial(late_kernel, s, scale), result, *lefts, *blocks,
-        grid=(4,), in_specs=[by_rows(x) for x in lefts] + [VMEM] * len(blocks), out_specs=by_rows(result),
-        scratch=[pltpu.VMEM((2 * len(blocks) * s.tokens, s.width), BF16)],
+        functools.partial(late_kernel, s, scale), result, early, turned, turned_other, *blocks,
+        out_specs=pl.BlockSpec(memory_space=pl.ANY),
+        scratch=[
+            pltpu.VMEM((2 * len(blocks) * s.tokens, s.width), BF16),
+            pltpu.VMEM((s.taken, s.width), F32),
+            pltpu.SemaphoreType.DMA((4,)),
+        ],
     )
     return (context_grad, weight_grad)
 

time: 83 us -> 82.2 us (level)
  Pallas kernels: 8.37 us -> 6.96 us
    pallas_call x8, Pallas kernels: 8.37 us -> 6.96 us  [call(): pl.pallas_call(kernel, out_shape=out, in_specs=[VMEM] * len(args), out_sp...]
  transfers between devices with their start and end apart: 22 -> 22, of which waited for: 12 -> 12; matrix products, arithmetic and copies ran while one was open for 1% -> 1% of each run, Pallas kernels for 7% -> 6%
where the time goes in v6:
time: 82.2 us; the launch traced here: 82 us
  waiting for transfers between devices  52.5 us (64%)
  starting transfers between devices  20.6 us (25%)
  Pallas kernels  6.96 us (8%)
  other arithmetic  0.93 us (1%)
    ppermute x3, waiting for transfers between devices, along_node(): lax.ppermute(array, 'node', [((i + d) % node, i) for i in range(node)])  25.2 us
    ppermute x18, waiting for transfers between devices, shift(): lax.ppermute(array, 'outer', [(place(o, db, da, dc), o) for o in range(la...  23.4 us
    ppermute x18, starting transfers between devices, shift(): lax.ppermute(array, 'outer', [(place(o, db, da, dc), o) for o in range(la...  14.1 us
    pallas_call x8, Pallas kernels, call(): pl.pallas_call(kernel, out_shape=out, in_specs=[VMEM] * len(args), out_sp...  6.96 us
    ppermute x3, starting transfers between devices, along_node(): lax.ppermute(array, 'node', [((i + d) % node, i) for i in range(node)])  4.95 us
    ppermute x1, waiting for transfers between devices, body(): lax.ppermute(x, 'node', [(i ^ 1, i) for i in range(s.node)])  3.86 us
  transfers between devices with their start and end apart: 22, of which 12 were waited for; matrix products, arithmetic and copies ran while one was open for 1% of the time, Pallas kernels for 6%

profile of v6, /device:TPU:0, one launch (start us, length us, event | category | flops | bytes accessed | tf_op | source)
XLA Modules:
  0.0 82.0 jit_solution(7163985342221275793)
XLA Ops:
  0.6 3.0 %collective-permute-start = (bf16[1024,512]{1,0:T(8,128)(2,1)}, bf16[1024,512]{1,0:T(8,128)(2,1)S(1)}, u32[]{:S(2)}, u32[]{:S(2)}) collective-permute-start(bf16[1024,512]{1,0:T(8,128)(2,1)} %refs_0_.3), channel_id=1, source_target_pairs={{8,0},{12,4},{0,8},{4,12},{24,16},{28,20},{16,24},{20,28},{9,1},{1... | collective-permute-start | bytes 3145736 | tf_op jit(solution)/shard_map/ppermute | solution.py:41
  3.6 1.5 %collective-permute-start.1 = (bf16[1024,512]{1,0:T(8,128)(2,1)}, bf16[1024,512]{1,0:T(8,128)(2,1)S(1)}, u32[]{:S(2)}, u32[]{:S(2)}) collective-permute-start(bf16[1024,512]{1,0:T(8,128)(2,1)} %refs_0_.3), channel_id=1, source_target_pairs={{16,0},{20,4},{24,8},{28,12},{0,16},{4,20},{8,24},{12,28},{17,1},{... | collective-permute-start | bytes 3145736 | tf_op jit(solution)/shard_map/ppermute | solution.py:41
  5.2 1.6 %collective-permute-start.3 = (bf16[256,1024]{1,0:T(8,128)(2,1)}, bf16[256,1024]{1,0:T(8,128)(2,1)S(1)}, u32[]{:S(2)}, u32[]{:S(2)}) collective-permute-start(bf16[256,1024]{1,0:T(8,128)(2,1)} %refs_0_.2), channel_id=1, source_target_pairs={{3,0},{0,1},{1,2},{2,3},{7,4},{4,5},{5,6},{6,7},{11,8},{8,9},{9,10... | collective-permute-start | bytes 1572872 | tf_op jit(solution)/shard_map/ppermute | solution.py:52
  6.7 2.2 %collective-permute-start.2 = (bf16[256,1024]{1,0:T(8,128)(2,1)}, bf16[256,1024]{1,0:T(8,128)(2,1)S(1)}, u32[]{:S(2)}, u32[]{:S(2)}) collective-permute-start(bf16[256,1024]{1,0:T(8,128)(2,1)} %refs_0_.2), channel_id=1, source_target_pairs={{1,0},{2,1},{3,2},{0,3},{5,4},{6,5},{7,6},{4,7},{9,8},{10,9},{11,1... | collective-permute-start | bytes 1572872 | tf_op jit(solution)/shard_map/ppermute | solution.py:52
  9.5 12.6 %collective-permute-done.3.refs_3_ = bf16[256,1024]{1,0:T(8,128)(2,1)S(1)} collective-permute-done((bf16[256,1024]{1,0:T(8,128)(2,1)}, bf16[256,1024]{1,0:T(8,128)(2,1)S(1)}, u32[]{:S(2)}, u32[]{:S(2)}) %collective-permute-start.3) | collective-permute-done | bytes 524320 | tf_op jit(solution)/shard_map/ppermute | solution.py:52
  22.6 8.4 %collective-permute-done.2.refs_1_ = bf16[256,1024]{1,0:T(8,128)(2,1)S(1)} collective-permute-done((bf16[256,1024]{1,0:T(8,128)(2,1)}, bf16[256,1024]{1,0:T(8,128)(2,1)S(1)}, u32[]{:S(2)}, u32[]{:S(2)}) %collective-permute-start.2) | collective-permute-done | bytes 524320 | tf_op jit(solution)/shard_map/ppermute | solution.py:52
  31.0 1.1 %collective-permute-start.4 = (bf16[256,1024]{1,0:T(8,128)(2,1)S(1)}, bf16[256,1024]{1,0:T(8,128)(2,1)S(1)}, u32[]{:S(2)}, u32[]{:S(2)}) collective-permute-start(bf16[256,1024]{1,0:T(8,128)(2,1)S(1)} %collective-permute-done.3.refs_3_), channel_id=1, source_target_pairs={{3,0},{0,1},{1,2},{2,3},{7,4},{4,5},{5,6},{6,7},{11,8},{8,9},{9,10... | collective-permute-start | bytes 1572872 | tf_op jit(solution)/shard_map/ppermute | solution.py:52
  33.7 5.3 %collective-permute-done.12.refs_1_ = bf16[256,1024]{1,0:T(8,128)(2,1)S(1)} collective-permute-done((bf16[256,1024]{1,0:T(8,128)(2,1)}, bf16[256,1024]{1,0:T(8,128)(2,1)S(1)}, u32[]{:S(2)}, u32[]{:S(2)}) %collective-permute-start.12) | collective-permute-done | bytes 524320 | tf_op jit(solution)/shard_map/ppermute | solution.py:41
  39.1 2.1 %collective-permute-done.13.refs_2_ = bf16[256,1024]{1,0:T(8,128)(2,1)S(1)} collective-permute-done((bf16[256,1024]{1,0:T(8,128)(2,1)}, bf16[256,1024]{1,0:T(8,128)(2,1)S(1)}, u32[]{:S(2)}, u32[]{:S(2)}) %collective-permute-start.13) | collective-permute-done | bytes 524320 | tf_op jit(solution)/shard_map/ppermute | solution.py:41
  41.7 4.3 %collective-permute-done.4.refs_2_ = bf16[256,1024]{1,0:T(8,128)(2,1)S(1)} collective-permute-done((bf16[256,1024]{1,0:T(8,128)(2,1)S(1)}, bf16[256,1024]{1,0:T(8,128)(2,1)S(1)}, u32[]{:S(2)}, u32[]{:S(2)}) %collective-permute-start.4) | collective-permute-done | bytes 524320 | tf_op jit(solution)/shard_map/ppermute | solution.py:52
  46.3 3.2 %collective-permute-done.6.refs_1_ = bf16[512,512]{1,0:T(8,128)(2,1)S(1)} collective-permute-done((bf16[512,512]{1,0:T(8,128)(2,1)S(1)}, bf16[512,512]{1,0:T(8,128)(2,1)S(1)}, u32[]{:S(2)}, u32[]{:S(2)}) %collective-permute-start.6) | collective-permute-done | bytes 524320 | tf_op jit(solution)/shard_map/ppermute | solution.py:41
  49.5 1.5 %collective-permute-done.5.refs_0_ = bf16[512,512]{1,0:T(8,128)(2,1)S(1)} collective-permute-done((bf16[512,512]{1,0:T(8,128)(2,1)S(1)}, bf16[512,512]{1,0:T(8,128)(2,1)S(1)}, u32[]{:S(2)}, u32[]{:S(2)}) %collective-permute-start.5) | collective-permute-done | bytes 524320 | tf_op jit(solution)/shard_map/ppermute | solution.py:41
  51.0 1.6 %collective-permute-start.15 = (bf16[128,1024]{1,0:T(8,128)(2,1)S(1)}, bf16[128,1024]{1,0:T(8,128)(2,1)S(1)}, u32[]{:S(2)}, u32[]{:S(2)}) collective-permute-start(bf16[128,1024]{1,0:T(8,128)(2,1)S(1)} %slice.32), channel_id=1, source_target_pairs={{16,0},{20,4},{24,8},{28,12},{0,16},{4,20},{8,24},{12,28},{17,1},{... | collective-permute-start | bytes 786440 | tf_op jit(solution)/shard_map/ppermute | solution.py:41
  53.6 1.8 %shard_map.51.near = f32[512,1024]{1,0:T(8,128)S(1)} custom-call(bf16[4,256,512]{2,1,0:T(8,128)(2,1)S(1)} %get-tuple-element.20.mine, bf16[4,256,512]{2,1,0:T(8,128)(2,1)S(1)} %collective-permute-done.7.theirs.other, bf16[1024,512]{1,0:T(8,128)(2,1)S(1)} %copy-done, bf16[1024,512]{1,0:T(8,128)(2,1)S(1)} %collective-permute-done.refs_1_, ...), custom_call_target="tpu_custom_call" | custom-call | tf_op jit(solution)/shard_map/pallas_call | solution.py:60
  57.1 2.7 %collective-permute-done.15.refs_0_ = bf16[128,1024]{1,0:T(8,128)(2,1)S(1)} collective-permute-done((bf16[128,1024]{1,0:T(8,128)(2,1)S(1)}, bf16[128,1024]{1,0:T(8,128)(2,1)S(1)}, u32[]{:S(2)}, u32[]{:S(2)}) %collective-permute-start.15) | collective-permute-done | bytes 262176 | tf_op jit(solution)/shard_map/ppermute | solution.py:41
  59.8 1.5 %collective-permute-start.18 = (bf16[256,512]{1,0:T(8,128)(2,1)S(1)}, bf16[256,512]{1,0:T(8,128)(2,1)S(1)}, u32[]{:S(2)}, u32[]{:S(2)}) collective-permute-start(bf16[256,512]{1,0:T(8,128)(2,1)S(1)} %get-tuple-element.29), channel_id=1, source_target_pairs={{24,0},{28,4},{16,8},{20,12},{8,16},{12,20},{0,24},{4,28},{25,1},{... | collective-permute-start | bytes 786440 | tf_op jit(solution)/shard_map/ppermute | solution.py:41
  62.0 1.5 %collective-permute-start.20 = (bf16[512,512]{1,0:T(8,128)(2,1)S(1)}, bf16[512,512]{1,0:T(8,128)(2,1)S(1)}, u32[]{:S(2)}, u32[]{:S(2)}) collective-permute-start(bf16[512,512]{1,0:T(8,128)(2,1)S(1)} %get-tuple-element.30), channel_id=1, source_target_pairs={{8,0},{12,4},{0,8},{4,12},{24,16},{28,20},{16,24},{20,28},{9,1},{1... | collective-permute-start | bytes 1572872 | tf_op jit(solution)/shard_map/ppermute | solution.py:41
  64.0 5.8 %collective-permute-done.18.refs_0_ = bf16[256,512]{1,0:T(8,128)(2,1)S(1)} collective-permute-done((bf16[256,512]{1,0:T(8,128)(2,1)S(1)}, bf16[256,512]{1,0:T(8,128)(2,1)S(1)}, u32[]{:S(2)}, u32[]{:S(2)}) %collective-permute-start.18) | collective-permute-done | bytes 262176 | tf_op jit(solution)/shard_map/ppermute | solution.py:41
  69.9 1.6 %collective-permute-start.19 = (bf16[256,512]{1,0:T(8,128)(2,1)S(1)}, bf16[256,512]{1,0:T(8,128)(2,1)S(1)}, u32[]{:S(2)}, u32[]{:S(2)}) collective-permute-start(bf16[256,512]{1,0:T(8,128)(2,1)S(1)} %collective-permute-done.18.refs_0_), channel_id=1, source_target_pairs={{1,0},{0,1},{3,2},{2,3},{5,4},{4,5},{7,6},{6,7},{9,8},{8,9},{11,10... | collective-permute-start | bytes 786440 | tf_op jit(solution)/shard_map/ppermute | solution.py:229
  71.4 0.9 %fusion = bf16[256,1024]{1,0:T(8,128)(2,1)} fusion(f32[256,1024]{1,0:T(8,128)S(1)} %get-tuple-element.25, f32[64,1024]{1,0:T(8,128)S(1)} %collective-permute-done.11, f32[64,1024]{1,0:T(8,128)S(1)} %collective-permute-done.10, f32[64,1024]{1,0:T(8,128)S(1)} %collective-permute-done.9, f32[64,1024]{1,0:T(8,128)S(1)} %collective-permute-done.8), kind=kLoop, calls=%fused_computation.1 | loop fusion | flops 1310720 | bytes 2621440 | tf_op jit(solution)/shard_map/convert_element_type | solution.py:237
  72.4 3.9 %collective-permute-done.19.refs_1_ = bf16[256,512]{1,0:T(8,128)(2,1)S(1)} collective-permute-done((bf16[256,512]{1,0:T(8,128)(2,1)S(1)}, bf16[256,512]{1,0:T(8,128)(2,1)S(1)}, u32[]{:S(2)}, u32[]{:S(2)}) %collective-permute-start.19) | collective-permute-done | bytes 262176 | tf_op jit(solution)/shard_map/ppermute | solution.py:229
  76.2 1.3 %shard_map.56.early = f32[1024,512]{1,0:T(8,128)S(1)} custom-call(bf16[1024,768]{1,0:T(8,128)(2,1)S(1)} %shard_map.53.turned, bf16[1024,768]{1,0:T(8,128)(2,1)S(1)} %collective-permute-done.14.theirs, bf16[1024,256]{1,0:T(8,128)(2,1)S(1)} %shard_map.54.far, bf16[1024,256]{1,0:T(8,128)(2,1)S(1)} %collective-permute-done.17.far_theirs, ...), custom_call_target="tpu_custom_call" | custom-call | tf_op jit(solution)/shard_map/pallas_call | solution.py:60
  77.5 2.4 %collective-permute-done.20.refs_0_ = bf16[512,512]{1,0:T(8,128)(2,1)S(1)} collective-permute-done((bf16[512,512]{1,0:T(8,128)(2,1)S(1)}, bf16[512,512]{1,0:T(8,128)(2,1)S(1)}, u32[]{:S(2)}, u32[]{:S(2)}) %collective-permute-start.20) | collective-permute-done | bytes 524320 | tf_op jit(solution)/shard_map/ppermute | solution.py:41
  79.9 2.1 %shard_map.57 = f32[1024,512]{1,0:T(8,128)} custom-call(f32[1024,512]{1,0:T(8,128)S(1)} %shard_map.56.early, bf16[1024,768]{1,0:T(8,128)(2,1)S(1)} %shard_map.53.turned, bf16[1024,768]{1,0:T(8,128)(2,1)S(1)} %collective-permute-done.14.theirs, bf16[512,512]{1,0:T(8,128)(2,1)S(1)} %collective-permute-done.20.refs_0_, ...), custom_call_target="tpu_custom_call" | custom-call | tf_op jit(solution)/shard_map/pallas_call | solution.py:60
  (40 shorter events, 7.4 us)
Async XLA Ops:
  0.6 40.5 %copy-start.1 = (bf16[256,1024]{1,0:T(8,128)(2,1)S(1)}, bf16[256,1024]{1,0:T(8,128)(2,1)}, u32[]{:S(2)}) copy-start(bf16[256,1024]{1,0:T(8,128)(2,1)} %refs_0_.4) | copy-start | bytes 1572868
  0.6 30.4 %collective-permute-start = (bf16[1024,512]{1,0:T(8,128)(2,1)}, bf16[1024,512]{1,0:T(8,128)(2,1)S(1)}, u32[]{:S(2)}, u32[]{:S(2)}) collective-permute-start(bf16[1024,512]{1,0:T(8,128)(2,1)} %refs_0_.3), channel_id=1, source_target_pairs={{8,0},{12,4},{0,8},{4,12},{24,16},{28,20},{16,24},{20,28},{9,1},{1... | collective-permute-start | bytes 3145736 | tf_op jit(solution)/shard_map/ppermute | solution.py:41
  3.6 27.4 %collective-permute-start.1 = (bf16[1024,512]{1,0:T(8,128)(2,1)}, bf16[1024,512]{1,0:T(8,128)(2,1)S(1)}, u32[]{:S(2)}, u32[]{:S(2)}) collective-permute-start(bf16[1024,512]{1,0:T(8,128)(2,1)} %refs_0_.3), channel_id=1, source_target_pairs={{16,0},{20,4},{24,8},{28,12},{0,16},{4,20},{8,24},{12,28},{17,1},{... | collective-permute-start | bytes 3145736 | tf_op jit(solution)/shard_map/ppermute | solution.py:41
  5.2 16.9 %collective-permute-start.3 = (bf16[256,1024]{1,0:T(8,128)(2,1)}, bf16[256,1024]{1,0:T(8,128)(2,1)S(1)}, u32[]{:S(2)}, u32[]{:S(2)}) collective-permute-start(bf16[256,1024]{1,0:T(8,128)(2,1)} %refs_0_.2), channel_id=1, source_target_pairs={{3,0},{0,1},{1,2},{2,3},{7,4},{4,5},{5,6},{6,7},{11,8},{8,9},{9,10... | collective-permute-start | bytes 1572872 | tf_op jit(solution)/shard_map/ppermute | solution.py:52
  6.7 24.3 %collective-permute-start.2 = (bf16[256,1024]{1,0:T(8,128)(2,1)}, bf16[256,1024]{1,0:T(8,128)(2,1)S(1)}, u32[]{:S(2)}, u32[]{:S(2)}) collective-permute-start(bf16[256,1024]{1,0:T(8,128)(2,1)} %refs_0_.2), channel_id=1, source_target_pairs={{1,0},{2,1},{3,2},{0,3},{5,4},{6,5},{7,6},{4,7},{9,8},{10,9},{11,1... | collective-permute-start | bytes 1572872 | tf_op jit(solution)/shard_map/ppermute | solution.py:52
  9.0 30.1 %collective-permute-start.12 = (bf16[256,1024]{1,0:T(8,128)(2,1)}, bf16[256,1024]{1,0:T(8,128)(2,1)S(1)}, u32[]{:S(2)}, u32[]{:S(2)}) collective-permute-start(bf16[256,1024]{1,0:T(8,128)(2,1)} %refs_0_.4), channel_id=1, source_target_pairs={{8,0},{12,4},{0,8},{4,12},{24,16},{28,20},{16,24},{20,28},{9,1},{1... | collective-permute-start | bytes 1572872 | tf_op jit(solution)/shard_map/ppermute | solution.py:41
  22.1 19.1 %collective-permute-start.13 = (bf16[256,1024]{1,0:T(8,128)(2,1)}, bf16[256,1024]{1,0:T(8,128)(2,1)S(1)}, u32[]{:S(2)}, u32[]{:S(2)}) collective-permute-start(bf16[256,1024]{1,0:T(8,128)(2,1)} %refs_0_.4), channel_id=1, source_target_pairs={{16,0},{20,4},{24,8},{28,12},{0,16},{4,20},{8,24},{12,28},{17,1},{... | collective-permute-start | bytes 1572872 | tf_op jit(solution)/shard_map/ppermute | solution.py:41
  31.0 15.0 %collective-permute-start.4 = (bf16[256,1024]{1,0:T(8,128)(2,1)S(1)}, bf16[256,1024]{1,0:T(8,128)(2,1)S(1)}, u32[]{:S(2)}, u32[]{:S(2)}) collective-permute-start(bf16[256,1024]{1,0:T(8,128)(2,1)S(1)} %collective-permute-done.3.refs_3_), channel_id=1, source_target_pairs={{3,0},{0,1},{1,2},{2,3},{7,4},{4,5},{5,6},{6,7},{11,8},{8,9},{9,10... | collective-permute-start | bytes 1572872 | tf_op jit(solution)/shard_map/ppermute | solution.py:52
  32.2 13.8 %copy-start.2 = (bf16[256,1024]{1,0:T(8,128)(2,1)S(1)}, bf16[256,1024]{1,0:T(8,128)(2,1)}, u32[]{:S(2)}) copy-start(bf16[256,1024]{1,0:T(8,128)(2,1)} %refs_0_.2) | copy-start | bytes 1572868
  32.2 17.2 %collective-permute-start.6 = (bf16[512,512]{1,0:T(8,128)(2,1)S(1)}, bf16[512,512]{1,0:T(8,128)(2,1)S(1)}, u32[]{:S(2)}, u32[]{:S(2)}) collective-permute-start(bf16[512,512]{1,0:T(8,128)(2,1)S(1)} %slice.25), channel_id=1, source_target_pairs={{8,0},{12,4},{0,8},{4,12},{24,16},{28,20},{16,24},{20,28},{9,1},{1... | collective-permute-start | bytes 1572872 | tf_op jit(solution)/shard_map/ppermute | solution.py:41
  32.8 18.1 %collective-permute-start.5 = (bf16[512,512]{1,0:T(8,128)(2,1)S(1)}, bf16[512,512]{1,0:T(8,128)(2,1)S(1)}, u32[]{:S(2)}, u32[]{:S(2)}) collective-permute-start(bf16[512,512]{1,0:T(8,128)(2,1)S(1)} %slice.24), channel_id=1, source_target_pairs={{16,0},{20,4},{24,8},{28,12},{0,16},{4,20},{8,24},{12,28},{17,1},{... | collective-permute-start | bytes 1572872 | tf_op jit(solution)/shard_map/ppermute | solution.py:41
  41.6 15.2 %collective-permute-start.14 = (bf16[1024,768]{1,0:T(8,128)(2,1)S(1)}, bf16[1024,768]{1,0:T(8,128)(2,1)S(1)}, u32[]{:S(2)}, u32[]{:S(2)}) collective-permute-start(bf16[1024,768]{1,0:T(8,128)(2,1)S(1)} %shard_map.53.turned), channel_id=1, source_target_pairs={{4,0},{0,4},{12,8},{8,12},{20,16},{16,20},{28,24},{24,28},{5,1},{1... | collective-permute-start | bytes 4718600 | tf_op jit(solution)/shard_map/ppermute | solution.py:41
  50.9 2.7 %collective-permute-start.7 = (bf16[4,256,512]{2,1,0:T(8,128)(2,1)S(1)}, bf16[4,256,512]{2,1,0:T(8,128)(2,1)S(1)}, u32[]{:S(2)}, u32[]{:S(2)}) collective-permute-start(bf16[4,256,512]{2,1,0:T(8,128)(2,1)S(1)} %get-tuple-element.24), channel_id=1, source_target_pairs={{4,0},{0,4},{12,8},{8,12},{20,16},{16,20},{28,24},{24,28},{5,1},{1... | collective-permute-start | bytes 3145736 | tf_op jit(solution)/shard_map/ppermute | solution.py:41
  51.0 8.8 %collective-permute-start.15 = (bf16[128,1024]{1,0:T(8,128)(2,1)S(1)}, bf16[128,1024]{1,0:T(8,128)(2,1)S(1)}, u32[]{:S(2)}, u32[]{:S(2)}) collective-permute-start(bf16[128,1024]{1,0:T(8,128)(2,1)S(1)} %slice.32), channel_id=1, source_target_pairs={{16,0},{20,4},{24,8},{28,12},{0,16},{4,20},{8,24},{12,28},{17,1},{... | collective-permute-start | bytes 786440 | tf_op jit(solution)/shard_map/ppermute | solution.py:41
  52.6 8.7 %collective-permute-start.16 = (bf16[128,1024]{1,0:T(8,128)(2,1)S(1)}, bf16[128,1024]{1,0:T(8,128)(2,1)S(1)}, u32[]{:S(2)}, u32[]{:S(2)}) collective-permute-start(bf16[128,1024]{1,0:T(8,128)(2,1)S(1)} %slice.33), channel_id=1, source_target_pairs={{8,0},{12,4},{0,8},{4,12},{24,16},{28,20},{16,24},{20,28},{9,1},{1... | collective-permute-start | bytes 786440 | tf_op jit(solution)/shard_map/ppermute | solution.py:41
  56.3 5.2 %collective-permute-start.8 = (f32[64,1024]{1,0:T(8,128)S(1)}, f32[64,1024]{1,0:T(8,128)S(1)}, u32[]{:S(2)}, u32[]{:S(2)}) collective-permute-start(f32[64,1024]{1,0:T(8,128)S(1)} %get-tuple-element.32), channel_id=1, source_target_pairs={{4,0},{0,4},{12,8},{8,12},{20,16},{16,20},{28,24},{24,28},{5,1},{1... | collective-permute-start | bytes 786440 | tf_op jit(solution)/shard_map/ppermute | solution.py:41
  56.5 5.5 %collective-permute-start.11 = (f32[64,1024]{1,0:T(8,128)S(1)}, f32[64,1024]{1,0:T(8,128)S(1)}, u32[]{:S(2)}, u32[]{:S(2)}) collective-permute-start(f32[64,1024]{1,0:T(8,128)S(1)} %get-tuple-element.33), channel_id=1, source_target_pairs={{4,0},{0,4},{12,8},{8,12},{20,16},{16,20},{28,24},{24,28},{5,1},{1... | collective-permute-start | bytes 786440 | tf_op jit(solution)/shard_map/ppermute | solution.py:41
  56.9 6.7 %collective-permute-start.10 = (f32[64,1024]{1,0:T(8,128)S(1)}, f32[64,1024]{1,0:T(8,128)S(1)}, u32[]{:S(2)}, u32[]{:S(2)}) collective-permute-start(f32[64,1024]{1,0:T(8,128)S(1)} %get-tuple-element.34), channel_id=1, source_target_pairs={{4,0},{0,4},{12,8},{8,12},{20,16},{16,20},{28,24},{24,28},{5,1},{1... | collective-permute-start | bytes 786440 | tf_op jit(solution)/shard_map/ppermute | solution.py:41
  59.8 10.1 %collective-permute-start.18 = (bf16[256,512]{1,0:T(8,128)(2,1)S(1)}, bf16[256,512]{1,0:T(8,128)(2,1)S(1)}, u32[]{:S(2)}, u32[]{:S(2)}) collective-permute-start(bf16[256,512]{1,0:T(8,128)(2,1)S(1)} %get-tuple-element.29), channel_id=1, source_target_pairs={{24,0},{28,4},{16,8},{20,12},{8,16},{12,20},{0,24},{4,28},{25,1},{... | collective-permute-start | bytes 786440 | tf_op jit(solution)/shard_map/ppermute | solution.py:41
  61.2 10.2 %collective-permute-start.9 = (f32[64,1024]{1,0:T(8,128)S(1)}, f32[64,1024]{1,0:T(8,128)S(1)}, u32[]{:S(2)}, u32[]{:S(2)}) collective-permute-start(f32[64,1024]{1,0:T(8,128)S(1)} %get-tuple-element.35), channel_id=1, source_target_pairs={{4,0},{0,4},{12,8},{8,12},{20,16},{16,20},{28,24},{24,28},{5,1},{1... | collective-permute-start | bytes 786440 | tf_op jit(solution)/shard_map/ppermute | solution.py:41
  61.5 10.9 %collective-permute-start.17 = (bf16[1024,256]{1,0:T(8,128)(2,1)S(1)}, bf16[1024,256]{1,0:T(8,128)(2,1)S(1)}, u32[]{:S(2)}, u32[]{:S(2)}) collective-permute-start(bf16[1024,256]{1,0:T(8,128)(2,1)S(1)} %shard_map.54.far), channel_id=1, source_target_pairs={{4,0},{0,4},{12,8},{8,12},{20,16},{16,20},{28,24},{24,28},{5,1},{1... | collective-permute-start | bytes 1572872 | tf_op jit(solution)/shard_map/ppermute | solution.py:41
  62.0 17.9 %collective-permute-start.20 = (bf16[512,512]{1,0:T(8,128)(2,1)S(1)}, bf16[512,512]{1,0:T(8,128)(2,1)S(1)}, u32[]{:S(2)}, u32[]{:S(2)}) collective-permute-start(bf16[512,512]{1,0:T(8,128)(2,1)S(1)} %get-tuple-element.30), channel_id=1, source_target_pairs={{8,0},{12,4},{0,8},{4,12},{24,16},{28,20},{16,24},{20,28},{9,1},{1... | collective-permute-start | bytes 1572872 | tf_op jit(solution)/shard_map/ppermute | solution.py:41
  63.5 16.4 %collective-permute-start.21 = (bf16[512,512]{1,0:T(8,128)(2,1)S(1)}, bf16[512,512]{1,0:T(8,128)(2,1)S(1)}, u32[]{:S(2)}, u32[]{:S(2)}) collective-permute-start(bf16[512,512]{1,0:T(8,128)(2,1)S(1)} %get-tuple-element.31), channel_id=1, source_target_pairs={{16,0},{20,4},{24,8},{28,12},{0,16},{4,20},{8,24},{12,28},{17,1},{... | collective-permute-start | bytes 1572872 | tf_op jit(solution)/shard_map/ppermute | solution.py:41
  69.9 6.4 %collective-permute-start.19 = (bf16[256,512]{1,0:T(8,128)(2,1)S(1)}, bf16[256,512]{1,0:T(8,128)(2,1)S(1)}, u32[]{:S(2)}, u32[]{:S(2)}) collective-permute-start(bf16[256,512]{1,0:T(8,128)(2,1)S(1)} %collective-permute-done.18.refs_0_), channel_id=1, source_target_pairs={{1,0},{0,1},{3,2},{2,3},{5,4},{4,5},{7,6},{6,7},{9,8},{8,9},{11,10... | collective-permute-start | bytes 786440 | tf_op jit(solution)/shard_map/ppermute | solution.py:229
  (1 other events, 12.0 us)

commit v7 on v6

--- a/solution.py
+++ b/solution.py
@@ -64,7 +64,6 @@
         out_specs=out_specs or jax.tree.map(lambda _: VMEM, out),
         scratch_shapes=scratch,
         compiler_params=pltpu.CompilerParams(vmem_limit_bytes=40 * 2**20),
-        cost_estimate=pl.CostEstimate(flops=0, bytes_accessed=0, transcendentals=0),
     )(*args)
 
 
@@ -79,7 +78,8 @@
         self.column = [(db, 0) for db in range(1, self.rows)]
         self.across = [(db, da) for db in range(1, self.rows) for da in range(1, self.cols)]
         self.half = self.taken // 2
-        self.fits = self.width % 128 == 0 and self.held % (self.width * self.cores) == 0 and self.node % 2 == 0 and self.node > 2
+        whole = self.held % (self.width * self.cores) == 0 and self.node % 2 == 0 and self.node > 2
+        self.fits = whole and self.width % 128 == 0 and self.tokens % 128 == 0 and self.taken % 256 == 0
 
 
 def route_kernel(s, *refs):
@@ -163,17 +163,20 @@
         out[rows] = jnp.dot(jnp.concatenate(left, axis=1), packed[...], preferred_element_type=F32)
 
 
-def late_kernel(s, scale, early, turned, theirs, *refs):
-    *blocks, out, packed, sums, sems = refs
-    n = len(blocks)
-    for k, block in enumerate(blocks):
-        packed[k * s.tokens : (k + 1) * s.tokens] = block[: s.tokens]
-        packed[(n + k) * s.tokens : (n + k + 1) * s.tokens] = block[s.tokens :]
+def add_kernel(s, k, sums, turned, theirs, block, out):
+    at = slice((1 + k) * s.tokens, (2 + k) * s.tokens)
+    for rows in blocks_of(s.taken):
+        left = jnp.concatenate([turned[rows, at], theirs[rows, at]], axis=1)
+        out[rows] = sums[rows] + jnp.dot(left, block[...], preferred_element_type=F32)
+
+
+def last_kernel(s, scale, k, sums, turned, theirs, block, out, done, sems):
+    at = slice((1 + k) * s.tokens, (2 + k) * s.tokens)
     copies = []
     for i, rows in enumerate(blocks_of(s.taken)):
-        left = jnp.concatenate([turned[rows, s.tokens :], theirs[rows, s.tokens :]], axis=1)
-        sums[rows] = (early[rows] + jnp.dot(left, packed[...], preferred_element_type=F32)) * scale
-        copies.append(pltpu.make_async_copy(sums.at[rows], out.at[rows], sems.at[i]))
+        left = jnp.concatenate([turned[rows, at], theirs[rows, at]], axis=1)
+        done[rows] = (sums[rows] + jnp.dot(left, block[...], preferred_element_type=F32)) * scale
+        copies.append(pltpu.make_async_copy(done.at[rows], out.at[rows], sems.at[i]))
         copies[-1].start()
     for copy in copies:
         copy.wait()
@@ -213,7 +216,7 @@
     turned = call(turn, shape(s.taken, (1 + len(near)) * s.tokens), context, *contexts.values())
     turned_other = sibling(turned)
     turned_far = call(turn, shape(s.taken, len(s.across) * s.tokens), *contexts_far)
-    turned_far_other = sibling(turned_far, ())
+    turned_far_other = sibling(turned_far)
 
     columns = shape(s.chips, s.tokens, s.width)
     mine, other = call(
@@ -229,27 +232,25 @@
     far = [(x, lax.ppermute(x, "node", [(i ^ 1, i) for i in range(s.node)])) for x in shares]
 
     half_sums = shape(s.tokens, s.taken, dtype=F32)
+    near_sums = call(
+        functools.partial(context_kernel, s), shape(s.cores * s.tokens, s.taken, dtype=F32),
+        mine, theirs, out_weight, *after([*weights.values()], turned_other),
+    )
+    own, others = call(functools.partial(context_far_kernel, s), [half_sums] * 2, mine, theirs, near_sums, *weights_far)
+    context_grad = (own + sibling(others, (0.4375, 0.875))).astype(BF16)
+
+    result = shape(s.taken, s.width, dtype=F32)
     sums = call(
-        functools.partial(context_kernel, s), shape(s.cores * s.tokens, s.taken, dtype=F32),
-        mine, theirs, out_weight, *weights.values(),
-    )
-    own, others = call(functools.partial(context_far_kernel, s), [half_sums] * 2, mine, theirs, sums, *weights_far)
-    context_grad = (own + sibling(others, (0.25, 0.5, 0.75))).astype(BF16)
-
-    result = shape(s.taken, s.width, dtype=F32)
-    early = call(
         functools.partial(early_kernel, s), result,
         turned, turned_other, turned_far, turned_far_other, mine, theirs, *[x for two in far for x in two],
         scratch=[pltpu.VMEM((2 * (1 + len(far)) * s.tokens, s.width), BF16)],
     )
+    for k, block in enumerate(blocks[:-1]):
+        sums = call(functools.partial(add_kernel, s, k), result, sums, turned, turned_other, block)
     weight_grad = call(
-        functools.partial(late_kernel, s, scale), result, early, turned, turned_other, *blocks,
+        functools.partial(last_kernel, s, scale, len(blocks) - 1), result, sums, turned, turned_other, blocks[-1],
         out_specs=pl.BlockSpec(memory_space=pl.ANY),
-        scratch=[
-            pltpu.VMEM((2 * len(blocks) * s.tokens, s.width), BF16),
-            pltpu.VMEM((s.taken, s.width), F32),
-            pltpu.SemaphoreType.DMA((4,)),
-        ],
+        scratch=[pltpu.VMEM((s.taken, s.width), F32), pltpu.SemaphoreType.DMA((4,))],
     )
     return (context_grad, weight_grad)
 

time: 82.2 us -> 81.7 us (level)
    ppermute x18 -> x17, waiting for transfers between devices: 23.4 us -> 22.8 us  [shift(): lax.ppermute(array, 'outer', [(place(o, db, da, dc), o) for o in range(la...]
    ppermute x18 -> x17, starting transfers between devices: 14.1 us -> 13.6 us  [shift(): lax.ppermute(array, 'outer', [(place(o, db, da, dc), o) for o in range(la...]
    pallas_call x8 -> x9, Pallas kernels: 6.96 us -> 7.22 us  [call(): pl.pallas_call(kernel, out_shape=out, in_specs=[VMEM] * len(args), out_sp...]
  transfers between devices with their start and end apart: 22 -> 21, of which waited for: 12 -> 14; matrix products, arithmetic and copies ran while one was open for 1% -> 1% of each run, Pallas kernels for 6% -> 7%
where the time goes in v7:
time: 81.7 us; the launch traced here: 81.5 us
  waiting for transfers between devices  52.2 us (64%)
  starting transfers between devices  20.2 us (25%)
  Pallas kernels  7.22 us (9%)
  other arithmetic  0.93 us (1%)
    ppermute x3, waiting for transfers between devices, along_node(): lax.ppermute(array, 'node', [((i + d) % node, i) for i in range(node)])  25.3 us
    ppermute x17, waiting for transfers between devices, shift(): lax.ppermute(array, 'outer', [(place(o, db, da, dc), o) for o in range(la...  22.8 us
    ppermute x17, starting transfers between devices, shift(): lax.ppermute(array, 'outer', [(place(o, db, da, dc), o) for o in range(la...  13.6 us
    pallas_call x9, Pallas kernels, call(): pl.pallas_call(kernel, out_shape=out, in_specs=[VMEM] * len(args), out_sp...  7.22 us
    ppermute x3, starting transfers between devices, along_node(): lax.ppermute(array, 'node', [((i + d) % node, i) for i in range(node)])  4.95 us
    ppermute x1, waiting for transfers between devices, body(): lax.ppermute(x, 'node', [(i ^ 1, i) for i in range(s.node)])  4.12 us
  transfers between devices with their start and end apart: 21, of which 14 were waited for; matrix products, arithmetic and copies ran while one was open for 1% of the time, Pallas kernels for 7%

profile of v7, /device:TPU:0, one launch (start us, length us, event | category | flops | bytes accessed | tf_op | source)
XLA Modules:
  0.0 81.5 jit_solution(6005739392711794593)
XLA Ops:
  0.6 3.0 %collective-permute-start = (bf16[1024,512]{1,0:T(8,128)(2,1)}, bf16[1024,512]{1,0:T(8,128)(2,1)S(1)}, u32[]{:S(2)}, u32[]{:S(2)}) collective-permute-start(bf16[1024,512]{1,0:T(8,128)(2,1)} %refs_0_.4), channel_id=1, source_target_pairs={{8,0},{12,4},{0,8},{4,12},{24,16},{28,20},{16,24},{20,28},{9,1},{1... | collective-permute-start | bytes 3145736 | tf_op jit(solution)/shard_map/ppermute | solution.py:41
  3.6 1.5 %collective-permute-start.1 = (bf16[1024,512]{1,0:T(8,128)(2,1)}, bf16[1024,512]{1,0:T(8,128)(2,1)S(1)}, u32[]{:S(2)}, u32[]{:S(2)}) collective-permute-start(bf16[1024,512]{1,0:T(8,128)(2,1)} %refs_0_.4), channel_id=1, source_target_pairs={{16,0},{20,4},{24,8},{28,12},{0,16},{4,20},{8,24},{12,28},{17,1},{... | collective-permute-start | bytes 3145736 | tf_op jit(solution)/shard_map/ppermute | solution.py:41
  5.2 1.6 %collective-permute-start.3 = (bf16[256,1024]{1,0:T(8,128)(2,1)}, bf16[256,1024]{1,0:T(8,128)(2,1)S(1)}, u32[]{:S(2)}, u32[]{:S(2)}) collective-permute-start(bf16[256,1024]{1,0:T(8,128)(2,1)} %refs_0_.2), channel_id=1, source_target_pairs={{3,0},{0,1},{1,2},{2,3},{7,4},{4,5},{5,6},{6,7},{11,8},{8,9},{9,10... | collective-permute-start | bytes 1572872 | tf_op jit(solution)/shard_map/ppermute | solution.py:52
  6.7 2.2 %collective-permute-start.2 = (bf16[256,1024]{1,0:T(8,128)(2,1)}, bf16[256,1024]{1,0:T(8,128)(2,1)S(1)}, u32[]{:S(2)}, u32[]{:S(2)}) collective-permute-start(bf16[256,1024]{1,0:T(8,128)(2,1)} %refs_0_.2), channel_id=1, source_target_pairs={{1,0},{2,1},{3,2},{0,3},{5,4},{6,5},{7,6},{4,7},{9,8},{10,9},{11,1... | collective-permute-start | bytes 1572872 | tf_op jit(solution)/shard_map/ppermute | solution.py:52
  9.5 12.6 %collective-permute-done.3.refs_3_ = bf16[256,1024]{1,0:T(8,128)(2,1)S(1)} collective-permute-done((bf16[256,1024]{1,0:T(8,128)(2,1)}, bf16[256,1024]{1,0:T(8,128)(2,1)S(1)}, u32[]{:S(2)}, u32[]{:S(2)}) %collective-permute-start.3) | collective-permute-done | bytes 524320 | tf_op jit(solution)/shard_map/ppermute | solution.py:52
  22.6 8.4 %collective-permute-done.2.refs_1_ = bf16[256,1024]{1,0:T(8,128)(2,1)S(1)} collective-permute-done((bf16[256,1024]{1,0:T(8,128)(2,1)}, bf16[256,1024]{1,0:T(8,128)(2,1)S(1)}, u32[]{:S(2)}, u32[]{:S(2)}) %collective-permute-start.2) | collective-permute-done | bytes 524320 | tf_op jit(solution)/shard_map/ppermute | solution.py:52
  33.7 5.3 %collective-permute-done.8.refs_1_ = bf16[256,1024]{1,0:T(8,128)(2,1)S(1)} collective-permute-done((bf16[256,1024]{1,0:T(8,128)(2,1)}, bf16[256,1024]{1,0:T(8,128)(2,1)S(1)}, u32[]{:S(2)}, u32[]{:S(2)}) %collective-permute-start.8) | collective-permute-done | bytes 524320 | tf_op jit(solution)/shard_map/ppermute | solution.py:41
  39.1 2.1 %collective-permute-done.9.refs_2_ = bf16[256,1024]{1,0:T(8,128)(2,1)S(1)} collective-permute-done((bf16[256,1024]{1,0:T(8,128)(2,1)}, bf16[256,1024]{1,0:T(8,128)(2,1)S(1)}, u32[]{:S(2)}, u32[]{:S(2)}) %collective-permute-start.9) | collective-permute-done | bytes 524320 | tf_op jit(solution)/shard_map/ppermute | solution.py:41
  41.7 4.3 %collective-permute-done.4.refs_2_ = bf16[256,1024]{1,0:T(8,128)(2,1)S(1)} collective-permute-done((bf16[256,1024]{1,0:T(8,128)(2,1)S(1)}, bf16[256,1024]{1,0:T(8,128)(2,1)S(1)}, u32[]{:S(2)}, u32[]{:S(2)}) %collective-permute-start.4) | collective-permute-done | bytes 524320 | tf_op jit(solution)/shard_map/ppermute | solution.py:52
  46.3 3.2 %collective-permute-done.6.refs_1_ = bf16[512,512]{1,0:T(8,128)(2,1)S(1)} collective-permute-done((bf16[512,512]{1,0:T(8,128)(2,1)S(1)}, bf16[512,512]{1,0:T(8,128)(2,1)S(1)}, u32[]{:S(2)}, u32[]{:S(2)}) %collective-permute-start.6) | collective-permute-done | bytes 524320 | tf_op jit(solution)/shard_map/ppermute | solution.py:41
  49.5 1.5 %collective-permute-done.5.refs_0_ = bf16[512,512]{1,0:T(8,128)(2,1)S(1)} collective-permute-done((bf16[512,512]{1,0:T(8,128)(2,1)S(1)}, bf16[512,512]{1,0:T(8,128)(2,1)S(1)}, u32[]{:S(2)}, u32[]{:S(2)}) %collective-permute-start.5) | collective-permute-done | bytes 524320 | tf_op jit(solution)/shard_map/ppermute | solution.py:41
  51.0 1.6 %collective-permute-start.14 = (bf16[128,1024]{1,0:T(8,128)(2,1)S(1)}, bf16[128,1024]{1,0:T(8,128)(2,1)S(1)}, u32[]{:S(2)}, u32[]{:S(2)}) collective-permute-start(bf16[128,1024]{1,0:T(8,128)(2,1)S(1)} %slice.28), channel_id=1, source_target_pairs={{16,0},{20,4},{24,8},{28,12},{0,16},{4,20},{8,24},{12,28},{17,1},{... | collective-permute-start | bytes 786440 | tf_op jit(solution)/shard_map/ppermute | solution.py:41
  53.7 1.6 %collective-permute-start.17 = (bf16[256,512]{1,0:T(8,128)(2,1)S(1)}, bf16[256,512]{1,0:T(8,128)(2,1)S(1)}, u32[]{:S(2)}, u32[]{:S(2)}) collective-permute-start(bf16[256,512]{1,0:T(8,128)(2,1)S(1)} %get-tuple-element.33), channel_id=1, source_target_pairs={{24,0},{28,4},{16,8},{20,12},{8,16},{12,20},{0,24},{4,28},{25,1},{... | collective-permute-start | bytes 786440 | tf_op jit(solution)/shard_map/ppermute | solution.py:41
  55.3 1.8 %shard_map.52.near = f32[512,1024]{1,0:T(8,128)S(1)} custom-call(bf16[4,256,512]{2,1,0:T(8,128)(2,1)S(1)} %get-tuple-element.22.mine, bf16[4,256,512]{2,1,0:T(8,128)(2,1)S(1)} %collective-permute-done.7.theirs.other, bf16[1024,512]{1,0:T(8,128)(2,1)S(1)} %copy-done, bf16[1024,512]{1,0:T(8,128)(2,1)S(1)} %collective-permute-done.refs_1_, ...), custom_call_target="tpu_custom_call" | custom-call | tf_op jit(solution)/shard_map/pallas_call | solution.py:60
  58.5 1.2 %collective-permute-done.14.refs_0_ = bf16[128,1024]{1,0:T(8,128)(2,1)S(1)} collective-permute-done((bf16[128,1024]{1,0:T(8,128)(2,1)S(1)}, bf16[128,1024]{1,0:T(8,128)(2,1)S(1)}, u32[]{:S(2)}, u32[]{:S(2)}) %collective-permute-start.14) | collective-permute-done | bytes 262176 | tf_op jit(solution)/shard_map/ppermute | solution.py:41
  59.8 2.0 %collective-permute-done.15.refs_1_ = bf16[128,1024]{1,0:T(8,128)(2,1)S(1)} collective-permute-done((bf16[128,1024]{1,0:T(8,128)(2,1)S(1)}, bf16[128,1024]{1,0:T(8,128)(2,1)S(1)}, u32[]{:S(2)}, u32[]{:S(2)}) %collective-permute-start.15) | collective-permute-done | bytes 262176 | tf_op jit(solution)/shard_map/ppermute | solution.py:41
  62.7 4.7 %collective-permute-done.17.refs_0_ = bf16[256,512]{1,0:T(8,128)(2,1)S(1)} collective-permute-done((bf16[256,512]{1,0:T(8,128)(2,1)S(1)}, bf16[256,512]{1,0:T(8,128)(2,1)S(1)}, u32[]{:S(2)}, u32[]{:S(2)}) %collective-permute-start.17) | collective-permute-done | bytes 262176 | tf_op jit(solution)/shard_map/ppermute | solution.py:41
  67.3 1.5 %collective-permute-start.20 = (bf16[512,512]{1,0:T(8,128)(2,1)S(1)}, bf16[512,512]{1,0:T(8,128)(2,1)S(1)}, u32[]{:S(2)}, u32[]{:S(2)}) collective-permute-start(bf16[512,512]{1,0:T(8,128)(2,1)S(1)} %get-tuple-element.35), channel_id=1, source_target_pairs={{16,0},{20,4},{24,8},{28,12},{0,16},{4,20},{8,24},{12,28},{17,1},{... | collective-permute-start | bytes 1572872 | tf_op jit(solution)/shard_map/ppermute | solution.py:41
  68.9 1.6 %collective-permute-start.18 = (bf16[256,512]{1,0:T(8,128)(2,1)S(1)}, bf16[256,512]{1,0:T(8,128)(2,1)S(1)}, u32[]{:S(2)}, u32[]{:S(2)}) collective-permute-start(bf16[256,512]{1,0:T(8,128)(2,1)S(1)} %collective-permute-done.17.refs_0_), channel_id=1, source_target_pairs={{1,0},{0,1},{3,2},{2,3},{5,4},{4,5},{7,6},{6,7},{9,8},{8,9},{11,10... | collective-permute-start | bytes 786440 | tf_op jit(solution)/shard_map/ppermute | solution.py:232
  71.4 4.1 %collective-permute-done.18.refs_1_ = bf16[256,512]{1,0:T(8,128)(2,1)S(1)} collective-permute-done((bf16[256,512]{1,0:T(8,128)(2,1)S(1)}, bf16[256,512]{1,0:T(8,128)(2,1)S(1)}, u32[]{:S(2)}, u32[]{:S(2)}) %collective-permute-start.18) | collective-permute-done | bytes 262176 | tf_op jit(solution)/shard_map/ppermute | solution.py:232
  75.5 1.3 %shard_map.56.sums = f32[1024,512]{1,0:T(8,128)S(1)} custom-call(bf16[1024,768]{1,0:T(8,128)(2,1)S(1)} %shard_map.51.turned, bf16[1024,768]{1,0:T(8,128)(2,1)S(1)} %collective-permute-done.10.theirs, bf16[1024,256]{1,0:T(8,128)(2,1)S(1)} %shard_map.54.far, bf16[1024,256]{1,0:T(8,128)(2,1)S(1)} %collective-permute-done.16.far_theirs, ...), custom_call_target="tpu_custom_call" | custom-call | tf_op jit(solution)/shard_map/pallas_call | solution.py:60
  76.8 1.1 %collective-permute-done.19.block = bf16[512,512]{1,0:T(8,128)(2,1)S(1)} collective-permute-done((bf16[512,512]{1,0:T(8,128)(2,1)S(1)}, bf16[512,512]{1,0:T(8,128)(2,1)S(1)}, u32[]{:S(2)}, u32[]{:S(2)}) %collective-permute-start.19) | collective-permute-done | bytes 524320 | tf_op jit(solution)/shard_map/ppermute | solution.py:41
  78.6 1.2 %collective-permute-done.20.block = bf16[512,512]{1,0:T(8,128)(2,1)S(1)} collective-permute-done((bf16[512,512]{1,0:T(8,128)(2,1)S(1)}, bf16[512,512]{1,0:T(8,128)(2,1)S(1)}, u32[]{:S(2)}, u32[]{:S(2)}) %collective-permute-start.20) | collective-permute-done | bytes 524320 | tf_op jit(solution)/shard_map/ppermute | solution.py:41
  79.9 1.7 %shard_map.58 = f32[1024,512]{1,0:T(8,128)} custom-call(f32[1024,512]{1,0:T(8,128)S(1)} %shard_map.57.sums, bf16[1024,768]{1,0:T(8,128)(2,1)S(1)} %shard_map.51.turned, bf16[1024,768]{1,0:T(8,128)(2,1)S(1)} %collective-permute-done.10.theirs, bf16[512,512]{1,0:T(8,128)(2,1)S(1)} %collective-permute-done.20.block), custom_call_target="tpu_custom_call" | custom-call | tf_op jit(solution)/shard_map/pallas_call | solution.py:60
  (40 shorter events, 9.6 us)
Async XLA Ops:
  0.6 40.5 %copy-start.1 = (bf16[256,1024]{1,0:T(8,128)(2,1)S(1)}, bf16[256,1024]{1,0:T(8,128)(2,1)}, u32[]{:S(2)}) copy-start(bf16[256,1024]{1,0:T(8,128)(2,1)} %refs_0_.3) | copy-start | bytes 1572868
  0.6 30.4 %collective-permute-start = (bf16[1024,512]{1,0:T(8,128)(2,1)}, bf16[1024,512]{1,0:T(8,128)(2,1)S(1)}, u32[]{:S(2)}, u32[]{:S(2)}) collective-permute-start(bf16[1024,512]{1,0:T(8,128)(2,1)} %refs_0_.4), channel_id=1, source_target_pairs={{8,0},{12,4},{0,8},{4,12},{24,16},{28,20},{16,24},{20,28},{9,1},{1... | collective-permute-start | bytes 3145736 | tf_op jit(solution)/shard_map/ppermute | solution.py:41
  3.6 27.4 %collective-permute-start.1 = (bf16[1024,512]{1,0:T(8,128)(2,1)}, bf16[1024,512]{1,0:T(8,128)(2,1)S(1)}, u32[]{:S(2)}, u32[]{:S(2)}) collective-permute-start(bf16[1024,512]{1,0:T(8,128)(2,1)} %refs_0_.4), channel_id=1, source_target_pairs={{16,0},{20,4},{24,8},{28,12},{0,16},{4,20},{8,24},{12,28},{17,1},{... | collective-permute-start | bytes 3145736 | tf_op jit(solution)/shard_map/ppermute | solution.py:41
  5.2 16.9 %collective-permute-start.3 = (bf16[256,1024]{1,0:T(8,128)(2,1)}, bf16[256,1024]{1,0:T(8,128)(2,1)S(1)}, u32[]{:S(2)}, u32[]{:S(2)}) collective-permute-start(bf16[256,1024]{1,0:T(8,128)(2,1)} %refs_0_.2), channel_id=1, source_target_pairs={{3,0},{0,1},{1,2},{2,3},{7,4},{4,5},{5,6},{6,7},{11,8},{8,9},{9,10... | collective-permute-start | bytes 1572872 | tf_op jit(solution)/shard_map/ppermute | solution.py:52
  6.7 24.3 %collective-permute-start.2 = (bf16[256,1024]{1,0:T(8,128)(2,1)}, bf16[256,1024]{1,0:T(8,128)(2,1)S(1)}, u32[]{:S(2)}, u32[]{:S(2)}) collective-permute-start(bf16[256,1024]{1,0:T(8,128)(2,1)} %refs_0_.2), channel_id=1, source_target_pairs={{1,0},{2,1},{3,2},{0,3},{5,4},{6,5},{7,6},{4,7},{9,8},{10,9},{11,1... | collective-permute-start | bytes 1572872 | tf_op jit(solution)/shard_map/ppermute | solution.py:52
  9.0 30.1 %collective-permute-start.8 = (bf16[256,1024]{1,0:T(8,128)(2,1)}, bf16[256,1024]{1,0:T(8,128)(2,1)S(1)}, u32[]{:S(2)}, u32[]{:S(2)}) collective-permute-start(bf16[256,1024]{1,0:T(8,128)(2,1)} %refs_0_.3), channel_id=1, source_target_pairs={{8,0},{12,4},{0,8},{4,12},{24,16},{28,20},{16,24},{20,28},{9,1},{1... | collective-permute-start | bytes 1572872 | tf_op jit(solution)/shard_map/ppermute | solution.py:41
  22.1 19.1 %collective-permute-start.9 = (bf16[256,1024]{1,0:T(8,128)(2,1)}, bf16[256,1024]{1,0:T(8,128)(2,1)S(1)}, u32[]{:S(2)}, u32[]{:S(2)}) collective-permute-start(bf16[256,1024]{1,0:T(8,128)(2,1)} %refs_0_.3), channel_id=1, source_target_pairs={{16,0},{20,4},{24,8},{28,12},{0,16},{4,20},{8,24},{12,28},{17,1},{... | collective-permute-start | bytes 1572872 | tf_op jit(solution)/shard_map/ppermute | solution.py:41
  31.0 15.0 %collective-permute-start.4 = (bf16[256,1024]{1,0:T(8,128)(2,1)S(1)}, bf16[256,1024]{1,0:T(8,128)(2,1)S(1)}, u32[]{:S(2)}, u32[]{:S(2)}) collective-permute-start(bf16[256,1024]{1,0:T(8,128)(2,1)S(1)} %collective-permute-done.3.refs_3_), channel_id=1, source_target_pairs={{3,0},{0,1},{1,2},{2,3},{7,4},{4,5},{5,6},{6,7},{11,8},{8,9},{9,10... | collective-permute-start | bytes 1572872 | tf_op jit(solution)/shard_map/ppermute | solution.py:52
  32.2 13.8 %copy-start.2 = (bf16[256,1024]{1,0:T(8,128)(2,1)S(1)}, bf16[256,1024]{1,0:T(8,128)(2,1)}, u32[]{:S(2)}) copy-start(bf16[256,1024]{1,0:T(8,128)(2,1)} %refs_0_.2) | copy-start | bytes 1572868
  32.2 17.2 %collective-permute-start.6 = (bf16[512,512]{1,0:T(8,128)(2,1)S(1)}, bf16[512,512]{1,0:T(8,128)(2,1)S(1)}, u32[]{:S(2)}, u32[]{:S(2)}) collective-permute-start(bf16[512,512]{1,0:T(8,128)(2,1)S(1)} %slice.22), channel_id=1, source_target_pairs={{8,0},{12,4},{0,8},{4,12},{24,16},{28,20},{16,24},{20,28},{9,1},{1... | collective-permute-start | bytes 1572872 | tf_op jit(solution)/shard_map/ppermute | solution.py:41
  32.8 18.1 %collective-permute-start.5 = (bf16[512,512]{1,0:T(8,128)(2,1)S(1)}, bf16[512,512]{1,0:T(8,128)(2,1)S(1)}, u32[]{:S(2)}, u32[]{:S(2)}) collective-permute-start(bf16[512,512]{1,0:T(8,128)(2,1)S(1)} %slice.21), channel_id=1, source_target_pairs={{16,0},{20,4},{24,8},{28,12},{0,16},{4,20},{8,24},{12,28},{17,1},{... | collective-permute-start | bytes 1572872 | tf_op jit(solution)/shard_map/ppermute | solution.py:41
  41.6 12.0 %collective-permute-start.10 = (bf16[1024,768]{1,0:T(8,128)(2,1)S(1)}, bf16[1024,768]{1,0:T(8,128)(2,1)S(1)}, u32[]{:S(2)}, u32[]{:S(2)}) collective-permute-start(bf16[1024,768]{1,0:T(8,128)(2,1)S(1)} %shard_map.51.turned), channel_id=1, source_target_pairs={{4,0},{0,4},{12,8},{8,12},{20,16},{16,20},{28,24},{24,28},{5,1},{1... | collective-permute-start | bytes 4718600 | tf_op jit(solution)/shard_map/ppermute | solution.py:41
  46.3 9.0 %copy-start = (bf16[1024,512]{1,0:T(8,128)(2,1)S(1)}, bf16[1024,512]{1,0:T(8,128)(2,1)}, u32[]{:S(2)}) copy-start(bf16[1024,512]{1,0:T(8,128)(2,1)} %refs_0_.4) | copy-start | bytes 3145732
  50.9 2.7 %collective-permute-start.7 = (bf16[4,256,512]{2,1,0:T(8,128)(2,1)S(1)}, bf16[4,256,512]{2,1,0:T(8,128)(2,1)S(1)}, u32[]{:S(2)}, u32[]{:S(2)}) collective-permute-start(bf16[4,256,512]{2,1,0:T(8,128)(2,1)S(1)} %get-tuple-element.26), channel_id=1, source_target_pairs={{4,0},{0,4},{12,8},{8,12},{20,16},{16,20},{28,24},{24,28},{5,1},{1... | collective-permute-start | bytes 3145736 | tf_op jit(solution)/shard_map/ppermute | solution.py:41
  51.0 8.8 %collective-permute-start.14 = (bf16[128,1024]{1,0:T(8,128)(2,1)S(1)}, bf16[128,1024]{1,0:T(8,128)(2,1)S(1)}, u32[]{:S(2)}, u32[]{:S(2)}) collective-permute-start(bf16[128,1024]{1,0:T(8,128)(2,1)S(1)} %slice.28), channel_id=1, source_target_pairs={{16,0},{20,4},{24,8},{28,12},{0,16},{4,20},{8,24},{12,28},{17,1},{... | collective-permute-start | bytes 786440 | tf_op jit(solution)/shard_map/ppermute | solution.py:41
  52.6 9.2 %collective-permute-start.15 = (bf16[128,1024]{1,0:T(8,128)(2,1)S(1)}, bf16[128,1024]{1,0:T(8,128)(2,1)S(1)}, u32[]{:S(2)}, u32[]{:S(2)}) collective-permute-start(bf16[128,1024]{1,0:T(8,128)(2,1)S(1)} %slice.29), channel_id=1, source_target_pairs={{8,0},{12,4},{0,8},{4,12},{24,16},{28,20},{16,24},{20,28},{9,1},{1... | collective-permute-start | bytes 786440 | tf_op jit(solution)/shard_map/ppermute | solution.py:41
  53.7 13.6 %collective-permute-start.17 = (bf16[256,512]{1,0:T(8,128)(2,1)S(1)}, bf16[256,512]{1,0:T(8,128)(2,1)S(1)}, u32[]{:S(2)}, u32[]{:S(2)}) collective-permute-start(bf16[256,512]{1,0:T(8,128)(2,1)S(1)} %get-tuple-element.33), channel_id=1, source_target_pairs={{24,0},{28,4},{16,8},{20,12},{8,16},{12,20},{0,24},{4,28},{25,1},{... | collective-permute-start | bytes 786440 | tf_op jit(solution)/shard_map/ppermute | solution.py:41
  57.9 10.9 %collective-permute-start.11 = (f32[112,1024]{1,0:T(8,128)S(1)}, f32[112,1024]{1,0:T(8,128)S(1)}, u32[]{:S(2)}, u32[]{:S(2)}) collective-permute-start(f32[112,1024]{1,0:T(8,128)S(1)} %get-tuple-element.36), channel_id=1, source_target_pairs={{4,0},{0,4},{12,8},{8,12},{20,16},{16,20},{28,24},{24,28},{5,1},{1... | collective-permute-start | bytes 1376264 | tf_op jit(solution)/shard_map/ppermute | solution.py:41
  58.0 12.4 %collective-permute-start.12 = (f32[112,1024]{1,0:T(8,128)S(1)}, f32[112,1024]{1,0:T(8,128)S(1)}, u32[]{:S(2)}, u32[]{:S(2)}) collective-permute-start(f32[112,1024]{1,0:T(8,128)S(1)} %get-tuple-element.37), channel_id=1, source_target_pairs={{4,0},{0,4},{12,8},{8,12},{20,16},{16,20},{28,24},{24,28},{5,1},{1... | collective-permute-start | bytes 1376264 | tf_op jit(solution)/shard_map/ppermute | solution.py:41
  59.8 2.3 %collective-permute-start.13 = (f32[32,1024]{1,0:T(8,128)S(1)}, f32[32,1024]{1,0:T(8,128)S(1)}, u32[]{:S(2)}, u32[]{:S(2)}) collective-permute-start(f32[32,1024]{1,0:T(8,128)S(1)} %slice.25), channel_id=1, source_target_pairs={{4,0},{0,4},{12,8},{8,12},{20,16},{16,20},{28,24},{24,28},{5,1},{1... | collective-permute-start | bytes 393224 | tf_op jit(solution)/shard_map/ppermute | solution.py:41
  62.0 9.4 %collective-permute-start.16 = (bf16[1024,256]{1,0:T(8,128)(2,1)S(1)}, bf16[1024,256]{1,0:T(8,128)(2,1)S(1)}, u32[]{:S(2)}, u32[]{:S(2)}) collective-permute-start(bf16[1024,256]{1,0:T(8,128)(2,1)S(1)} %shard_map.54.far), channel_id=1, source_target_pairs={{4,0},{0,4},{12,8},{8,12},{20,16},{16,20},{28,24},{24,28},{5,1},{1... | collective-permute-start | bytes 1572872 | tf_op jit(solution)/shard_map/ppermute | solution.py:41
  62.1 15.9 %collective-permute-start.19 = (bf16[512,512]{1,0:T(8,128)(2,1)S(1)}, bf16[512,512]{1,0:T(8,128)(2,1)S(1)}, u32[]{:S(2)}, u32[]{:S(2)}) collective-permute-start(bf16[512,512]{1,0:T(8,128)(2,1)S(1)} %get-tuple-element.34), channel_id=1, source_target_pairs={{8,0},{12,4},{0,8},{4,12},{24,16},{28,20},{16,24},{20,28},{9,1},{1... | collective-permute-start | bytes 1572872 | tf_op jit(solution)/shard_map/ppermute | solution.py:41
  67.3 12.5 %collective-permute-start.20 = (bf16[512,512]{1,0:T(8,128)(2,1)S(1)}, bf16[512,512]{1,0:T(8,128)(2,1)S(1)}, u32[]{:S(2)}, u32[]{:S(2)}) collective-permute-start(bf16[512,512]{1,0:T(8,128)(2,1)S(1)} %get-tuple-element.35), channel_id=1, source_target_pairs={{16,0},{20,4},{24,8},{28,12},{0,16},{4,20},{8,24},{12,28},{17,1},{... | collective-permute-start | bytes 1572872 | tf_op jit(solution)/shard_map/ppermute | solution.py:41
  68.9 6.6 %collective-permute-start.18 = (bf16[256,512]{1,0:T(8,128)(2,1)S(1)}, bf16[256,512]{1,0:T(8,128)(2,1)S(1)}, u32[]{:S(2)}, u32[]{:S(2)}) collective-permute-start(bf16[256,512]{1,0:T(8,128)(2,1)S(1)} %collective-permute-done.17.refs_0_), channel_id=1, source_target_pairs={{1,0},{0,1},{3,2},{2,3},{5,4},{4,5},{7,6},{6,7},{9,8},{8,9},{11,10... | collective-permute-start | bytes 786440 | tf_op jit(solution)/shard_map/ppermute | solution.py:232

commit v8 on v7

--- a/solution.py
+++ b/solution.py
@@ -147,8 +147,8 @@
         others[:, side] = total[s.tokens :]
 
 
-def blocks_of(rows):
-    return [slice(i * rows // 4, (i + 1) * rows // 4) for i in range(4)]
+def blocks_of(rows, count=4):
+    return [slice(i * rows // count, (i + 1) * rows // count) for i in range(count)]
 
 
 def early_kernel(s, turned, theirs, far, far_theirs, mine, other, *refs):
@@ -173,7 +173,7 @@
 def last_kernel(s, scale, k, sums, turned, theirs, block, out, done, sems):
     at = slice((1 + k) * s.tokens, (2 + k) * s.tokens)
     copies = []
-    for i, rows in enumerate(blocks_of(s.taken)):
+    for i, rows in enumerate(blocks_of(s.taken, sems.shape[0])):
         left = jnp.concatenate([turned[rows, at], theirs[rows, at]], axis=1)
         done[rows] = (sums[rows] + jnp.dot(left, block[...], preferred_element_type=F32)) * scale
         copies.append(pltpu.make_async_copy(done.at[rows], out.at[rows], sems.at[i]))
@@ -250,7 +250,7 @@
     weight_grad = call(
         functools.partial(last_kernel, s, scale, len(blocks) - 1), result, sums, turned, turned_other, blocks[-1],
         out_specs=pl.BlockSpec(memory_space=pl.ANY),
-        scratch=[pltpu.VMEM((s.taken, s.width), F32), pltpu.SemaphoreType.DMA((4,))],
+        scratch=[pltpu.VMEM((s.taken, s.width), F32), pltpu.SemaphoreType.DMA((8,))],
     )
     return (context_grad, weight_grad)
 

time: 81.7 us -> 81.6 us (level)
  no operation moved by 1% of the time
where the time goes in v8:
time: 81.6 us; the launch traced here: 81.5 us
  waiting for transfers between devices  52.2 us (64%)
  starting transfers between devices  20.2 us (25%)
  Pallas kernels  7.19 us (9%)
  other arithmetic  0.93 us (1%)
    ppermute x3, waiting for transfers between devices, along_node(): lax.ppermute(array, 'node', [((i + d) % node, i) for i in range(node)])  25.3 us
    ppermute x17, waiting for transfers between devices, shift(): lax.ppermute(array, 'outer', [(place(o, db, da, dc), o) for o in range(la...  22.8 us
    ppermute x17, starting transfers between devices, shift(): lax.ppermute(array, 'outer', [(place(o, db, da, dc), o) for o in range(la...  13.6 us
    pallas_call x9, Pallas kernels, call(): pl.pallas_call(kernel, out_shape=out, in_specs=[VMEM] * len(args), out_sp...  7.19 us
    ppermute x3, starting transfers between devices, along_node(): lax.ppermute(array, 'node', [((i + d) % node, i) for i in range(node)])  4.95 us
    ppermute x1, waiting for transfers between devices, body(): lax.ppermute(x, 'node', [(i ^ 1, i) for i in range(s.node)])  4.12 us
  transfers between devices with their start and end apart: 21, of which 14 were waited for; matrix products, arithmetic and copies ran while one was open for 1% of the time, Pallas kernels for 7%

profile of v8, /device:TPU:0, one launch (start us, length us, event | category | flops | bytes accessed | tf_op | source)
XLA Modules:
  0.0 81.5 jit_solution(3185038174637420519)
XLA Ops:
  0.6 3.0 %collective-permute-start = (bf16[1024,512]{1,0:T(8,128)(2,1)}, bf16[1024,512]{1,0:T(8,128)(2,1)S(1)}, u32[]{:S(2)}, u32[]{:S(2)}) collective-permute-start(bf16[1024,512]{1,0:T(8,128)(2,1)} %refs_0_.4), channel_id=1, source_target_pairs={{8,0},{12,4},{0,8},{4,12},{24,16},{28,20},{16,24},{20,28},{9,1},{1... | collective-permute-start | bytes 3145736 | tf_op jit(solution)/shard_map/ppermute | solution.py:41
  3.6 1.5 %collective-permute-start.1 = (bf16[1024,512]{1,0:T(8,128)(2,1)}, bf16[1024,512]{1,0:T(8,128)(2,1)S(1)}, u32[]{:S(2)}, u32[]{:S(2)}) collective-permute-start(bf16[1024,512]{1,0:T(8,128)(2,1)} %refs_0_.4), channel_id=1, source_target_pairs={{16,0},{20,4},{24,8},{28,12},{0,16},{4,20},{8,24},{12,28},{17,1},{... | collective-permute-start | bytes 3145736 | tf_op jit(solution)/shard_map/ppermute | solution.py:41
  5.2 1.6 %collective-permute-start.3 = (bf16[256,1024]{1,0:T(8,128)(2,1)}, bf16[256,1024]{1,0:T(8,128)(2,1)S(1)}, u32[]{:S(2)}, u32[]{:S(2)}) collective-permute-start(bf16[256,1024]{1,0:T(8,128)(2,1)} %refs_0_.2), channel_id=1, source_target_pairs={{3,0},{0,1},{1,2},{2,3},{7,4},{4,5},{5,6},{6,7},{11,8},{8,9},{9,10... | collective-permute-start | bytes 1572872 | tf_op jit(solution)/shard_map/ppermute | solution.py:52
  6.7 2.2 %collective-permute-start.2 = (bf16[256,1024]{1,0:T(8,128)(2,1)}, bf16[256,1024]{1,0:T(8,128)(2,1)S(1)}, u32[]{:S(2)}, u32[]{:S(2)}) collective-permute-start(bf16[256,1024]{1,0:T(8,128)(2,1)} %refs_0_.2), channel_id=1, source_target_pairs={{1,0},{2,1},{3,2},{0,3},{5,4},{6,5},{7,6},{4,7},{9,8},{10,9},{11,1... | collective-permute-start | bytes 1572872 | tf_op jit(solution)/shard_map/ppermute | solution.py:52
  9.5 12.6 %collective-permute-done.3.refs_3_ = bf16[256,1024]{1,0:T(8,128)(2,1)S(1)} collective-permute-done((bf16[256,1024]{1,0:T(8,128)(2,1)}, bf16[256,1024]{1,0:T(8,128)(2,1)S(1)}, u32[]{:S(2)}, u32[]{:S(2)}) %collective-permute-start.3) | collective-permute-done | bytes 524320 | tf_op jit(solution)/shard_map/ppermute | solution.py:52
  22.6 8.4 %collective-permute-done.2.refs_1_ = bf16[256,1024]{1,0:T(8,128)(2,1)S(1)} collective-permute-done((bf16[256,1024]{1,0:T(8,128)(2,1)}, bf16[256,1024]{1,0:T(8,128)(2,1)S(1)}, u32[]{:S(2)}, u32[]{:S(2)}) %collective-permute-start.2) | collective-permute-done | bytes 524320 | tf_op jit(solution)/shard_map/ppermute | solution.py:52
  33.7 5.3 %collective-permute-done.8.refs_1_ = bf16[256,1024]{1,0:T(8,128)(2,1)S(1)} collective-permute-done((bf16[256,1024]{1,0:T(8,128)(2,1)}, bf16[256,1024]{1,0:T(8,128)(2,1)S(1)}, u32[]{:S(2)}, u32[]{:S(2)}) %collective-permute-start.8) | collective-permute-done | bytes 524320 | tf_op jit(solution)/shard_map/ppermute | solution.py:41
  39.1 2.1 %collective-permute-done.9.refs_2_ = bf16[256,1024]{1,0:T(8,128)(2,1)S(1)} collective-permute-done((bf16[256,1024]{1,0:T(8,128)(2,1)}, bf16[256,1024]{1,0:T(8,128)(2,1)S(1)}, u32[]{:S(2)}, u32[]{:S(2)}) %collective-permute-start.9) | collective-permute-done | bytes 524320 | tf_op jit(solution)/shard_map/ppermute | solution.py:41
  41.7 4.3 %collective-permute-done.4.refs_2_ = bf16[256,1024]{1,0:T(8,128)(2,1)S(1)} collective-permute-done((bf16[256,1024]{1,0:T(8,128)(2,1)S(1)}, bf16[256,1024]{1,0:T(8,128)(2,1)S(1)}, u32[]{:S(2)}, u32[]{:S(2)}) %collective-permute-start.4) | collective-permute-done | bytes 524320 | tf_op jit(solution)/shard_map/ppermute | solution.py:52
  46.3 3.2 %collective-permute-done.6.refs_1_ = bf16[512,512]{1,0:T(8,128)(2,1)S(1)} collective-permute-done((bf16[512,512]{1,0:T(8,128)(2,1)S(1)}, bf16[512,512]{1,0:T(8,128)(2,1)S(1)}, u32[]{:S(2)}, u32[]{:S(2)}) %collective-permute-start.6) | collective-permute-done | bytes 524320 | tf_op jit(solution)/shard_map/ppermute | solution.py:41
  49.5 1.5 %collective-permute-done.5.refs_0_ = bf16[512,512]{1,0:T(8,128)(2,1)S(1)} collective-permute-done((bf16[512,512]{1,0:T(8,128)(2,1)S(1)}, bf16[512,512]{1,0:T(8,128)(2,1)S(1)}, u32[]{:S(2)}, u32[]{:S(2)}) %collective-permute-start.5) | collective-permute-done | bytes 524320 | tf_op jit(solution)/shard_map/ppermute | solution.py:41
  51.0 1.6 %collective-permute-start.14 = (bf16[128,1024]{1,0:T(8,128)(2,1)S(1)}, bf16[128,1024]{1,0:T(8,128)(2,1)S(1)}, u32[]{:S(2)}, u32[]{:S(2)}) collective-permute-start(bf16[128,1024]{1,0:T(8,128)(2,1)S(1)} %slice.28), channel_id=1, source_target_pairs={{16,0},{20,4},{24,8},{28,12},{0,16},{4,20},{8,24},{12,28},{17,1},{... | collective-permute-start | bytes 786440 | tf_op jit(solution)/shard_map/ppermute | solution.py:41
  53.7 1.6 %collective-permute-start.17 = (bf16[256,512]{1,0:T(8,128)(2,1)S(1)}, bf16[256,512]{1,0:T(8,128)(2,1)S(1)}, u32[]{:S(2)}, u32[]{:S(2)}) collective-permute-start(bf16[256,512]{1,0:T(8,128)(2,1)S(1)} %get-tuple-element.33), channel_id=1, source_target_pairs={{24,0},{28,4},{16,8},{20,12},{8,16},{12,20},{0,24},{4,28},{25,1},{... | collective-permute-start | bytes 786440 | tf_op jit(solution)/shard_map/ppermute | solution.py:41
  55.3 1.8 %shard_map.52.near = f32[512,1024]{1,0:T(8,128)S(1)} custom-call(bf16[4,256,512]{2,1,0:T(8,128)(2,1)S(1)} %get-tuple-element.22.mine, bf16[4,256,512]{2,1,0:T(8,128)(2,1)S(1)} %collective-permute-done.7.theirs.other, bf16[1024,512]{1,0:T(8,128)(2,1)S(1)} %copy-done, bf16[1024,512]{1,0:T(8,128)(2,1)S(1)} %collective-permute-done.refs_1_, ...), custom_call_target="tpu_custom_call" | custom-call | tf_op jit(solution)/shard_map/pallas_call | solution.py:60
  58.5 1.2 %collective-permute-done.14.refs_0_ = bf16[128,1024]{1,0:T(8,128)(2,1)S(1)} collective-permute-done((bf16[128,1024]{1,0:T(8,128)(2,1)S(1)}, bf16[128,1024]{1,0:T(8,128)(2,1)S(1)}, u32[]{:S(2)}, u32[]{:S(2)}) %collective-permute-start.14) | collective-permute-done | bytes 262176 | tf_op jit(solution)/shard_map/ppermute | solution.py:41
  59.8 2.0 %collective-permute-done.15.refs_1_ = bf16[128,1024]{1,0:T(8,128)(2,1)S(1)} collective-permute-done((bf16[128,1024]{1,0:T(8,128)(2,1)S(1)}, bf16[128,1024]{1,0:T(8,128)(2,1)S(1)}, u32[]{:S(2)}, u32[]{:S(2)}) %collective-permute-start.15) | collective-permute-done | bytes 262176 | tf_op jit(solution)/shard_map/ppermute | solution.py:41
  62.7 4.7 %collective-permute-done.17.refs_0_ = bf16[256,512]{1,0:T(8,128)(2,1)S(1)} collective-permute-done((bf16[256,512]{1,0:T(8,128)(2,1)S(1)}, bf16[256,512]{1,0:T(8,128)(2,1)S(1)}, u32[]{:S(2)}, u32[]{:S(2)}) %collective-permute-start.17) | collective-permute-done | bytes 262176 | tf_op jit(solution)/shard_map/ppermute | solution.py:41
  67.3 1.5 %collective-permute-start.20 = (bf16[512,512]{1,0:T(8,128)(2,1)S(1)}, bf16[512,512]{1,0:T(8,128)(2,1)S(1)}, u32[]{:S(2)}, u32[]{:S(2)}) collective-permute-start(bf16[512,512]{1,0:T(8,128)(2,1)S(1)} %get-tuple-element.35), channel_id=1, source_target_pairs={{16,0},{20,4},{24,8},{28,12},{0,16},{4,20},{8,24},{12,28},{17,1},{... | collective-permute-start | bytes 1572872 | tf_op jit(solution)/shard_map/ppermute | solution.py:41
  68.9 1.6 %collective-permute-start.18 = (bf16[256,512]{1,0:T(8,128)(2,1)S(1)}, bf16[256,512]{1,0:T(8,128)(2,1)S(1)}, u32[]{:S(2)}, u32[]{:S(2)}) collective-permute-start(bf16[256,512]{1,0:T(8,128)(2,1)S(1)} %collective-permute-done.17.refs_0_), channel_id=1, source_target_pairs={{1,0},{0,1},{3,2},{2,3},{5,4},{4,5},{7,6},{6,7},{9,8},{8,9},{11,10... | collective-permute-start | bytes 786440 | tf_op jit(solution)/shard_map/ppermute | solution.py:232
  71.4 4.1 %collective-permute-done.18.refs_1_ = bf16[256,512]{1,0:T(8,128)(2,1)S(1)} collective-permute-done((bf16[256,512]{1,0:T(8,128)(2,1)S(1)}, bf16[256,512]{1,0:T(8,128)(2,1)S(1)}, u32[]{:S(2)}, u32[]{:S(2)}) %collective-permute-start.18) | collective-permute-done | bytes 262176 | tf_op jit(solution)/shard_map/ppermute | solution.py:232
  75.5 1.3 %shard_map.56.sums = f32[1024,512]{1,0:T(8,128)S(1)} custom-call(bf16[1024,768]{1,0:T(8,128)(2,1)S(1)} %shard_map.51.turned, bf16[1024,768]{1,0:T(8,128)(2,1)S(1)} %collective-permute-done.10.theirs, bf16[1024,256]{1,0:T(8,128)(2,1)S(1)} %shard_map.54.far, bf16[1024,256]{1,0:T(8,128)(2,1)S(1)} %collective-permute-done.16.far_theirs, ...), custom_call_target="tpu_custom_call" | custom-call | tf_op jit(solution)/shard_map/pallas_call | solution.py:60
  76.8 1.1 %collective-permute-done.19.block = bf16[512,512]{1,0:T(8,128)(2,1)S(1)} collective-permute-done((bf16[512,512]{1,0:T(8,128)(2,1)S(1)}, bf16[512,512]{1,0:T(8,128)(2,1)S(1)}, u32[]{:S(2)}, u32[]{:S(2)}) %collective-permute-start.19) | collective-permute-done | bytes 524320 | tf_op jit(solution)/shard_map/ppermute | solution.py:41
  78.6 1.2 %collective-permute-done.20.block = bf16[512,512]{1,0:T(8,128)(2,1)S(1)} collective-permute-done((bf16[512,512]{1,0:T(8,128)(2,1)S(1)}, bf16[512,512]{1,0:T(8,128)(2,1)S(1)}, u32[]{:S(2)}, u32[]{:S(2)}) %collective-permute-start.20) | collective-permute-done | bytes 524320 | tf_op jit(solution)/shard_map/ppermute | solution.py:41
  79.9 1.6 %shard_map.58 = f32[1024,512]{1,0:T(8,128)} custom-call(f32[1024,512]{1,0:T(8,128)S(1)} %shard_map.57.sums, bf16[1024,768]{1,0:T(8,128)(2,1)S(1)} %shard_map.51.turned, bf16[1024,768]{1,0:T(8,128)(2,1)S(1)} %collective-permute-done.10.theirs, bf16[512,512]{1,0:T(8,128)(2,1)S(1)} %collective-permute-done.20.block), custom_call_target="tpu_custom_call" | custom-call | tf_op jit(solution)/shard_map/pallas_call | solution.py:60
  (40 shorter events, 9.6 us)
Async XLA Ops:
  0.6 40.5 %copy-start.1 = (bf16[256,1024]{1,0:T(8,128)(2,1)S(1)}, bf16[256,1024]{1,0:T(8,128)(2,1)}, u32[]{:S(2)}) copy-start(bf16[256,1024]{1,0:T(8,128)(2,1)} %refs_0_.3) | copy-start | bytes 1572868
  0.6 30.4 %collective-permute-start = (bf16[1024,512]{1,0:T(8,128)(2,1)}, bf16[1024,512]{1,0:T(8,128)(2,1)S(1)}, u32[]{:S(2)}, u32[]{:S(2)}) collective-permute-start(bf16[1024,512]{1,0:T(8,128)(2,1)} %refs_0_.4), channel_id=1, source_target_pairs={{8,0},{12,4},{0,8},{4,12},{24,16},{28,20},{16,24},{20,28},{9,1},{1... | collective-permute-start | bytes 3145736 | tf_op jit(solution)/shard_map/ppermute | solution.py:41
  3.6 27.4 %collective-permute-start.1 = (bf16[1024,512]{1,0:T(8,128)(2,1)}, bf16[1024,512]{1,0:T(8,128)(2,1)S(1)}, u32[]{:S(2)}, u32[]{:S(2)}) collective-permute-start(bf16[1024,512]{1,0:T(8,128)(2,1)} %refs_0_.4), channel_id=1, source_target_pairs={{16,0},{20,4},{24,8},{28,12},{0,16},{4,20},{8,24},{12,28},{17,1},{... | collective-permute-start | bytes 3145736 | tf_op jit(solution)/shard_map/ppermute | solution.py:41
  5.2 16.9 %collective-permute-start.3 = (bf16[256,1024]{1,0:T(8,128)(2,1)}, bf16[256,1024]{1,0:T(8,128)(2,1)S(1)}, u32[]{:S(2)}, u32[]{:S(2)}) collective-permute-start(bf16[256,1024]{1,0:T(8,128)(2,1)} %refs_0_.2), channel_id=1, source_target_pairs={{3,0},{0,1},{1,2},{2,3},{7,4},{4,5},{5,6},{6,7},{11,8},{8,9},{9,10... | collective-permute-start | bytes 1572872 | tf_op jit(solution)/shard_map/ppermute | solution.py:52
  6.7 24.3 %collective-permute-start.2 = (bf16[256,1024]{1,0:T(8,128)(2,1)}, bf16[256,1024]{1,0:T(8,128)(2,1)S(1)}, u32[]{:S(2)}, u32[]{:S(2)}) collective-permute-start(bf16[256,1024]{1,0:T(8,128)(2,1)} %refs_0_.2), channel_id=1, source_target_pairs={{1,0},{2,1},{3,2},{0,3},{5,4},{6,5},{7,6},{4,7},{9,8},{10,9},{11,1... | collective-permute-start | bytes 1572872 | tf_op jit(solution)/shard_map/ppermute | solution.py:52
  9.0 30.1 %collective-permute-start.8 = (bf16[256,1024]{1,0:T(8,128)(2,1)}, bf16[256,1024]{1,0:T(8,128)(2,1)S(1)}, u32[]{:S(2)}, u32[]{:S(2)}) collective-permute-start(bf16[256,1024]{1,0:T(8,128)(2,1)} %refs_0_.3), channel_id=1, source_target_pairs={{8,0},{12,4},{0,8},{4,12},{24,16},{28,20},{16,24},{20,28},{9,1},{1... | collective-permute-start | bytes 1572872 | tf_op jit(solution)/shard_map/ppermute | solution.py:41
  22.1 19.1 %collective-permute-start.9 = (bf16[256,1024]{1,0:T(8,128)(2,1)}, bf16[256,1024]{1,0:T(8,128)(2,1)S(1)}, u32[]{:S(2)}, u32[]{:S(2)}) collective-permute-start(bf16[256,1024]{1,0:T(8,128)(2,1)} %refs_0_.3), channel_id=1, source_target_pairs={{16,0},{20,4},{24,8},{28,12},{0,16},{4,20},{8,24},{12,28},{17,1},{... | collective-permute-start | bytes 1572872 | tf_op jit(solution)/shard_map/ppermute | solution.py:41
  31.0 15.0 %collective-permute-start.4 = (bf16[256,1024]{1,0:T(8,128)(2,1)S(1)}, bf16[256,1024]{1,0:T(8,128)(2,1)S(1)}, u32[]{:S(2)}, u32[]{:S(2)}) collective-permute-start(bf16[256,1024]{1,0:T(8,128)(2,1)S(1)} %collective-permute-done.3.refs_3_), channel_id=1, source_target_pairs={{3,0},{0,1},{1,2},{2,3},{7,4},{4,5},{5,6},{6,7},{11,8},{8,9},{9,10... | collective-permute-start | bytes 1572872 | tf_op jit(solution)/shard_map/ppermute | solution.py:52
  32.2 13.8 %copy-start.2 = (bf16[256,1024]{1,0:T(8,128)(2,1)S(1)}, bf16[256,1024]{1,0:T(8,128)(2,1)}, u32[]{:S(2)}) copy-start(bf16[256,1024]{1,0:T(8,128)(2,1)} %refs_0_.2) | copy-start | bytes 1572868
  32.2 17.2 %collective-permute-start.6 = (bf16[512,512]{1,0:T(8,128)(2,1)S(1)}, bf16[512,512]{1,0:T(8,128)(2,1)S(1)}, u32[]{:S(2)}, u32[]{:S(2)}) collective-permute-start(bf16[512,512]{1,0:T(8,128)(2,1)S(1)} %slice.22), channel_id=1, source_target_pairs={{8,0},{12,4},{0,8},{4,12},{24,16},{28,20},{16,24},{20,28},{9,1},{1... | collective-permute-start | bytes 1572872 | tf_op jit(solution)/shard_map/ppermute | solution.py:41
  32.8 18.1 %collective-permute-start.5 = (bf16[512,512]{1,0:T(8,128)(2,1)S(1)}, bf16[512,512]{1,0:T(8,128)(2,1)S(1)}, u32[]{:S(2)}, u32[]{:S(2)}) collective-permute-start(bf16[512,512]{1,0:T(8,128)(2,1)S(1)} %slice.21), channel_id=1, source_target_pairs={{16,0},{20,4},{24,8},{28,12},{0,16},{4,20},{8,24},{12,28},{17,1},{... | collective-permute-start | bytes 1572872 | tf_op jit(solution)/shard_map/ppermute | solution.py:41
  41.6 12.0 %collective-permute-start.10 = (bf16[1024,768]{1,0:T(8,128)(2,1)S(1)}, bf16[1024,768]{1,0:T(8,128)(2,1)S(1)}, u32[]{:S(2)}, u32[]{:S(2)}) collective-permute-start(bf16[1024,768]{1,0:T(8,128)(2,1)S(1)} %shard_map.51.turned), channel_id=1, source_target_pairs={{4,0},{0,4},{12,8},{8,12},{20,16},{16,20},{28,24},{24,28},{5,1},{1... | collective-permute-start | bytes 4718600 | tf_op jit(solution)/shard_map/ppermute | solution.py:41
  46.3 9.0 %copy-start = (bf16[1024,512]{1,0:T(8,128)(2,1)S(1)}, bf16[1024,512]{1,0:T(8,128)(2,1)}, u32[]{:S(2)}) copy-start(bf16[1024,512]{1,0:T(8,128)(2,1)} %refs_0_.4) | copy-start | bytes 3145732
  50.9 2.7 %collective-permute-start.7 = (bf16[4,256,512]{2,1,0:T(8,128)(2,1)S(1)}, bf16[4,256,512]{2,1,0:T(8,128)(2,1)S(1)}, u32[]{:S(2)}, u32[]{:S(2)}) collective-permute-start(bf16[4,256,512]{2,1,0:T(8,128)(2,1)S(1)} %get-tuple-element.26), channel_id=1, source_target_pairs={{4,0},{0,4},{12,8},{8,12},{20,16},{16,20},{28,24},{24,28},{5,1},{1... | collective-permute-start | bytes 3145736 | tf_op jit(solution)/shard_map/ppermute | solution.py:41
  51.0 8.8 %collective-permute-start.14 = (bf16[128,1024]{1,0:T(8,128)(2,1)S(1)}, bf16[128,1024]{1,0:T(8,128)(2,1)S(1)}, u32[]{:S(2)}, u32[]{:S(2)}) collective-permute-start(bf16[128,1024]{1,0:T(8,128)(2,1)S(1)} %slice.28), channel_id=1, source_target_pairs={{16,0},{20,4},{24,8},{28,12},{0,16},{4,20},{8,24},{12,28},{17,1},{... | collective-permute-start | bytes 786440 | tf_op jit(solution)/shard_map/ppermute | solution.py:41
  52.6 9.2 %collective-permute-start.15 = (bf16[128,1024]{1,0:T(8,128)(2,1)S(1)}, bf16[128,1024]{1,0:T(8,128)(2,1)S(1)}, u32[]{:S(2)}, u32[]{:S(2)}) collective-permute-start(bf16[128,1024]{1,0:T(8,128)(2,1)S(1)} %slice.29), channel_id=1, source_target_pairs={{8,0},{12,4},{0,8},{4,12},{24,16},{28,20},{16,24},{20,28},{9,1},{1... | collective-permute-start | bytes 786440 | tf_op jit(solution)/shard_map/ppermute | solution.py:41
  53.7 13.6 %collective-permute-start.17 = (bf16[256,512]{1,0:T(8,128)(2,1)S(1)}, bf16[256,512]{1,0:T(8,128)(2,1)S(1)}, u32[]{:S(2)}, u32[]{:S(2)}) collective-permute-start(bf16[256,512]{1,0:T(8,128)(2,1)S(1)} %get-tuple-element.33), channel_id=1, source_target_pairs={{24,0},{28,4},{16,8},{20,12},{8,16},{12,20},{0,24},{4,28},{25,1},{... | collective-permute-start | bytes 786440 | tf_op jit(solution)/shard_map/ppermute | solution.py:41
  57.9 10.9 %collective-permute-start.11 = (f32[112,1024]{1,0:T(8,128)S(1)}, f32[112,1024]{1,0:T(8,128)S(1)}, u32[]{:S(2)}, u32[]{:S(2)}) collective-permute-start(f32[112,1024]{1,0:T(8,128)S(1)} %get-tuple-element.36), channel_id=1, source_target_pairs={{4,0},{0,4},{12,8},{8,12},{20,16},{16,20},{28,24},{24,28},{5,1},{1... | collective-permute-start | bytes 1376264 | tf_op jit(solution)/shard_map/ppermute | solution.py:41
  58.0 12.4 %collective-permute-start.12 = (f32[112,1024]{1,0:T(8,128)S(1)}, f32[112,1024]{1,0:T(8,128)S(1)}, u32[]{:S(2)}, u32[]{:S(2)}) collective-permute-start(f32[112,1024]{1,0:T(8,128)S(1)} %get-tuple-element.37), channel_id=1, source_target_pairs={{4,0},{0,4},{12,8},{8,12},{20,16},{16,20},{28,24},{24,28},{5,1},{1... | collective-permute-start | bytes 1376264 | tf_op jit(solution)/shard_map/ppermute | solution.py:41
  59.8 2.3 %collective-permute-start.13 = (f32[32,1024]{1,0:T(8,128)S(1)}, f32[32,1024]{1,0:T(8,128)S(1)}, u32[]{:S(2)}, u32[]{:S(2)}) collective-permute-start(f32[32,1024]{1,0:T(8,128)S(1)} %slice.25), channel_id=1, source_target_pairs={{4,0},{0,4},{12,8},{8,12},{20,16},{16,20},{28,24},{24,28},{5,1},{1... | collective-permute-start | bytes 393224 | tf_op jit(solution)/shard_map/ppermute | solution.py:41
  62.0 9.4 %collective-permute-start.16 = (bf16[1024,256]{1,0:T(8,128)(2,1)S(1)}, bf16[1024,256]{1,0:T(8,128)(2,1)S(1)}, u32[]{:S(2)}, u32[]{:S(2)}) collective-permute-start(bf16[1024,256]{1,0:T(8,128)(2,1)S(1)} %shard_map.54.far), channel_id=1, source_target_pairs={{4,0},{0,4},{12,8},{8,12},{20,16},{16,20},{28,24},{24,28},{5,1},{1... | collective-permute-start | bytes 1572872 | tf_op jit(solution)/shard_map/ppermute | solution.py:41
  62.1 15.9 %collective-permute-start.19 = (bf16[512,512]{1,0:T(8,128)(2,1)S(1)}, bf16[512,512]{1,0:T(8,128)(2,1)S(1)}, u32[]{:S(2)}, u32[]{:S(2)}) collective-permute-start(bf16[512,512]{1,0:T(8,128)(2,1)S(1)} %get-tuple-element.34), channel_id=1, source_target_pairs={{8,0},{12,4},{0,8},{4,12},{24,16},{28,20},{16,24},{20,28},{9,1},{1... | collective-permute-start | bytes 1572872 | tf_op jit(solution)/shard_map/ppermute | solution.py:41
  67.3 12.5 %collective-permute-start.20 = (bf16[512,512]{1,0:T(8,128)(2,1)S(1)}, bf16[512,512]{1,0:T(8,128)(2,1)S(1)}, u32[]{:S(2)}, u32[]{:S(2)}) collective-permute-start(bf16[512,512]{1,0:T(8,128)(2,1)S(1)} %get-tuple-element.35), channel_id=1, source_target_pairs={{16,0},{20,4},{24,8},{28,12},{0,16},{4,20},{8,24},{12,28},{17,1},{... | collective-permute-start | bytes 1572872 | tf_op jit(solution)/shard_map/ppermute | solution.py:41
  68.9 6.6 %collective-permute-start.18 = (bf16[256,512]{1,0:T(8,128)(2,1)S(1)}, bf16[256,512]{1,0:T(8,128)(2,1)S(1)}, u32[]{:S(2)}, u32[]{:S(2)}) collective-permute-start(bf16[256,512]{1,0:T(8,128)(2,1)S(1)} %collective-permute-done.17.refs_0_), channel_id=1, source_target_pairs={{1,0},{0,1},{3,2},{2,3},{5,4},{4,5},{7,6},{6,7},{9,8},{8,9},{11,10... | collective-permute-start | bytes 786440 | tf_op jit(solution)/shard_map/ppermute | solution.py:232

commit v9 on v7

--- a/solution.py
+++ b/solution.py
@@ -237,7 +237,7 @@
         mine, theirs, out_weight, *after([*weights.values()], turned_other),
     )
     own, others = call(functools.partial(context_far_kernel, s), [half_sums] * 2, mine, theirs, near_sums, *weights_far)
-    context_grad = (own + sibling(others, (0.4375, 0.875))).astype(BF16)
+    context_grad = (own + sibling(others, (0.375, 0.59375))).astype(BF16)
 
     result = shape(s.taken, s.width, dtype=F32)
     sums = call(

time: 81.7 us -> 81.7 us (level)
  no operation moved by 1% of the time
where the time goes in v9:
time: 81.7 us; the launch traced here: 81.5 us
  waiting for transfers between devices  52.2 us (64%)
  starting transfers between devices  20.2 us (25%)
  Pallas kernels  7.22 us (9%)
  other arithmetic  0.93 us (1%)
    ppermute x3, waiting for transfers between devices, along_node(): lax.ppermute(array, 'node', [((i + d) % node, i) for i in range(node)])  25.3 us
    ppermute x17, waiting for transfers between devices, shift(): lax.ppermute(array, 'outer', [(place(o, db, da, dc), o) for o in range(la...  22.8 us
    ppermute x17, starting transfers between devices, shift(): lax.ppermute(array, 'outer', [(place(o, db, da, dc), o) for o in range(la...  13.7 us
    pallas_call x9, Pallas kernels, call(): pl.pallas_call(kernel, out_shape=out, in_specs=[VMEM] * len(args), out_sp...  7.22 us
    ppermute x3, starting transfers between devices, along_node(): lax.ppermute(array, 'node', [((i + d) % node, i) for i in range(node)])  4.95 us
    ppermute x1, waiting for transfers between devices, body(): lax.ppermute(x, 'node', [(i ^ 1, i) for i in range(s.node)])  4.12 us
  transfers between devices with their start and end apart: 21, of which 14 were waited for; matrix products, arithmetic and copies ran while one was open for 1% of the time, Pallas kernels for 7%

profile of v9, /device:TPU:0, one launch (start us, length us, event | category | flops | bytes accessed | tf_op | source)
XLA Modules:
  0.0 81.5 jit_solution(6025661907846316289)
XLA Ops:
  0.6 3.0 %collective-permute-start = (bf16[1024,512]{1,0:T(8,128)(2,1)}, bf16[1024,512]{1,0:T(8,128)(2,1)S(1)}, u32[]{:S(2)}, u32[]{:S(2)}) collective-permute-start(bf16[1024,512]{1,0:T(8,128)(2,1)} %refs_0_.4), channel_id=1, source_target_pairs={{8,0},{12,4},{0,8},{4,12},{24,16},{28,20},{16,24},{20,28},{9,1},{1... | collective-permute-start | bytes 3145736 | tf_op jit(solution)/shard_map/ppermute | solution.py:41
  3.6 1.5 %collective-permute-start.1 = (bf16[1024,512]{1,0:T(8,128)(2,1)}, bf16[1024,512]{1,0:T(8,128)(2,1)S(1)}, u32[]{:S(2)}, u32[]{:S(2)}) collective-permute-start(bf16[1024,512]{1,0:T(8,128)(2,1)} %refs_0_.4), channel_id=1, source_target_pairs={{16,0},{20,4},{24,8},{28,12},{0,16},{4,20},{8,24},{12,28},{17,1},{... | collective-permute-start | bytes 3145736 | tf_op jit(solution)/shard_map/ppermute | solution.py:41
  5.2 1.6 %collective-permute-start.3 = (bf16[256,1024]{1,0:T(8,128)(2,1)}, bf16[256,1024]{1,0:T(8,128)(2,1)S(1)}, u32[]{:S(2)}, u32[]{:S(2)}) collective-permute-start(bf16[256,1024]{1,0:T(8,128)(2,1)} %refs_0_.2), channel_id=1, source_target_pairs={{3,0},{0,1},{1,2},{2,3},{7,4},{4,5},{5,6},{6,7},{11,8},{8,9},{9,10... | collective-permute-start | bytes 1572872 | tf_op jit(solution)/shard_map/ppermute | solution.py:52
  6.7 2.2 %collective-permute-start.2 = (bf16[256,1024]{1,0:T(8,128)(2,1)}, bf16[256,1024]{1,0:T(8,128)(2,1)S(1)}, u32[]{:S(2)}, u32[]{:S(2)}) collective-permute-start(bf16[256,1024]{1,0:T(8,128)(2,1)} %refs_0_.2), channel_id=1, source_target_pairs={{1,0},{2,1},{3,2},{0,3},{5,4},{6,5},{7,6},{4,7},{9,8},{10,9},{11,1... | collective-permute-start | bytes 1572872 | tf_op jit(solution)/shard_map/ppermute | solution.py:52
  9.5 12.6 %collective-permute-done.3.refs_3_ = bf16[256,1024]{1,0:T(8,128)(2,1)S(1)} collective-permute-done((bf16[256,1024]{1,0:T(8,128)(2,1)}, bf16[256,1024]{1,0:T(8,128)(2,1)S(1)}, u32[]{:S(2)}, u32[]{:S(2)}) %collective-permute-start.3) | collective-permute-done | bytes 524320 | tf_op jit(solution)/shard_map/ppermute | solution.py:52
  22.6 8.4 %collective-permute-done.2.refs_1_ = bf16[256,1024]{1,0:T(8,128)(2,1)S(1)} collective-permute-done((bf16[256,1024]{1,0:T(8,128)(2,1)}, bf16[256,1024]{1,0:T(8,128)(2,1)S(1)}, u32[]{:S(2)}, u32[]{:S(2)}) %collective-permute-start.2) | collective-permute-done | bytes 524320 | tf_op jit(solution)/shard_map/ppermute | solution.py:52
  33.7 5.3 %collective-permute-done.8.refs_1_ = bf16[256,1024]{1,0:T(8,128)(2,1)S(1)} collective-permute-done((bf16[256,1024]{1,0:T(8,128)(2,1)}, bf16[256,1024]{1,0:T(8,128)(2,1)S(1)}, u32[]{:S(2)}, u32[]{:S(2)}) %collective-permute-start.8) | collective-permute-done | bytes 524320 | tf_op jit(solution)/shard_map/ppermute | solution.py:41
  39.1 2.1 %collective-permute-done.9.refs_2_ = bf16[256,1024]{1,0:T(8,128)(2,1)S(1)} collective-permute-done((bf16[256,1024]{1,0:T(8,128)(2,1)}, bf16[256,1024]{1,0:T(8,128)(2,1)S(1)}, u32[]{:S(2)}, u32[]{:S(2)}) %collective-permute-start.9) | collective-permute-done | bytes 524320 | tf_op jit(solution)/shard_map/ppermute | solution.py:41
  41.7 4.3 %collective-permute-done.4.refs_2_ = bf16[256,1024]{1,0:T(8,128)(2,1)S(1)} collective-permute-done((bf16[256,1024]{1,0:T(8,128)(2,1)S(1)}, bf16[256,1024]{1,0:T(8,128)(2,1)S(1)}, u32[]{:S(2)}, u32[]{:S(2)}) %collective-permute-start.4) | collective-permute-done | bytes 524320 | tf_op jit(solution)/shard_map/ppermute | solution.py:52
  46.3 3.2 %collective-permute-done.6.refs_1_ = bf16[512,512]{1,0:T(8,128)(2,1)S(1)} collective-permute-done((bf16[512,512]{1,0:T(8,128)(2,1)S(1)}, bf16[512,512]{1,0:T(8,128)(2,1)S(1)}, u32[]{:S(2)}, u32[]{:S(2)}) %collective-permute-start.6) | collective-permute-done | bytes 524320 | tf_op jit(solution)/shard_map/ppermute | solution.py:41
  49.5 1.5 %collective-permute-done.5.refs_0_ = bf16[512,512]{1,0:T(8,128)(2,1)S(1)} collective-permute-done((bf16[512,512]{1,0:T(8,128)(2,1)S(1)}, bf16[512,512]{1,0:T(8,128)(2,1)S(1)}, u32[]{:S(2)}, u32[]{:S(2)}) %collective-permute-start.5) | collective-permute-done | bytes 524320 | tf_op jit(solution)/shard_map/ppermute | solution.py:41
  51.0 1.6 %collective-permute-start.14 = (bf16[128,1024]{1,0:T(8,128)(2,1)S(1)}, bf16[128,1024]{1,0:T(8,128)(2,1)S(1)}, u32[]{:S(2)}, u32[]{:S(2)}) collective-permute-start(bf16[128,1024]{1,0:T(8,128)(2,1)S(1)} %slice.28), channel_id=1, source_target_pairs={{16,0},{20,4},{24,8},{28,12},{0,16},{4,20},{8,24},{12,28},{17,1},{... | collective-permute-start | bytes 786440 | tf_op jit(solution)/shard_map/ppermute | solution.py:41
  53.7 1.6 %collective-permute-start.17 = (bf16[256,512]{1,0:T(8,128)(2,1)S(1)}, bf16[256,512]{1,0:T(8,128)(2,1)S(1)}, u32[]{:S(2)}, u32[]{:S(2)}) collective-permute-start(bf16[256,512]{1,0:T(8,128)(2,1)S(1)} %get-tuple-element.33), channel_id=1, source_target_pairs={{24,0},{28,4},{16,8},{20,12},{8,16},{12,20},{0,24},{4,28},{25,1},{... | collective-permute-start | bytes 786440 | tf_op jit(solution)/shard_map/ppermute | solution.py:41
  55.3 1.8 %shard_map.52.near = f32[512,1024]{1,0:T(8,128)S(1)} custom-call(bf16[4,256,512]{2,1,0:T(8,128)(2,1)S(1)} %get-tuple-element.22.mine, bf16[4,256,512]{2,1,0:T(8,128)(2,1)S(1)} %collective-permute-done.7.theirs.other, bf16[1024,512]{1,0:T(8,128)(2,1)S(1)} %copy-done, bf16[1024,512]{1,0:T(8,128)(2,1)S(1)} %collective-permute-done.refs_1_, ...), custom_call_target="tpu_custom_call" | custom-call | tf_op jit(solution)/shard_map/pallas_call | solution.py:60
  58.6 1.2 %collective-permute-done.14.refs_0_ = bf16[128,1024]{1,0:T(8,128)(2,1)S(1)} collective-permute-done((bf16[128,1024]{1,0:T(8,128)(2,1)S(1)}, bf16[128,1024]{1,0:T(8,128)(2,1)S(1)}, u32[]{:S(2)}, u32[]{:S(2)}) %collective-permute-start.14) | collective-permute-done | bytes 262176 | tf_op jit(solution)/shard_map/ppermute | solution.py:41
  59.8 2.0 %collective-permute-done.15.refs_1_ = bf16[128,1024]{1,0:T(8,128)(2,1)S(1)} collective-permute-done((bf16[128,1024]{1,0:T(8,128)(2,1)S(1)}, bf16[128,1024]{1,0:T(8,128)(2,1)S(1)}, u32[]{:S(2)}, u32[]{:S(2)}) %collective-permute-start.15) | collective-permute-done | bytes 262176 | tf_op jit(solution)/shard_map/ppermute | solution.py:41
  62.7 4.7 %collective-permute-done.17.refs_0_ = bf16[256,512]{1,0:T(8,128)(2,1)S(1)} collective-permute-done((bf16[256,512]{1,0:T(8,128)(2,1)S(1)}, bf16[256,512]{1,0:T(8,128)(2,1)S(1)}, u32[]{:S(2)}, u32[]{:S(2)}) %collective-permute-start.17) | collective-permute-done | bytes 262176 | tf_op jit(solution)/shard_map/ppermute | solution.py:41
  67.3 1.5 %collective-permute-start.20 = (bf16[512,512]{1,0:T(8,128)(2,1)S(1)}, bf16[512,512]{1,0:T(8,128)(2,1)S(1)}, u32[]{:S(2)}, u32[]{:S(2)}) collective-permute-start(bf16[512,512]{1,0:T(8,128)(2,1)S(1)} %get-tuple-element.35), channel_id=1, source_target_pairs={{16,0},{20,4},{24,8},{28,12},{0,16},{4,20},{8,24},{12,28},{17,1},{... | collective-permute-start | bytes 1572872 | tf_op jit(solution)/shard_map/ppermute | solution.py:41
  68.9 1.6 %collective-permute-start.18 = (bf16[256,512]{1,0:T(8,128)(2,1)S(1)}, bf16[256,512]{1,0:T(8,128)(2,1)S(1)}, u32[]{:S(2)}, u32[]{:S(2)}) collective-permute-start(bf16[256,512]{1,0:T(8,128)(2,1)S(1)} %collective-permute-done.17.refs_0_), channel_id=1, source_target_pairs={{1,0},{0,1},{3,2},{2,3},{5,4},{4,5},{7,6},{6,7},{9,8},{8,9},{11,10... | collective-permute-start | bytes 786440 | tf_op jit(solution)/shard_map/ppermute | solution.py:232
  71.4 4.1 %collective-permute-done.18.refs_1_ = bf16[256,512]{1,0:T(8,128)(2,1)S(1)} collective-permute-done((bf16[256,512]{1,0:T(8,128)(2,1)S(1)}, bf16[256,512]{1,0:T(8,128)(2,1)S(1)}, u32[]{:S(2)}, u32[]{:S(2)}) %collective-permute-start.18) | collective-permute-done | bytes 262176 | tf_op jit(solution)/shard_map/ppermute | solution.py:232
  75.5 1.3 %shard_map.56.sums = f32[1024,512]{1,0:T(8,128)S(1)} custom-call(bf16[1024,768]{1,0:T(8,128)(2,1)S(1)} %shard_map.51.turned, bf16[1024,768]{1,0:T(8,128)(2,1)S(1)} %collective-permute-done.10.theirs, bf16[1024,256]{1,0:T(8,128)(2,1)S(1)} %shard_map.54.far, bf16[1024,256]{1,0:T(8,128)(2,1)S(1)} %collective-permute-done.16.far_theirs, ...), custom_call_target="tpu_custom_call" | custom-call | tf_op jit(solution)/shard_map/pallas_call | solution.py:60
  76.8 1.1 %collective-permute-done.19.block = bf16[512,512]{1,0:T(8,128)(2,1)S(1)} collective-permute-done((bf16[512,512]{1,0:T(8,128)(2,1)S(1)}, bf16[512,512]{1,0:T(8,128)(2,1)S(1)}, u32[]{:S(2)}, u32[]{:S(2)}) %collective-permute-start.19) | collective-permute-done | bytes 524320 | tf_op jit(solution)/shard_map/ppermute | solution.py:41
  78.6 1.2 %collective-permute-done.20.block = bf16[512,512]{1,0:T(8,128)(2,1)S(1)} collective-permute-done((bf16[512,512]{1,0:T(8,128)(2,1)S(1)}, bf16[512,512]{1,0:T(8,128)(2,1)S(1)}, u32[]{:S(2)}, u32[]{:S(2)}) %collective-permute-start.20) | collective-permute-done | bytes 524320 | tf_op jit(solution)/shard_map/ppermute | solution.py:41
  79.9 1.7 %shard_map.58 = f32[1024,512]{1,0:T(8,128)} custom-call(f32[1024,512]{1,0:T(8,128)S(1)} %shard_map.57.sums, bf16[1024,768]{1,0:T(8,128)(2,1)S(1)} %shard_map.51.turned, bf16[1024,768]{1,0:T(8,128)(2,1)S(1)} %collective-permute-done.10.theirs, bf16[512,512]{1,0:T(8,128)(2,1)S(1)} %collective-permute-done.20.block), custom_call_target="tpu_custom_call" | custom-call | tf_op jit(solution)/shard_map/pallas_call | solution.py:60
  (41 shorter events, 9.7 us)
Async XLA Ops:
  0.6 40.5 %copy-start.1 = (bf16[256,1024]{1,0:T(8,128)(2,1)S(1)}, bf16[256,1024]{1,0:T(8,128)(2,1)}, u32[]{:S(2)}) copy-start(bf16[256,1024]{1,0:T(8,128)(2,1)} %refs_0_.3) | copy-start | bytes 1572868
  0.6 30.4 %collective-permute-start = (bf16[1024,512]{1,0:T(8,128)(2,1)}, bf16[1024,512]{1,0:T(8,128)(2,1)S(1)}, u32[]{:S(2)}, u32[]{:S(2)}) collective-permute-start(bf16[1024,512]{1,0:T(8,128)(2,1)} %refs_0_.4), channel_id=1, source_target_pairs={{8,0},{12,4},{0,8},{4,12},{24,16},{28,20},{16,24},{20,28},{9,1},{1... | collective-permute-start | bytes 3145736 | tf_op jit(solution)/shard_map/ppermute | solution.py:41
  3.6 27.4 %collective-permute-start.1 = (bf16[1024,512]{1,0:T(8,128)(2,1)}, bf16[1024,512]{1,0:T(8,128)(2,1)S(1)}, u32[]{:S(2)}, u32[]{:S(2)}) collective-permute-start(bf16[1024,512]{1,0:T(8,128)(2,1)} %refs_0_.4), channel_id=1, source_target_pairs={{16,0},{20,4},{24,8},{28,12},{0,16},{4,20},{8,24},{12,28},{17,1},{... | collective-permute-start | bytes 3145736 | tf_op jit(solution)/shard_map/ppermute | solution.py:41
  5.2 16.9 %collective-permute-start.3 = (bf16[256,1024]{1,0:T(8,128)(2,1)}, bf16[256,1024]{1,0:T(8,128)(2,1)S(1)}, u32[]{:S(2)}, u32[]{:S(2)}) collective-permute-start(bf16[256,1024]{1,0:T(8,128)(2,1)} %refs_0_.2), channel_id=1, source_target_pairs={{3,0},{0,1},{1,2},{2,3},{7,4},{4,5},{5,6},{6,7},{11,8},{8,9},{9,10... | collective-permute-start | bytes 1572872 | tf_op jit(solution)/shard_map/ppermute | solution.py:52
  6.7 24.3 %collective-permute-start.2 = (bf16[256,1024]{1,0:T(8,128)(2,1)}, bf16[256,1024]{1,0:T(8,128)(2,1)S(1)}, u32[]{:S(2)}, u32[]{:S(2)}) collective-permute-start(bf16[256,1024]{1,0:T(8,128)(2,1)} %refs_0_.2), channel_id=1, source_target_pairs={{1,0},{2,1},{3,2},{0,3},{5,4},{6,5},{7,6},{4,7},{9,8},{10,9},{11,1... | collective-permute-start | bytes 1572872 | tf_op jit(solution)/shard_map/ppermute | solution.py:52
  9.0 30.1 %collective-permute-start.8 = (bf16[256,1024]{1,0:T(8,128)(2,1)}, bf16[256,1024]{1,0:T(8,128)(2,1)S(1)}, u32[]{:S(2)}, u32[]{:S(2)}) collective-permute-start(bf16[256,1024]{1,0:T(8,128)(2,1)} %refs_0_.3), channel_id=1, source_target_pairs={{8,0},{12,4},{0,8},{4,12},{24,16},{28,20},{16,24},{20,28},{9,1},{1... | collective-permute-start | bytes 1572872 | tf_op jit(solution)/shard_map/ppermute | solution.py:41
  22.1 19.1 %collective-permute-start.9 = (bf16[256,1024]{1,0:T(8,128)(2,1)}, bf16[256,1024]{1,0:T(8,128)(2,1)S(1)}, u32[]{:S(2)}, u32[]{:S(2)}) collective-permute-start(bf16[256,1024]{1,0:T(8,128)(2,1)} %refs_0_.3), channel_id=1, source_target_pairs={{16,0},{20,4},{24,8},{28,12},{0,16},{4,20},{8,24},{12,28},{17,1},{... | collective-permute-start | bytes 1572872 | tf_op jit(solution)/shard_map/ppermute | solution.py:41
  31.0 15.0 %collective-permute-start.4 = (bf16[256,1024]{1,0:T(8,128)(2,1)S(1)}, bf16[256,1024]{1,0:T(8,128)(2,1)S(1)}, u32[]{:S(2)}, u32[]{:S(2)}) collective-permute-start(bf16[256,1024]{1,0:T(8,128)(2,1)S(1)} %collective-permute-done.3.refs_3_), channel_id=1, source_target_pairs={{3,0},{0,1},{1,2},{2,3},{7,4},{4,5},{5,6},{6,7},{11,8},{8,9},{9,10... | collective-permute-start | bytes 1572872 | tf_op jit(solution)/shard_map/ppermute | solution.py:52
  32.2 13.8 %copy-start.2 = (bf16[256,1024]{1,0:T(8,128)(2,1)S(1)}, bf16[256,1024]{1,0:T(8,128)(2,1)}, u32[]{:S(2)}) copy-start(bf16[256,1024]{1,0:T(8,128)(2,1)} %refs_0_.2) | copy-start | bytes 1572868
  32.2 17.2 %collective-permute-start.6 = (bf16[512,512]{1,0:T(8,128)(2,1)S(1)}, bf16[512,512]{1,0:T(8,128)(2,1)S(1)}, u32[]{:S(2)}, u32[]{:S(2)}) collective-permute-start(bf16[512,512]{1,0:T(8,128)(2,1)S(1)} %slice.22), channel_id=1, source_target_pairs={{8,0},{12,4},{0,8},{4,12},{24,16},{28,20},{16,24},{20,28},{9,1},{1... | collective-permute-start | bytes 1572872 | tf_op jit(solution)/shard_map/ppermute | solution.py:41
  32.8 18.1 %collective-permute-start.5 = (bf16[512,512]{1,0:T(8,128)(2,1)S(1)}, bf16[512,512]{1,0:T(8,128)(2,1)S(1)}, u32[]{:S(2)}, u32[]{:S(2)}) collective-permute-start(bf16[512,512]{1,0:T(8,128)(2,1)S(1)} %slice.21), channel_id=1, source_target_pairs={{16,0},{20,4},{24,8},{28,12},{0,16},{4,20},{8,24},{12,28},{17,1},{... | collective-permute-start | bytes 1572872 | tf_op jit(solution)/shard_map/ppermute | solution.py:41
  41.6 12.0 %collective-permute-start.10 = (bf16[1024,768]{1,0:T(8,128)(2,1)S(1)}, bf16[1024,768]{1,0:T(8,128)(2,1)S(1)}, u32[]{:S(2)}, u32[]{:S(2)}) collective-permute-start(bf16[1024,768]{1,0:T(8,128)(2,1)S(1)} %shard_map.51.turned), channel_id=1, source_target_pairs={{4,0},{0,4},{12,8},{8,12},{20,16},{16,20},{28,24},{24,28},{5,1},{1... | collective-permute-start | bytes 4718600 | tf_op jit(solution)/shard_map/ppermute | solution.py:41
  46.3 9.0 %copy-start = (bf16[1024,512]{1,0:T(8,128)(2,1)S(1)}, bf16[1024,512]{1,0:T(8,128)(2,1)}, u32[]{:S(2)}) copy-start(bf16[1024,512]{1,0:T(8,128)(2,1)} %refs_0_.4) | copy-start | bytes 3145732
  50.9 2.7 %collective-permute-start.7 = (bf16[4,256,512]{2,1,0:T(8,128)(2,1)S(1)}, bf16[4,256,512]{2,1,0:T(8,128)(2,1)S(1)}, u32[]{:S(2)}, u32[]{:S(2)}) collective-permute-start(bf16[4,256,512]{2,1,0:T(8,128)(2,1)S(1)} %get-tuple-element.26), channel_id=1, source_target_pairs={{4,0},{0,4},{12,8},{8,12},{20,16},{16,20},{28,24},{24,28},{5,1},{1... | collective-permute-start | bytes 3145736 | tf_op jit(solution)/shard_map/ppermute | solution.py:41
  51.0 8.8 %collective-permute-start.14 = (bf16[128,1024]{1,0:T(8,128)(2,1)S(1)}, bf16[128,1024]{1,0:T(8,128)(2,1)S(1)}, u32[]{:S(2)}, u32[]{:S(2)}) collective-permute-start(bf16[128,1024]{1,0:T(8,128)(2,1)S(1)} %slice.28), channel_id=1, source_target_pairs={{16,0},{20,4},{24,8},{28,12},{0,16},{4,20},{8,24},{12,28},{17,1},{... | collective-permute-start | bytes 786440 | tf_op jit(solution)/shard_map/ppermute | solution.py:41
  52.6 9.2 %collective-permute-start.15 = (bf16[128,1024]{1,0:T(8,128)(2,1)S(1)}, bf16[128,1024]{1,0:T(8,128)(2,1)S(1)}, u32[]{:S(2)}, u32[]{:S(2)}) collective-permute-start(bf16[128,1024]{1,0:T(8,128)(2,1)S(1)} %slice.29), channel_id=1, source_target_pairs={{8,0},{12,4},{0,8},{4,12},{24,16},{28,20},{16,24},{20,28},{9,1},{1... | collective-permute-start | bytes 786440 | tf_op jit(solution)/shard_map/ppermute | solution.py:41
  53.7 13.6 %collective-permute-start.17 = (bf16[256,512]{1,0:T(8,128)(2,1)S(1)}, bf16[256,512]{1,0:T(8,128)(2,1)S(1)}, u32[]{:S(2)}, u32[]{:S(2)}) collective-permute-start(bf16[256,512]{1,0:T(8,128)(2,1)S(1)} %get-tuple-element.33), channel_id=1, source_target_pairs={{24,0},{28,4},{16,8},{20,12},{8,16},{12,20},{0,24},{4,28},{25,1},{... | collective-permute-start | bytes 786440 | tf_op jit(solution)/shard_map/ppermute | solution.py:41
  57.9 4.2 %collective-permute-start.12 = (f32[56,1024]{1,0:T(8,128)S(1)}, f32[56,1024]{1,0:T(8,128)S(1)}, u32[]{:S(2)}, u32[]{:S(2)}) collective-permute-start(f32[56,1024]{1,0:T(8,128)S(1)} %slice.24), channel_id=1, source_target_pairs={{4,0},{0,4},{12,8},{8,12},{20,16},{16,20},{28,24},{24,28},{5,1},{1... | collective-permute-start | bytes 688136 | tf_op jit(solution)/shard_map/ppermute | solution.py:41
  58.0 12.5 %collective-permute-start.13 = (f32[104,1024]{1,0:T(8,128)S(1)}, f32[104,1024]{1,0:T(8,128)S(1)}, u32[]{:S(2)}, u32[]{:S(2)}) collective-permute-start(f32[104,1024]{1,0:T(8,128)S(1)} %slice.25), channel_id=1, source_target_pairs={{4,0},{0,4},{12,8},{8,12},{20,16},{16,20},{28,24},{24,28},{5,1},{1... | collective-permute-start | bytes 1277960 | tf_op jit(solution)/shard_map/ppermute | solution.py:41
  59.8 9.1 %collective-permute-start.11 = (f32[96,1024]{1,0:T(8,128)S(1)}, f32[96,1024]{1,0:T(8,128)S(1)}, u32[]{:S(2)}, u32[]{:S(2)}) collective-permute-start(f32[96,1024]{1,0:T(8,128)S(1)} %slice.23), channel_id=1, source_target_pairs={{4,0},{0,4},{12,8},{8,12},{20,16},{16,20},{28,24},{24,28},{5,1},{1... | collective-permute-start | bytes 1179656 | tf_op jit(solution)/shard_map/ppermute | solution.py:41
  62.0 9.4 %collective-permute-start.16 = (bf16[1024,256]{1,0:T(8,128)(2,1)S(1)}, bf16[1024,256]{1,0:T(8,128)(2,1)S(1)}, u32[]{:S(2)}, u32[]{:S(2)}) collective-permute-start(bf16[1024,256]{1,0:T(8,128)(2,1)S(1)} %shard_map.54.far), channel_id=1, source_target_pairs={{4,0},{0,4},{12,8},{8,12},{20,16},{16,20},{28,24},{24,28},{5,1},{1... | collective-permute-start | bytes 1572872 | tf_op jit(solution)/shard_map/ppermute | solution.py:41
  62.1 15.9 %collective-permute-start.19 = (bf16[512,512]{1,0:T(8,128)(2,1)S(1)}, bf16[512,512]{1,0:T(8,128)(2,1)S(1)}, u32[]{:S(2)}, u32[]{:S(2)}) collective-permute-start(bf16[512,512]{1,0:T(8,128)(2,1)S(1)} %get-tuple-element.34), channel_id=1, source_target_pairs={{8,0},{12,4},{0,8},{4,12},{24,16},{28,20},{16,24},{20,28},{9,1},{1... | collective-permute-start | bytes 1572872 | tf_op jit(solution)/shard_map/ppermute | solution.py:41
  67.3 12.5 %collective-permute-start.20 = (bf16[512,512]{1,0:T(8,128)(2,1)S(1)}, bf16[512,512]{1,0:T(8,128)(2,1)S(1)}, u32[]{:S(2)}, u32[]{:S(2)}) collective-permute-start(bf16[512,512]{1,0:T(8,128)(2,1)S(1)} %get-tuple-element.35), channel_id=1, source_target_pairs={{16,0},{20,4},{24,8},{28,12},{0,16},{4,20},{8,24},{12,28},{17,1},{... | collective-permute-start | bytes 1572872 | tf_op jit(solution)/shard_map/ppermute | solution.py:41
  68.9 6.6 %collective-permute-start.18 = (bf16[256,512]{1,0:T(8,128)(2,1)S(1)}, bf16[256,512]{1,0:T(8,128)(2,1)S(1)}, u32[]{:S(2)}, u32[]{:S(2)}) collective-permute-start(bf16[256,512]{1,0:T(8,128)(2,1)S(1)} %collective-permute-done.17.refs_0_), channel_id=1, source_target_pairs={{1,0},{0,1},{3,2},{2,3},{5,4},{4,5},{7,6},{6,7},{9,8},{8,9},{11,10... | collective-permute-start | bytes 786440 | tf_op jit(solution)/shard_map/ppermute | solution.py:232
